TPU v7x, 1024 devices: a whole 4x4x32 slice. The times are simulated.
1024 devices in a mesh: dom: 64 (over z, core), dp: 16 (over y, x).
Axes of the slice: x: 4, y: 4, z: 32, core: 2. Of those that a mesh axis runs over, the one named last changes fastest.
Arguments:
- features: bfloat16 [65536, 256], P('dom'), may hold values from -6 to 6
- degree: int32 [65536], P('dom'), may hold values from 8 to 63
- send_rows: int32 [64, 64, 16], P('dom'), may hold values from 0 to 1023
- send_counts: int32 [64, 64], P('dom'), may hold values from 4 to 16, as said below
- edge_slots: int32 [64, 16, 8, 2, 128], P('dom', 'dp'), may hold values from -1 to 127, as said below
- tile_blocks: int32 [64, 16, 8, 2], P('dom', 'dp'), may hold values from 0 to 15
- w_in: bfloat16 [512, 256], replicated, may hold values from -0.25 to 0.25
- b_in: float32 [256], replicated, may hold values from -3 to 3
- w_out: bfloat16 [256, 256], replicated, may hold values from -0.375 to 0.375
- b_out: float32 [256], replicated, may hold values from -3 to 3
- cotangent: bfloat16 [65536, 256], P('dom'), may hold values from -6 to 6
Outputs:
- output: bfloat16 [65536, 256], P(('dom', 'dp'))
- grad_features: bfloat16 [65536, 256], P(('dom', 'dp'))
- grad_w_in: float32 [512, 256], replicated
- grad_b_in: float32 [256], replicated
- grad_w_out: float32 [256, 256], replicated
- grad_b_out: float32 [256], replicated
Inputs may be any that keep to these rules, and one draw needn't show every extreme that they name: `send_counts`: every owner sends 16 rows to at least one partition, and at least one partition receives 16 rows from every owner. `edge_slots`: -1 marks a padding edge in both of its entries; in each tile the live edges come first and at least half of its 128 edges are live; the first tile of every device is full.
All inputs are finite; a program needn't handle non-finite values.
Results may differ from a plain program's by a relative error of at most 0.007.
Values may be sent and summed in bfloat16 or wider, within the bound.
No kernel may reach another device: no remote copies, remote signals or barrier semaphores. Data moves between devices by JAX's collectives and lax.ppermute only.
A program may use at most 32 MiB of HBM per device.

v0:
```python
import math

import jax
import jax.numpy as jnp
from jax import lax
from jax.sharding import PartitionSpec as P


def silu_slope(pre_act):
    sigmoid_pre = jax.nn.sigmoid(pre_act)
    return sigmoid_pre * (1.0 + pre_act * (1.0 - sigmoid_pre))


def build_tiles(slot_group):
    positions = jnp.arange(slot_group.shape[-1], dtype=jnp.int32)
    source_hot = (slot_group[:, 0, :, None] == positions).astype(jnp.bfloat16)
    target_hot = (slot_group[:, 1, :, None] == positions).astype(jnp.bfloat16)
    counted = jnp.einsum("gei,gej->gij", target_hot, source_hot, preferred_element_type=jnp.float32)
    return counted.astype(jnp.bfloat16)


def place_products(running, adjacency, block_group, stacked, transpose):
    if transpose:
        inputs = jnp.take(stacked, block_group[:, 1], axis=0)
        products = jnp.einsum("gij,gid->gjd", adjacency, inputs, preferred_element_type=jnp.float32)
        target = block_group[:, 0]
    else:
        inputs = jnp.take(stacked, block_group[:, 0], axis=0)
        products = jnp.einsum("gij,gjd->gid", adjacency, inputs, preferred_element_type=jnp.float32)
        target = block_group[:, 1]
    return running.at[target].add(products)


def forward_edges(local_rows, tile_rows, slot_groups, block_groups):
    channels = local_rows.shape[1]
    stacked = local_rows.reshape(-1, tile_rows, channels)

    def forward_advance(running, members):
        slot_group, block_group = members
        adjacency = build_tiles(slot_group)
        return (place_products(running, adjacency, block_group, stacked, False), adjacency)

    initial = jnp.zeros(stacked.shape, jnp.float32)
    summed, adjacencies = lax.scan(forward_advance, initial, (slot_groups, block_groups))
    return (summed.reshape(-1, channels), adjacencies)


def backward_edges(local_rows, tile_rows, block_groups, sources):
    channels = local_rows.shape[1]
    stacked = local_rows.reshape(-1, tile_rows, channels)

    def backward_advance(running, members):
        block_group, source = members
        adjacency = build_tiles(source)
        return (place_products(running, adjacency, block_group, stacked, True), None)

    initial = jnp.zeros(stacked.shape, jnp.float32)
    summed, unused = lax.scan(backward_advance, initial, (block_groups, sources))
    return summed.reshape(-1, channels)


def copy_mirrors(rows_all, owned, usable):
    channels = rows_all.shape[1]
    picked = jnp.take(rows_all, owned.reshape(-1), axis=0).reshape(
        owned.shape[0], owned.shape[1], channels
    )
    picked = jnp.where(usable[:, :, None], picked, jnp.zeros((), rows_all.dtype))
    arrived = lax.all_to_all(picked, "dom", split_axis=0, concat_axis=0, tiled=True)
    return jnp.concatenate([rows_all, arrived.reshape(-1, channels)], 0)


def return_partials(partial_value, owned, usable):
    n_dom, capacity = owned.shape
    own_count = partial_value.shape[0] - n_dom * capacity
    rounded = partial_value.astype(jnp.bfloat16)
    channels = partial_value.shape[1]
    outgoing = rounded[own_count:].reshape(n_dom, capacity, channels)
    arrived = lax.all_to_all(outgoing, "dom", split_axis=0, concat_axis=0, tiled=True)
    arrived = jnp.where(usable[:, :, None], arrived.astype(jnp.float32), 0.0)
    owned_sum = (
        rounded[:own_count]
        .astype(jnp.float32)
        .at[owned.reshape(-1)]
        .add(arrived.reshape(-1, channels))
    )
    return lax.psum_scatter(
        owned_sum.astype(jnp.bfloat16), "dp", scatter_dimension=0, tiled=True
    ).astype(jnp.float32)


def replica_rows(values):
    return lax.all_gather(values, "dp", axis=0, tiled=True)


def on_device(
    features,
    degree,
    send_rows,
    send_counts,
    edge_slots,
    tile_blocks,
    w_in,
    b_in,
    w_out,
    b_out,
    cotangent,
):
    n_dp = lax.axis_size("dp")
    n_dom = lax.axis_size("dom")
    replica = lax.axis_index("dp")
    v_count, channels = features.shape
    share_rows = v_count // n_dp
    owned = send_rows[0]
    usable = jnp.arange(owned.shape[1], dtype=jnp.int32)[None, :] < send_counts[0][:, None]
    slot_ids = edge_slots[0, 0]
    tile_rows = slot_ids.shape[-1]
    tile_count = slot_ids.shape[0]
    group = math.gcd(tile_count, 16)
    slot_groups = slot_ids.reshape(tile_count // group, group, 2, tile_rows)
    block_groups = tile_blocks[0, 0].reshape(tile_count // group, group, 2)
    norm_scale = 1.0 / math.sqrt(v_count * n_dom)
    degrees = degree.astype(jnp.float32)[:, None]
    first_row = replica * share_rows
    degree_mine = lax.dynamic_slice_in_dim(degrees, first_row, share_rows, 0)
    features_mine = lax.dynamic_slice_in_dim(features, first_row, share_rows, 0)
    cotangent_mine = lax.dynamic_slice_in_dim(cotangent, first_row, share_rows, 0)
    w_self = w_in[:channels]
    w_neigh = w_in[channels:]
    forward_sum, adjacencies = forward_edges(
        copy_mirrors(features, owned, usable), tile_rows, slot_groups, block_groups
    )
    aggregate_mine = (return_partials(forward_sum, owned, usable) / degree_mine).astype(
        jnp.bfloat16
    )
    inputs_mine = jnp.concatenate([features_mine, aggregate_mine], 1)
    pre_act = jnp.dot(inputs_mine, w_in, preferred_element_type=jnp.float32) + b_in
    hidden_mine = jax.nn.silu(pre_act).astype(jnp.bfloat16)
    grad_hidden = jnp.dot(cotangent_mine, w_out.T, preferred_element_type=jnp.float32)
    grad_pre_mine = (grad_hidden * silu_slope(pre_act)).astype(jnp.bfloat16)
    spread_mine = (
        jnp.dot(grad_pre_mine, w_neigh.T, preferred_element_type=jnp.float32) / degree_mine
    ).astype(jnp.bfloat16)
    spread_all = replica_rows(spread_mine)
    output = (jnp.dot(hidden_mine, w_out, preferred_element_type=jnp.float32) + b_out).astype(
        jnp.bfloat16
    )
    grad_self = jnp.dot(grad_pre_mine, w_self.T, preferred_element_type=jnp.float32)
    local_w_out = (
        jnp.einsum("nk,nh->kh", hidden_mine, cotangent_mine, preferred_element_type=jnp.float32)
        * norm_scale
    )
    local_b_out = jnp.sum(cotangent_mine.astype(jnp.float32), 0) * norm_scale
    local_w_in = (
        jnp.einsum("nk,nh->kh", inputs_mine, grad_pre_mine, preferred_element_type=jnp.float32)
        * norm_scale
    )
    local_b_in = jnp.sum(grad_pre_mine.astype(jnp.float32), 0) * norm_scale
    grad_w_in, grad_b_in, grad_w_out, grad_b_out = lax.psum(
        (local_w_in, local_b_in, local_w_out, local_b_out), ("dom", "dp")
    )
    spread_table = copy_mirrors(spread_all, owned, usable)
    back_sum = backward_edges(spread_table, tile_rows, block_groups, slot_groups)
    grad_neigh = return_partials(back_sum, owned, usable)
    grad_features = (grad_self + grad_neigh).astype(jnp.bfloat16)
    return (output, grad_features, grad_w_in, grad_b_in, grad_w_out, grad_b_out)


def solution(mesh):
    in_specs = (
        P("dom", None),
        P("dom"),
        P("dom", None, None),
        P("dom", None),
        P("dom", "dp", None, None, None),
        P("dom", "dp", None, None),
        P(),
        P(),
        P(),
        P(),
        P("dom", None),
    )
    out_specs = (P(("dom", "dp"), None), P(("dom", "dp"), None), P(), P(), P(), P())
    return jax.shard_map(
        on_device, mesh=mesh, in_specs=in_specs, out_specs=out_specs, check_vma=False
    )
```

profile of v0, /device:TPU:1, one launch (start us, length us, event | category | flops | bytes accessed | tf_op | source)
XLA Modules:
  0.0 1517.0 jit_solution(10175701287719573494)
XLA Ops:
  7.2 0.8 copy.18
  8.1 0.7 iota_compare_fusion.4
  8.9 4.6 gather_fusion
  13.5 0.2 broadcast_select_fusion.1
  13.7 1.0 broadcast_select_fusion.3
  14.7 30.4 %all-to-all-start = ((bf16[64,16,256]{2,1,0:T(8,128)(2,1)}), bf16[64,16,256]{2,1,0:T(8,128)(2,1)S(1)}, u32[]{:S(2)}, u32[]{:S(2)}) async-start(bf16[64,16,256]{2,1,0:T(8,128)(2,1)} %broadcast_select_fusion.3), calls=%async_computation | async-start | bytes 1048576 | tf_op jit(solution)/shard_map/all_to_all | solution.py:68
  45.1 0.6 compare_and_fusion.1
  45.7 0.6 fusion.20
  46.3 0.4 convolution_convert_fusion
  46.7 62.5 %all-to-all-done = bf16[64,16,256]{2,1,0:T(8,128)(2,1)S(1)} async-done(((bf16[64,16,256]{2,1,0:T(8,128)(2,1)}), bf16[64,16,256]{2,1,0:T(8,128)(2,1)S(1)}, u32[]{:S(2)}, u32[]{:S(2)}) %all-to-all-start) | async-done | bytes 524320 | tf_op jit(solution)/shard_map/all_to_all | solution.py:68
  109.2 0.6 gather_fusion.1
  109.8 1.4 fusion.6
  111.4 2.5 scatter_fusion
  114.0 0.9 fusion.28
  114.9 6.2 all-to-all-start.1
  121.4 64.1 %all-to-all-done.1 = bf16[64,16,256]{2,1,0:T(8,128)(2,1)S(1)} async-done(((bf16[64,16,256]{2,1,0:T(8,128)(2,1)}), bf16[64,16,256]{2,1,0:T(8,128)(2,1)S(1)}, u32[]{:S(2)}, u32[]{:S(2)}) %all-to-all-start.1) | async-done | bytes 524320 | tf_op jit(solution)/shard_map/all_to_all | solution.py:78
  185.5 0.2 convert_select_fusion.1
  185.7 6.5 scatter_fusion.1
  192.2 0.8 convert_element_type.84
  193.2 88.8 %reduce-scatter.3.cloned.1.call-done = bf16[64,256]{1,0:T(8,128)(2,1)} async-done(((bf16[1024,256]{1,0:T(8,128)(2,1)}), bf16[64,256]{1,0:T(8,128)(2,1)}) %reduce-scatter.3.cloned.1.call-update) | async-done | bytes 32784 | tf_op jit(solution)/shard_map/reduce_scatter | solution.py:86
  282.0 0.8 divide_convert_fusion
  283.1 1.6 convert_reduce_fusion.1
  284.9 0.4 copy-done.10
  285.3 17.3 %all_gather.3 = bf16[1024,256]{1,0:T(8,128)(2,1)S(1)} all-gather(bf16[64,256]{1,0:T(8,128)(2,1)S(1)} %fusion.3), channel_id=1, replica_groups=mesh['dom'=64,'dp'=16] {'dp'}, dimensions={0}, use_global_device_ids=true | all-gather | bytes 557056 | tf_op jit(solution)/shard_map/all_gather | solution.py:92
  302.6 3.9 gather_fusion.2
  306.6 0.2 broadcast_select_fusion
  306.8 1.0 broadcast_select_fusion.2
  307.8 31.5 %all-to-all-start.2 = ((bf16[64,16,256]{2,1,0:T(8,128)(2,1)}), bf16[64,16,256]{2,1,0:T(8,128)(2,1)S(1)}, u32[]{:S(2)}, u32[]{:S(2)}) async-start(bf16[64,16,256]{2,1,0:T(8,128)(2,1)} %broadcast_select_fusion.2), calls=%async_computation.3 | async-start | bytes 1048576 | tf_op jit(solution)/shard_map/all_to_all | solution.py:68
  339.3 64.0 %all-to-all-done.2 = bf16[64,16,256]{2,1,0:T(8,128)(2,1)S(1)} async-done(((bf16[64,16,256]{2,1,0:T(8,128)(2,1)}), bf16[64,16,256]{2,1,0:T(8,128)(2,1)S(1)}, u32[]{:S(2)}, u32[]{:S(2)}) %all-to-all-start.2) | async-done | bytes 524320 | tf_op jit(solution)/shard_map/all_to_all | solution.py:68
  403.5 0.6 gather_fusion.3
  404.1 0.4 fusion.4
  404.4 0.2 broadcast.77
  404.7 1.3 scatter_fusion.2
  406.2 0.9 fusion.27
  407.1 6.4 all-to-all-start.3
  413.6 64.2 %all-to-all-done.3 = bf16[64,16,256]{2,1,0:T(8,128)(2,1)S(1)} async-done(((bf16[64,16,256]{2,1,0:T(8,128)(2,1)}), bf16[64,16,256]{2,1,0:T(8,128)(2,1)S(1)}, u32[]{:S(2)}, u32[]{:S(2)}) %all-to-all-start.3) | async-done | bytes 524320 | tf_op jit(solution)/shard_map/all_to_all | solution.py:78
  477.9 0.2 convert_select_fusion
  478.1 6.5 scatter_fusion.3
  484.6 0.8 convert_element_type.96
  485.5 0.8 convert_reduce_fusion
  486.3 152.2 %all-reduce = (f32[256]{0:T(256)}, f32[256]{0:T(256)}) all-reduce(f32[256]{0:T(256)S(1)} %get-tuple-element.59, f32[256]{0:T(256)S(1)} %get-tuple-element.58), channel_id=1, replica_groups=mesh['dom'=64,'dp'=16] {'dom','dp'}, use_global_device_ids=true, to_apply=%region_8.11 | all-reduce | flops 512 | bytes 4096 | tf_op jit(solution)/shard_map/psum | solution.py:158
  638.5 1.7 convolution_multiply_fusion.1
  640.2 1.1 convolution_multiply_fusion
  641.3 0.8 fusion
  642.1 1.6 fusion.2
  643.6 863.3 %all-reduce.4.cloned.1.call-done = (f32[512,256]{1,0:T(8,128)}, f32[256,256]{1,0:T(8,128)}) async-done(((f32[512,256]{1,0:T(8,128)}, f32[256,256]{1,0:T(8,128)}), (f32[512,256]{1,0:T(8,128)}, f32[256,256]{1,0:T(8,128)})) %all-reduce.4.cloned.1.call-update) | async-done | bytes 786448 | tf_op jit(solution)/shard_map/psum | solution.py:158
  1506.9 1.9 copy.28
  1508.8 1.7 copy.29
  (77 shorter events, 1.8 us)
Async XLA Ops:
  7.2 275.9 %copy-start = (bf16[256,256]{1,0:T(8,128)(2,1)S(1)}, bf16[256,256]{1,0:T(8,128)(2,1)}, u32[]{:S(2)}) copy-start(bf16[256,256]{1,0:T(8,128)(2,1)} %param.23) | copy-start | bytes 393220
  8.0 0.9 copy-start.8
  8.1 5.3 copy-start.14
  13.4 31.7 %copy-start.17 = (s32[1,1,8,2]{2,3,1,0:T(2,128)S(1)}, s32[1,1,8,2]{2,3,1,0:T(2,128)}, u32[]{:S(2)}) copy-start(s32[1,1,8,2]{2,3,1,0:T(2,128)} %param.20) | copy-start | bytes 196
  13.5 32.8 %copy-start.16 = (s32[1,1,8,2,128]{4,3,2,1,0:T(2,128)S(1)}, s32[1,1,8,2,128]{4,3,2,1,0:T(2,128)}, u32[]{:S(2)}) copy-start(s32[1,1,8,2,128]{4,3,2,1,0:T(2,128)} %param.19) | copy-start | bytes 24580
  13.5 95.7 %copy-start.1 = (bf16[1024,256]{1,0:T(8,128)(2,1)S(1)}, bf16[1024,256]{1,0:T(8,128)(2,1)}, u32[]{:S(2)}) copy-start(bf16[1024,256]{1,0:T(8,128)(2,1)} %param.15) | copy-start | bytes 1572868
  14.7 94.5 %all-to-all-start = ((bf16[64,16,256]{2,1,0:T(8,128)(2,1)}), bf16[64,16,256]{2,1,0:T(8,128)(2,1)S(1)}, u32[]{:S(2)}, u32[]{:S(2)}) async-start(bf16[64,16,256]{2,1,0:T(8,128)(2,1)} %broadcast_select_fusion.3), calls=%async_computation | async-start | bytes 1048576 | tf_op jit(solution)/shard_map/all_to_all | solution.py:68
  114.0 7.2 copy-start.9
  114.9 70.6 %all-to-all-start.1 = ((bf16[64,16,256]{2,1,0:T(8,128)(2,1)}), bf16[64,16,256]{2,1,0:T(8,128)(2,1)S(1)}, u32[]{:S(2)}, u32[]{:S(2)}) async-start(bf16[64,16,256]{2,1,0:T(8,128)(2,1)} %bitcast.12), calls=%async_computation.1 | async-start | bytes 1048576 | tf_op jit(solution)/shard_map/all_to_all | solution.py:78
  121.1 160.9 %reduce-scatter.3.cloned.1.call-start = ((), (), s32[]{:S(2)}) async-start(), calls=%async_computation.6 | async-start | bytes 557056 | tf_op jit(solution)/shard_map/reduce_scatter | solution.py:86
  192.2 0.9 copy-start.18
  192.2 90.7 %copy-start.2 = (bf16[512,256]{1,0:T(8,128)(2,1)S(1)}, bf16[512,256]{1,0:T(8,128)(2,1)}, u32[]{:S(2)}) copy-start(bf16[512,256]{1,0:T(8,128)(2,1)} %param.21) | copy-start | bytes 786436
  192.2 90.7 %copy-start.22 = (f32[256]{0:T(256)S(1)}, f32[256]{0:T(256)}, u32[]{:S(2)}) copy-start(f32[256]{0:T(256)} %param.22) | copy-start | bytes 3076
  193.2 91.6 %copy-start.4 = (bf16[64,256]{1,0:T(8,128)(2,1)}, bf16[64,256]{1,0:T(8,128)(2,1)S(1)}, u32[]{:S(2)}) copy-start(bf16[64,256]{1,0:T(8,128)(2,1)S(1)} %constant_dynamic-slice_fusion) | copy-start | bytes 98308
  282.9 2.0 copy-start.6
  283.1 1.8 copy-start.12
  284.7 0.6 copy-start.10
  302.6 4.0 copy-start.15
  306.6 32.8 %copy-start.19 = (s32[8]{0:T(128)S(1)}, s32[8]{0:T(128)}, u32[]{:S(2)}) copy-start(s32[8]{0:T(128)} %get-tuple-element.43) | copy-start | bytes 100
  307.8 96.3 %copy-start.21 = (pred[8]{0:T(512)(128)(4,1)S(1)}, pred[8]{0:T(512)(128)(4,1)}, u32[]{:S(2)}) copy-start(pred[8]{0:T(512)(128)(4,1)} %get-tuple-element.42) | copy-start | bytes 28
  307.8 95.6 %all-to-all-start.2 = ((bf16[64,16,256]{2,1,0:T(8,128)(2,1)}), bf16[64,16,256]{2,1,0:T(8,128)(2,1)S(1)}, u32[]{:S(2)}, u32[]{:S(2)}) async-start(bf16[64,16,256]{2,1,0:T(8,128)(2,1)} %broadcast_select_fusion.2), calls=%async_computation.3 | async-start | bytes 1048576 | tf_op jit(solution)/shard_map/all_to_all | solution.py:68
  404.0 0.7 copy-start.20
  407.1 70.8 %all-to-all-start.3 = ((bf16[64,16,256]{2,1,0:T(8,128)(2,1)}), bf16[64,16,256]{2,1,0:T(8,128)(2,1)S(1)}, u32[]{:S(2)}, u32[]{:S(2)}) async-start(bf16[64,16,256]{2,1,0:T(8,128)(2,1)} %bitcast.20), calls=%async_computation.4 | async-start | bytes 1048576 | tf_op jit(solution)/shard_map/all_to_all | solution.py:78
  413.5 228.6 %reduce-scatter.5.cloned.1.call-start = ((), (), s32[]{:S(2)}) async-start(), calls=%async_computation.7 | async-start | bytes 557056 | tf_op jit(solution)/shard_map/reduce_scatter | solution.py:86
  484.5 1.8 copy-start.23
  484.5 153.9 %copy-start.13 = (f32[64,256]{1,0:T(8,128)S(1)}, f32[64,256]{1,0:T(8,128)}, u32[]{:S(2)}) copy-start(f32[64,256]{1,0:T(8,128)} %copy-done.12) | copy-start | bytes 196612
  484.6 155.6 %copy-start.5 = (bf16[64,256]{1,0:T(8,128)(2,1)S(1)}, bf16[64,256]{1,0:T(8,128)(2,1)}, u32[]{:S(2)}) copy-start(bf16[64,256]{1,0:T(8,128)(2,1)} %copy-done.4) | copy-start | bytes 98308
  484.6 155.6 %copy-start.7 = (bf16[64,256]{1,0:T(8,128)(2,1)S(1)}, bf16[64,256]{1,0:T(8,128)(2,1)}, u32[]{:S(2)}) copy-start(bf16[64,256]{1,0:T(8,128)(2,1)} %copy-done.6) | copy-start | bytes 98308
  484.6 155.6 %copy-start.11 = (bf16[64,256]{1,0:T(8,128)(2,1)S(1)}, bf16[64,256]{1,0:T(8,128)(2,1)}, u32[]{:S(2)}) copy-start(bf16[64,256]{1,0:T(8,128)(2,1)} %copy-done.10) | copy-start | bytes 98308
  484.6 156.7 %copy-start.24 = (f32[256]{0:T(256)S(1)}, f32[256]{0:T(256)}, u32[]{:S(2)}) copy-start(f32[256]{0:T(256)} %param.24) | copy-start | bytes 3076
  484.6 157.5 %copy-start.3 = (bf16[512,256]{1,0:T(8,128)(2,1)S(1)}, bf16[512,256]{1,0:T(8,128)(2,1)}, u32[]{:S(2)}) copy-start(bf16[512,256]{1,0:T(8,128)(2,1)} %param.21) | copy-start | bytes 786436
  485.5 1021.4 %all-reduce.4.cloned.1.call-start = ((), (), s32[]{:S(2)}) async-start(), calls=%async_computation.8 | async-start | bytes 1572864 | tf_op jit(solution)/shard_map/psum | solution.py:158
Sparse Core Ops, SparseCore 0:
  193.2 88.7 reduce-scatter.2
  485.6 86.0 reduce-scatter.4
  641.4 865.4 all-reduce.3
where the time goes:
time: 1520 us
  waiting for transfers between devices  1210 us (80%)
  blocking collectives  169 us (11%)
  starting transfers between devices  74.7 us (5%)
  other arithmetic  25.4 us (2%)
  local copies, waits for them, and re-layouts  17 us (1%)
    psum x1, waiting for transfers between devices, on_device(): lax.psum((local_w_in, local_b_in, local_w_out, local_b_out), ('dom', 'dp'))  863 us
    psum x1, blocking collectives, on_device(): lax.psum((local_w_in, local_b_in, local_w_out, local_b_out), ('dom', 'dp'))  152 us
    all_to_all x2, waiting for transfers between devices, return_partials(): lax.all_to_all(outgoing, 'dom', split_axis=0, concat_axis=0, tiled=True)  128 us
    all_to_all x2, waiting for transfers between devices, copy_mirrors(): lax.all_to_all(picked, 'dom', split_axis=0, concat_axis=0, tiled=True)  127 us
    reduce_scatter x2, waiting for transfers between devices, return_partials(): lax.psum_scatter(owned_sum.astype(jnp.bfloat16), 'dp', scatter_dimension=...  88.8 us
    all_to_all x2, starting transfers between devices, copy_mirrors(): lax.all_to_all(picked, 'dom', split_axis=0, concat_axis=0, tiled=True)  61.9 us
  transfers between devices with their start and end apart: 7, of which 6 were waited for; matrix products, arithmetic and copies ran while one was open for 1% of the time, Pallas kernels for 0%

commit v1 on v0

v1 whole, which is shorter than its diff:
```python
import math

import jax
import jax.numpy as jnp
from jax import lax
from jax.experimental import pallas as pl
from jax.experimental.pallas import tpu as pltpu
from jax.sharding import PartitionSpec as P

BF = jnp.bfloat16
F32 = jnp.float32
LANES = 128
UNROLL = 8


def matmul(a, b, ca=1, cb=0):
    return lax.dot_general(a, b, (((ca,), (cb,)), ((), ())), preferred_element_type=F32)


def hot(condition):
    return jnp.where(condition, 1.0, 0.0).astype(BF)


def row_choice(slots_row, first, count):
    width = slots_row.shape[1]
    rows = lax.broadcasted_iota(jnp.int32, (count, width), 0)
    return hot(rows == slots_row - first)


def peer_choice(n_peers, n_slots):
    cap = n_slots // n_peers
    peers = lax.broadcasted_iota(jnp.int32, (n_peers, n_slots), 0)
    slots = lax.broadcasted_iota(jnp.int32, (n_peers, n_slots), 1)
    return hot((slots >= peers * cap) & (slots < peers * cap + cap))


def pick(table, slots_row):
    total = None
    for first in range(0, table.shape[1], LANES):
        choice = row_choice(slots_row, first, LANES)
        part = matmul(table[:, first : first + LANES], choice)
        total = part if total is None else total + part
    return total


def scatter(values, slots_row, count):
    parts = []
    for first in range(0, count, LANES):
        choice = row_choice(slots_row, first, LANES)
        parts.append(matmul(values, choice, 1, 1))
    return jnp.concatenate(parts, 1)


def cap_lane(shape, cap):
    return lax.rem(lax.broadcasted_iota(jnp.int32, shape, 1), cap)


def to_peers(columns, n_peers):
    k, n_slots = columns.shape
    cap = n_slots // n_peers
    lane = cap_lane(columns.shape, cap)
    spread_out = jnp.concatenate(
        [jnp.where(lane == c, columns, 0.0).astype(BF) for c in range(cap)], 0
    )
    return matmul(peer_choice(n_peers, n_slots), spread_out, 1, 1).astype(BF)


def from_peers(arrived, cap):
    n_peers, width = arrived.shape
    k = width // cap
    n_slots = n_peers * cap
    wide = matmul(arrived, peer_choice(n_peers, n_slots), 0, 0)
    lane = cap_lane((k, n_slots), cap)
    total = jnp.zeros((k, n_slots), F32)
    for c in range(cap):
        total = jnp.where(lane == c, wide[c * k : c * k + k], total)
    return total


def first_kernel(features_ref, slots_ref, replica_ref, table_ref, payload_ref):
    k = table_ref.shape[0]
    rows = lax.broadcasted_iota(jnp.int32, (k, features_ref.shape[1]), 0)
    columns = lax.broadcasted_iota(jnp.int32, (k, features_ref.shape[1]), 1)
    mine = hot(columns == rows + replica_ref[0] * k)
    table = matmul(mine, features_ref[...], 1, 1).astype(BF)
    table_ref[...] = table
    payload_ref[...] = to_peers(pick(table, slots_ref[...]), payload_ref.shape[0])


def edges_kernel(
    transpose, arrived_ref, owned_ref, edges_ref, blocks_ref, payload_ref, own_ref, table, total
):
    k, v_count = owned_ref.shape
    n_peers = arrived_ref.shape[0]
    cap = arrived_ref.shape[1] // k
    own_blocks = v_count // LANES
    all_blocks = table.shape[0]
    mirrors = from_peers(arrived_ref[...], cap).astype(BF)
    owned = owned_ref[...]
    for b in range(own_blocks):
        table[b] = owned[:, b * LANES : b * LANES + LANES]
    for b in range(own_blocks, all_blocks):
        first = (b - own_blocks) * LANES
        table[b] = mirrors[:, first : first + LANES]
    total[...] = jnp.zeros_like(total)
    n_groups, group_rows, width = edges_ref.shape
    per_group = UNROLL
    positions = lax.broadcasted_iota(jnp.int32, (LANES, width), 0)
    a, b = (1, 0) if transpose else (0, 1)

    def group(g, carry):
        gathered = []
        for t in range(per_group):
            block = blocks_ref[g, 2 * t + a]
            slots = edges_ref[g, 2 * t + a : 2 * t + a + 1, :]
            gathered.append(matmul(table[block], hot(positions == slots)).astype(BF))
        placed = []
        for t in range(per_group):
            slots = edges_ref[g, 2 * t + b : 2 * t + b + 1, :]
            placed.append(matmul(gathered[t], hot(positions == slots), 1, 1))
        for t in range(per_group):
            block = blocks_ref[g, 2 * t + b]
            total[block] = total[block] + placed[t]
        return carry

    lax.fori_loop(0, n_groups, group, 0)
    for b in range(own_blocks):
        own_ref[:, b * LANES : b * LANES + LANES] = total[b]
    back = jnp.concatenate([total[b] for b in range(own_blocks, all_blocks)], 1)
    payload_ref[...] = to_peers(back, n_peers)


def aggregate_kernel(arrived_ref, own_ref, slots_ref, degree_ref, aggregate_ref, copies_ref):
    k, v_count = own_ref.shape
    cap = arrived_ref.shape[1] // k
    returned = from_peers(arrived_ref[...], cap).astype(BF)
    summed = own_ref[...] + scatter(returned, slots_ref[...], v_count)
    aggregate = (summed / degree_ref[...]).astype(BF)
    aggregate_ref[...] = aggregate
    for r in range(copies_ref.shape[0]):
        copies_ref[r] = aggregate


def dense_kernel(
    aggregate_ref, self_ref, gh_ref, w_in_ref, degree_ref, slots_ref, replica_ref,
    hidden_ref, grad_pre_ref, spread_ref, payload_ref,
):
    k = spread_ref.shape[0]
    channels = aggregate_ref.shape[0]
    w_neigh = w_in_ref[channels:, :]
    pre = self_ref[...] + matmul(w_neigh, aggregate_ref[...], 0, 0)
    sigmoid = 1.0 / (1.0 + jnp.exp(-pre))
    hidden_ref[...] = (pre * sigmoid).astype(BF)
    grad_pre = (gh_ref[...] * (sigmoid * (1.0 + pre * (1.0 - sigmoid)))).astype(BF)
    grad_pre_ref[...] = grad_pre
    first = pl.multiple_of(channels + replica_ref[0] * k, k)
    spread = matmul(w_in_ref[pl.ds(first, k), :], grad_pre)
    spread = (spread / degree_ref[...]).astype(BF)
    spread_ref[...] = spread
    payload_ref[...] = to_peers(pick(spread, slots_ref[...]), payload_ref.shape[0])


def weights_kernel(
    scale, hidden_ref, grad_pre_ref, cotangent_ref, table_ref, aggregate_ref, w_in_ref, w_out_ref,
    b_out_ref, replica_ref, output_ref, grad_self_ref, grads_ref, rows_ref,
):
    k, v_count = table_ref.shape
    channels = hidden_ref.shape[0]
    share = output_ref.shape[0]
    replica = replica_ref[0]
    per_block = LANES // share
    block = pl.multiple_of((replica // per_block) * LANES, LANES)
    half = pl.multiple_of(lax.rem(replica, per_block) * share, share)
    rows_ref[...] = matmul(hidden_ref[:, pl.ds(block, LANES)], w_out_ref[...], 0, 0)
    output_ref[...] = (rows_ref[pl.ds(half, share), :] + b_out_ref[...]).astype(BF)
    grad_pre = grad_pre_ref[...]
    self_t = matmul(w_in_ref[:channels, :], grad_pre_ref[:, pl.ds(block, LANES)])
    rows_ref[...] = self_t.T
    grad_self_ref[...] = rows_ref[pl.ds(half, share), :]
    ones = jnp.ones((k, v_count), BF)
    left = jnp.concatenate([table_ref[...], aggregate_ref[...], ones], 0)
    grads_in = matmul(left, grad_pre, 1, 1) * scale
    first = pl.multiple_of(replica * k, k)
    left_out = jnp.concatenate([hidden_ref[pl.ds(first, k), :], ones], 0)
    grads_out = matmul(left_out, cotangent_ref[...]) * scale
    grads_ref[...] = jnp.zeros_like(grads_ref)
    grads_ref[: 2 * k, :] = grads_in[: 2 * k]
    grads_ref[2 * k : 3 * k, :] = grads_out[:k]
    grads_ref[3 * k : 3 * k + 1, :] = grads_in[2 * k : 2 * k + 1]
    grads_ref[3 * k + 1 : 3 * k + 2, :] = grads_out[k : k + 1]


def back_kernel(arrived_ref, own_ref, slots_ref, copies_ref):
    k, v_count = own_ref.shape
    cap = arrived_ref.shape[1] // k
    n_dp = copies_ref.shape[0]
    share = v_count // n_dp
    returned = from_peers(arrived_ref[...], cap).astype(BF)
    summed = (own_ref[...] + scatter(returned, slots_ref[...], v_count)).astype(BF)
    for r in range(n_dp):
        first = r * share // LANES * LANES
        copies_ref[r] = summed[:, first : first + LANES]


def last_kernel(arrived_ref, grad_self_ref, replica_ref, grad_features_ref, rows_ref):
    share = grad_features_ref.shape[0]
    half = pl.multiple_of(lax.rem(replica_ref[0], LANES // share) * share, share)
    rows_ref[...] = arrived_ref[...].astype(F32).T
    grad_features_ref[...] = (rows_ref[pl.ds(half, share), :] + grad_self_ref[...]).astype(BF)


def call(kernel, outs, args, smem=(), scratch=(), flops=0, name=None):
    in_specs = [
        pl.BlockSpec(memory_space=pltpu.SMEM if i in smem else pltpu.VMEM) for i in range(len(args))
    ]
    shapes = [jax.ShapeDtypeStruct(s, d) for s, d in outs]
    size = sum(math.prod(s) * jnp.dtype(d).itemsize for s, d in outs)
    size += sum(x.size * x.dtype.itemsize for x in args)
    return pl.pallas_call(
        kernel,
        out_shape=shapes,
        in_specs=in_specs,
        out_specs=[pl.BlockSpec(memory_space=pltpu.VMEM) for _ in outs],
        scratch_shapes=list(scratch),
        compiler_params=pltpu.CompilerParams(vmem_limit_bytes=48 * 1024 * 1024),
        cost_estimate=pl.CostEstimate(flops=flops, bytes_accessed=size, transcendentals=0),
        name=name,
    )(*args)


def swap(values, axis):
    return lax.all_to_all(values, axis, split_axis=0, concat_axis=0, tiled=True)


def on_device(
    features,
    degree,
    send_rows,
    send_counts,
    edge_slots,
    tile_blocks,
    w_in,
    b_in,
    w_out,
    b_out,
    cotangent,
):
    n_dp = lax.axis_size("dp")
    n_dom = lax.axis_size("dom")
    replica = lax.axis_index("dp").astype(jnp.int32).reshape(1)
    v_count, channels = features.shape
    cap = send_rows.shape[2]
    k = channels // n_dp
    share = v_count // n_dp
    n_slots = n_dom * cap
    n_tiles, _, tile_rows = edge_slots.shape[2:]
    blocks_count = (v_count + n_slots) // LANES
    scale = 1.0 / math.sqrt(v_count * n_dom)

    usable = jnp.arange(cap, dtype=jnp.int32)[None, :] < send_counts[0][:, None]
    slots_row = jnp.where(usable, send_rows[0], -1).reshape(1, n_slots)
    degree_row = degree.astype(F32).reshape(1, v_count)

    table, payload = call(
        first_kernel,
        [((k, v_count), BF), ((n_dom, channels), BF)],
        [features, slots_row, replica],
        smem=(2,),
        name="first",
    )
    edge_rows = edge_slots[0, 0].reshape(2 * n_tiles, tile_rows)
    block_row = jnp.pad(tile_blocks[0, 0].reshape(1, 2 * n_tiles), ((0, 7), (0, tile_rows - 2 * n_tiles)))
    edge_rows = jnp.concatenate([edge_rows, block_row], 0)
    edges = swap(jnp.broadcast_to(edge_rows[None], (n_dp, *edge_rows.shape)), "dp")
    blocks = edges[:, 2 * n_tiles, : 2 * n_tiles]
    arrived = swap(payload, "dom")

    w_self = w_in[:channels]
    self_t = jnp.einsum("ah,va->hv", w_self, features, preferred_element_type=F32) + b_in[:, None]
    gh_t = jnp.einsum("ho,vo->hv", w_out, cotangent, preferred_element_type=F32)

    def edge_pass(arrived, owned, transpose):
        return call(
            lambda *refs: edges_kernel(transpose, *refs),
            [((n_dom, channels), BF), ((k, v_count), F32)],
            [arrived, owned, edges, blocks],
            smem=(3,),
            scratch=[
                pltpu.VMEM((blocks_count, k, LANES), BF),
                pltpu.VMEM((blocks_count, k, LANES), F32),
            ],
            name="edges_back" if transpose else "edges",
        )

    payload, own = edge_pass(arrived, table, False)
    arrived = swap(payload, "dom")
    aggregate, copies = call(
        aggregate_kernel,
        [((k, v_count), BF), ((n_dp, k, v_count), BF)],
        [arrived, own, slots_row, degree_row],
        name="aggregate",
    )
    aggregate_all = swap(copies, "dp").reshape(channels, v_count)

    hidden, grad_pre, spread, payload = call(
        dense_kernel,
        [((channels, v_count), BF), ((channels, v_count), BF), ((k, v_count), BF), ((n_dom, channels), BF)],
        [aggregate_all, self_t, gh_t, w_in, degree_row, slots_row, replica],
        smem=(6,),
        name="dense",
    )
    arrived = swap(payload, "dom")
    output, grad_self, grads = call(
        lambda *refs: weights_kernel(scale, *refs),
        [((share, channels), BF), ((share, channels), F32), ((n_dom, channels), F32)],
        [hidden, grad_pre, cotangent, table, aggregate, w_in, w_out, b_out.reshape(1, -1), replica],
        smem=(8,),
        scratch=[pltpu.VMEM((LANES, channels), F32)],
        name="weights",
    )
    payload, own = edge_pass(arrived, spread, True)
    grads = swap(grads, "dom")
    arrived = swap(payload, "dom")
    (copies,) = call(
        back_kernel,
        [((n_dp, k, LANES), BF)],
        [arrived, own, slots_row],
        name="back",
    )
    arrived = swap(copies, "dp").reshape(channels, LANES)
    (grad_features,) = call(
        last_kernel,
        [((share, channels), BF)],
        [arrived, grad_self, replica],
        smem=(2,),
        scratch=[pltpu.VMEM((LANES, channels), F32)],
        name="last",
    )
    my_row = jnp.sum(grads, 0)
    rows = swap(jnp.broadcast_to(my_row[None], (n_dom, channels)), "dom")
    used = 3 * k + 2
    rows = rows[:used]
    everything = swap(jnp.broadcast_to(rows[None], (n_dp, used, channels)), "dp")
    grad_w_in = jnp.concatenate(
        [everything[:, :k].reshape(channels, channels), everything[:, k : 2 * k].reshape(channels, channels)], 0
    )
    grad_w_out = everything[:, 2 * k : 3 * k].reshape(channels, channels)
    grad_b_in = everything[0, 3 * k]
    grad_b_out = everything[0, 3 * k + 1]
    return (output, grad_features, grad_w_in, grad_b_in, grad_w_out, grad_b_out)


def solution(mesh):
    in_specs = (
        P("dom", None),
        P("dom"),
        P("dom", None, None),
        P("dom", None),
        P("dom", "dp", None, None, None),
        P("dom", "dp", None, None),
        P(),
        P(),
        P(),
        P(),
        P("dom", None),
    )
    out_specs = (P(("dom", "dp"), None), P(("dom", "dp"), None), P(), P(), P(), P())
    return jax.shard_map(
        on_device, mesh=mesh, in_specs=in_specs, out_specs=out_specs, check_vma=False
    )
```

time: 1520 us -> 282 us (0.19)
  waiting for transfers between devices: 1210 us -> 153 us
  blocking collectives: 169 us -> 0 us
  Pallas kernels: 0 us -> 21.2 us
  other arithmetic: 25.4 us -> 4.4 us
    psum x1 -> x0, waiting for transfers between devices: 863 us -> none  [on_device(): lax.psum((local_w_in, local_b_in, local_w_out, local_b_out), ('dom', 'dp'))]
    psum x1 -> x0, blocking collectives: 152 us -> none  [on_device(): lax.psum((local_w_in, local_b_in, local_w_out, local_b_out), ('dom', 'dp'))]
    all_to_all x4 -> x10, waiting for transfers between devices: 255 us -> 153 us  [swap(): return lax.all_to_all(values, axis, split_axis=0, concat_axis=0, tiled=True)]
    reduce_scatter x2 -> x0, waiting for transfers between devices: 88.8 us -> none  [return_partials(): lax.psum_scatter(owned_sum.astype(jnp.bfloat16), 'dp', scatter_dimension=...]
    pallas_call x0 -> x8, Pallas kernels: none -> 21.2 us  [call(): pl.pallas_call(kernel, out_shape=shapes, in_specs=in_specs, out_specs=[pl...]
    all_gather x1 -> x0, blocking collectives: 17.3 us -> none  [replica_rows(): return lax.all_gather(values, 'dp', axis=0, tiled=True)]
    scatter-add x4 -> x0, other arithmetic: 16.7 us -> none  [the longest x2 12.9 us: return_partials(): owned_sum = rounded[:own_count].astype(jnp.float32).at[owned.reshape(-1)]...]
    all_to_all x4 -> x10, starting transfers between devices: 74.5 us -> 80.1 us  [swap(): return lax.all_to_all(values, axis, split_axis=0, concat_axis=0, tiled=True)]
  transfers between devices with their start and end apart: 7 -> 10, of which waited for: 6 -> 10; matrix products, arithmetic and copies ran while one was open for 1% -> 2% of each run, Pallas kernels for 0% -> 4%
where the time goes in v1:
time: 282 us; the launch traced here: 279 us
  waiting for transfers between devices  153 us (54%)
  starting transfers between devices  80.1 us (28%)
  Pallas kernels  21.2 us (8%)
  local copies, waits for them, and re-layouts  18.7 us (7%)
  other arithmetic  4.4 us (2%)
    all_to_all x10, waiting for transfers between devices, swap(): return lax.all_to_all(values, axis, split_axis=0, concat_axis=0, tiled=True)  153 us
    all_to_all x10, starting transfers between devices, swap(): return lax.all_to_all(values, axis, split_axis=0, concat_axis=0, tiled=True)  80.1 us
    pallas_call x8, Pallas kernels, call(): pl.pallas_call(kernel, out_shape=shapes, in_specs=in_specs, out_specs=[pl...  21.2 us
    unnamed x55, local copies, waits for them, and re-layouts  13.6 us
  transfers between devices with their start and end apart: 10, of which 10 were waited for; matrix products, arithmetic and copies ran while one was open for 2% of the time, Pallas kernels for 4%

profile of v1, /device:TPU:1, one launch (start us, length us, event | category | flops | bytes accessed | tf_op | source)
XLA Modules:
  0.0 278.7 jit_solution(832214613216218259)
XLA Ops:
  0.7 0.8 copy.35
  1.6 0.7 broadcast_in_dim.13
  2.3 7.6 %all-to-all-start.1 = ((s32[16,24,128]{2,1,0:T(8,128)}), s32[16,24,128]{2,1,0:T(8,128)S(1)}, u32[]{:S(2)}, u32[]{:S(2)}) async-start(s32[16,24,128]{2,1,0:T(8,128)} %broadcast_in_dim.13), calls=%async_computation.1 | async-start | bytes 393216 | tf_op jit(solution)/shard_map/all_to_all | solution.py:232
  9.9 0.6 copy-done.19
  11.5 1.0 first.1
  13.0 0.7 reduce.1
  14.3 2.8 all-to-all-done.1.refs_2_
  17.0 31.0 %all-to-all-start = ((bf16[64,2,128]{2,1,0:T(2,128)(2,1)}), bf16[64,2,128]{2,1,0:T(2,128)(2,1)S(1)}, u32[]{:S(2)}, u32[]{:S(2)}) async-start(bf16[64,2,128]{2,1,0:T(2,128)(2,1)} %reshape.99), calls=%async_computation | async-start | bytes 65536 | tf_op jit(solution)/shard_map/all_to_all | solution.py:232
  48.1 22.3 %all-to-all-done = bf16[64,2,128]{2,1,0:T(2,128)(2,1)S(1)} async-done(((bf16[64,2,128]{2,1,0:T(2,128)(2,1)}), bf16[64,2,128]{2,1,0:T(2,128)(2,1)S(1)}, u32[]{:S(2)}, u32[]{:S(2)}) %all-to-all-start) | async-done | bytes 32800 | tf_op jit(solution)/shard_map/all_to_all | solution.py:232
  70.4 6.9 %edges.1 = (bf16[64,256]{1,0:T(8,128)(2,1)S(1)}, f32[16,1024]{1,0:T(8,128)S(1)}) custom-call(bf16[64,256]{1,0:T(8,128)(2,1)S(1)} %bitcast.43, bf16[16,1024]{1,0:T(8,128)(2,1)S(1)} %get-tuple-element.22.refs_1_.refs_3_, s32[16,24,128]{2,1,0:T(8,128)S(1)} %all-to-all-done.1.refs_2_, s32[16,16]{1,0:T(8,128)S(1)} %bitcast.46), custom_call_target="tpu_custom_call" | custom-call | bytes 361472 | tf_op jit(solution)/shard_map/edges/pallas_call | solution.py:219
  77.4 0.7 reduce.2
  78.7 5.8 %all-to-all-start.2 = ((bf16[64,2,128]{2,1,0:T(2,128)(2,1)}), bf16[64,2,128]{2,1,0:T(2,128)(2,1)S(1)}, u32[]{:S(2)}, u32[]{:S(2)}) async-start(bf16[64,2,128]{2,1,0:T(2,128)(2,1)} %reshape.101), calls=%async_computation.2 | async-start | bytes 65536 | tf_op jit(solution)/shard_map/all_to_all | solution.py:232
  84.5 22.0 %all-to-all-done.2 = bf16[64,2,128]{2,1,0:T(2,128)(2,1)S(1)} async-done(((bf16[64,2,128]{2,1,0:T(2,128)(2,1)}), bf16[64,2,128]{2,1,0:T(2,128)(2,1)S(1)}, u32[]{:S(2)}, u32[]{:S(2)}) %all-to-all-start.2) | async-done | bytes 32800 | tf_op jit(solution)/shard_map/all_to_all | solution.py:232
  106.5 1.7 aggregate.1
  108.2 3.7 %all-to-all-start.3 = ((bf16[16,16,1024]{2,1,0:T(8,128)(2,1)}), bf16[16,16,1024]{2,1,0:T(8,128)(2,1)S(1)}, u32[]{:S(2)}, u32[]{:S(2)}) async-start(bf16[16,16,1024]{2,1,0:T(8,128)(2,1)} %get-tuple-element.25), calls=%async_computation.3 | async-start | bytes 1048576 | tf_op jit(solution)/shard_map/all_to_all | solution.py:232
  113.3 8.3 %all-to-all-done.3 = bf16[16,16,1024]{2,1,0:T(8,128)(2,1)S(1)} async-done(((bf16[16,16,1024]{2,1,0:T(8,128)(2,1)}), bf16[16,16,1024]{2,1,0:T(8,128)(2,1)S(1)}, u32[]{:S(2)}, u32[]{:S(2)}) %all-to-all-start.3) | async-done | bytes 524320 | tf_op jit(solution)/shard_map/all_to_all | solution.py:232
  121.6 0.9 copy-done.4
  122.5 1.4 dense.1
  124.0 0.8 copy-done.6
  124.8 0.8 copy-done.8
  126.8 1.4 reduce.3
  128.8 6.9 %all-to-all-start.4 = ((bf16[64,2,128]{2,1,0:T(2,128)(2,1)}), bf16[64,2,128]{2,1,0:T(2,128)(2,1)S(1)}, u32[]{:S(2)}, u32[]{:S(2)}) async-start(bf16[64,2,128]{2,1,0:T(2,128)(2,1)} %reshape.103), calls=%async_computation.4 | async-start | bytes 65536 | tf_op jit(solution)/shard_map/all_to_all | solution.py:232
  135.7 0.7 copy-done.14
  136.4 0.9 copy-done.5
  137.3 1.0 copy-done.7
  138.4 1.0 copy-done.9
  139.4 0.9 weights.1
  140.3 0.7 copy.40
  141.0 16.7 %all-to-all-done.4 = bf16[64,2,128]{2,1,0:T(2,128)(2,1)S(1)} async-done(((bf16[64,2,128]{2,1,0:T(2,128)(2,1)}), bf16[64,2,128]{2,1,0:T(2,128)(2,1)S(1)}, u32[]{:S(2)}, u32[]{:S(2)}) %all-to-all-start.4) | async-done | bytes 32800 | tf_op jit(solution)/shard_map/all_to_all | solution.py:232
  157.7 6.1 %all-to-all-start.7 = ((f32[64,1,256]{2,1,0:T(1,128)}), f32[64,1,256]{2,1,0:T(1,128)S(1)}, u32[]{:S(2)}, u32[]{:S(2)}) async-start(f32[64,1,256]{2,1,0:T(1,128)} %copy.40), calls=%async_computation.7 | async-start | bytes 131072 | tf_op jit(solution)/shard_map/all_to_all | solution.py:232
  163.8 0.7 copy-done.12
  164.6 6.9 %edges_back.1 = (bf16[64,256]{1,0:T(8,128)(2,1)S(1)}, f32[16,1024]{1,0:T(8,128)S(1)}) custom-call(bf16[64,256]{1,0:T(8,128)(2,1)S(1)} %bitcast.42, bf16[16,1024]{1,0:T(8,128)(2,1)S(1)} %copy-done.12, s32[16,24,128]{2,1,0:T(8,128)S(1)} %all-to-all-done.1.refs_2_, s32[16,16]{1,0:T(8,128)S(1)} %bitcast.47), custom_call_target="tpu_custom_call" | custom-call | bytes 361472 | tf_op jit(solution)/shard_map/edges_back/pallas_call | solution.py:219
  171.5 0.7 reduce.4
  172.8 16.1 %all-to-all-done.7 = f32[64,1,256]{2,1,0:T(1,128)S(1)} async-done(((f32[64,1,256]{2,1,0:T(1,128)}), f32[64,1,256]{2,1,0:T(1,128)S(1)}, u32[]{:S(2)}, u32[]{:S(2)}) %all-to-all-start.7) | async-done | bytes 65568 | tf_op jit(solution)/shard_map/all_to_all | solution.py:232
  188.9 6.3 %all-to-all-start.5 = ((bf16[64,2,128]{2,1,0:T(2,128)(2,1)}), bf16[64,2,128]{2,1,0:T(2,128)(2,1)S(1)}, u32[]{:S(2)}, u32[]{:S(2)}) async-start(bf16[64,2,128]{2,1,0:T(2,128)(2,1)} %reshape.105), calls=%async_computation.5 | async-start | bytes 65536 | tf_op jit(solution)/shard_map/all_to_all | solution.py:232
  195.3 22.2 %all-to-all-done.5 = bf16[64,2,128]{2,1,0:T(2,128)(2,1)S(1)} async-done(((bf16[64,2,128]{2,1,0:T(2,128)(2,1)}), bf16[64,2,128]{2,1,0:T(2,128)(2,1)S(1)}, u32[]{:S(2)}, u32[]{:S(2)}) %all-to-all-start.5) | async-done | bytes 32800 | tf_op jit(solution)/shard_map/all_to_all | solution.py:232
  217.5 0.7 broadcast_in_dim.14
  218.2 5.6 %all-to-all-start.8 = ((f32[64,1,256]{2,1,0:T(1,128)}), f32[64,1,256]{2,1,0:T(1,128)S(1)}, u32[]{:S(2)}, u32[]{:S(2)}) async-start(f32[64,1,256]{2,1,0:T(1,128)} %broadcast_in_dim.14), calls=%async_computation.8 | async-start | bytes 131072 | tf_op jit(solution)/shard_map/all_to_all | solution.py:232
  223.9 1.5 back.1
  225.5 23.6 %all-to-all-done.8 = f32[64,1,256]{2,1,0:T(1,128)S(1)} async-done(((f32[64,1,256]{2,1,0:T(1,128)}), f32[64,1,256]{2,1,0:T(1,128)S(1)}, u32[]{:S(2)}, u32[]{:S(2)}) %all-to-all-start.8) | async-done | bytes 65568 | tf_op jit(solution)/shard_map/all_to_all | solution.py:232
  249.0 3.5 %all-to-all-start.6 = ((bf16[16,16,128]{2,1,0:T(8,128)(2,1)}), bf16[16,16,128]{2,1,0:T(8,128)(2,1)S(1)}, u32[]{:S(2)}, u32[]{:S(2)}) async-start(bf16[16,16,128]{2,1,0:T(8,128)(2,1)} %back.1), calls=%async_computation.6 | async-start | bytes 131072 | tf_op jit(solution)/shard_map/all_to_all | solution.py:232
  252.6 6.4 %all-to-all-done.6 = bf16[16,16,128]{2,1,0:T(8,128)(2,1)S(1)} async-done(((bf16[16,16,128]{2,1,0:T(8,128)(2,1)}), bf16[16,16,128]{2,1,0:T(8,128)(2,1)S(1)}, u32[]{:S(2)}, u32[]{:S(2)}) %all-to-all-start.6) | async-done | bytes 65568 | tf_op jit(solution)/shard_map/all_to_all | solution.py:232
  259.0 1.0 broadcast_in_dim.30
  260.0 3.6 %all-to-all-start.9 = ((f32[16,50,256]{2,1,0:T(8,128)}), f32[16,50,256]{2,1,0:T(8,128)S(1)}, u32[]{:S(2)}, u32[]{:S(2)}) async-start(f32[16,50,256]{2,1,0:T(8,128)} %broadcast_in_dim.30), calls=%async_computation.9 | async-start | bytes 1835008 | tf_op jit(solution)/shard_map/all_to_all | solution.py:232
  263.6 0.7 last.1
  264.4 12.2 %all-to-all-done.9 = f32[16,50,256]{2,1,0:T(8,128)S(1)} async-done(((f32[16,50,256]{2,1,0:T(8,128)}), f32[16,50,256]{2,1,0:T(8,128)S(1)}, u32[]{:S(2)}, u32[]{:S(2)}) %all-to-all-start.9) | async-done | bytes 819232 | tf_op jit(solution)/shard_map/all_to_all | solution.py:232
  276.6 0.8 fusion.2
  277.3 0.8 pad_maximum_fusion
  (59 shorter events, 7.4 us)
Async XLA Ops:
  0.6 0.9 copy-start.16
  0.6 10.8 %copy-start = (bf16[1024,256]{1,0:T(8,128)(2,1)S(1)}, bf16[1024,256]{1,0:T(8,128)(2,1)}, u32[]{:S(2)}) copy-start(bf16[1024,256]{1,0:T(8,128)(2,1)} %features_ref.1) | copy-start | bytes 1572868
  2.3 14.8 %all-to-all-start.1 = ((s32[16,24,128]{2,1,0:T(8,128)}), s32[16,24,128]{2,1,0:T(8,128)S(1)}, u32[]{:S(2)}, u32[]{:S(2)}) async-start(s32[16,24,128]{2,1,0:T(8,128)} %broadcast_in_dim.13), calls=%async_computation.1 | async-start | bytes 393216 | tf_op jit(solution)/shard_map/all_to_all | solution.py:232
  9.8 0.7 copy-start.19
  10.6 0.7 copy-start.15
  17.0 53.4 %all-to-all-start = ((bf16[64,2,128]{2,1,0:T(2,128)(2,1)}), bf16[64,2,128]{2,1,0:T(2,128)(2,1)S(1)}, u32[]{:S(2)}, u32[]{:S(2)}) async-start(bf16[64,2,128]{2,1,0:T(2,128)(2,1)} %reshape.99), calls=%async_computation | async-start | bytes 65536 | tf_op jit(solution)/shard_map/all_to_all | solution.py:232
  78.7 5.8 %copy-start.17 = (s32[1024]{0:T(1024)S(1)}, s32[1024]{0:T(1024)}, u32[]{:S(2)}) copy-start(s32[1024]{0:T(1024)} %param.12) | copy-start | bytes 12292
  78.7 27.8 %all-to-all-start.2 = ((bf16[64,2,128]{2,1,0:T(2,128)(2,1)}), bf16[64,2,128]{2,1,0:T(2,128)(2,1)S(1)}, u32[]{:S(2)}, u32[]{:S(2)}) async-start(bf16[64,2,128]{2,1,0:T(2,128)(2,1)} %reshape.101), calls=%async_computation.2 | async-start | bytes 65536 | tf_op jit(solution)/shard_map/all_to_all | solution.py:232
  108.2 3.7 %copy-start.1 = (bf16[1024,256]{1,0:T(8,128)(2,1)S(1)}, bf16[1024,256]{1,0:T(8,128)(2,1)}, u32[]{:S(2)}) copy-start(bf16[1024,256]{1,0:T(8,128)(2,1)} %refs_2_.1) | copy-start | bytes 1572868
  108.2 3.7 %copy-start.10 = (bf16[256,256]{1,0:T(8,128)(2,1)S(1)}, bf16[256,256]{1,0:T(8,128)(2,1)}, u32[]{:S(2)}) copy-start(bf16[256,256]{1,0:T(8,128)(2,1)} %refs_6_.1) | copy-start | bytes 393220
  108.2 13.3 %all-to-all-start.3 = ((bf16[16,16,1024]{2,1,0:T(8,128)(2,1)}), bf16[16,16,1024]{2,1,0:T(8,128)(2,1)S(1)}, u32[]{:S(2)}, u32[]{:S(2)}) async-start(bf16[16,16,1024]{2,1,0:T(8,128)(2,1)} %get-tuple-element.25), calls=%async_computation.3 | async-start | bytes 1048576 | tf_op jit(solution)/shard_map/all_to_all | solution.py:232
  111.9 1.0 copy-start.3
  112.0 0.9 copy-start.18
  121.6 1.0 copy-start.4
  122.5 13.2 %copy-start.2 = (bf16[1024,256]{1,0:T(8,128)(2,1)S(1)}, bf16[1024,256]{1,0:T(8,128)(2,1)}, u32[]{:S(2)}) copy-start(bf16[1024,256]{1,0:T(8,128)(2,1)} %refs_2_.1) | copy-start | bytes 1572868
  124.0 0.8 copy-start.6
  124.7 0.8 copy-start.8
  125.5 0.6 copy-start.11
  126.1 0.6 copy-start.13
  128.8 28.9 %all-to-all-start.4 = ((bf16[64,2,128]{2,1,0:T(2,128)(2,1)}), bf16[64,2,128]{2,1,0:T(2,128)(2,1)S(1)}, u32[]{:S(2)}, u32[]{:S(2)}) async-start(bf16[64,2,128]{2,1,0:T(2,128)(2,1)} %reshape.103), calls=%async_computation.4 | async-start | bytes 65536 | tf_op jit(solution)/shard_map/all_to_all | solution.py:232
  135.7 0.7 copy-start.14
  136.4 0.9 copy-start.5
  137.3 1.0 copy-start.7
  138.4 1.0 copy-start.9
  157.7 31.2 %all-to-all-start.7 = ((f32[64,1,256]{2,1,0:T(1,128)}), f32[64,1,256]{2,1,0:T(1,128)S(1)}, u32[]{:S(2)}, u32[]{:S(2)}) async-start(f32[64,1,256]{2,1,0:T(1,128)} %copy.40), calls=%async_computation.7 | async-start | bytes 131072 | tf_op jit(solution)/shard_map/all_to_all | solution.py:232
  163.8 0.8 copy-start.12
  188.9 28.6 %all-to-all-start.5 = ((bf16[64,2,128]{2,1,0:T(2,128)(2,1)}), bf16[64,2,128]{2,1,0:T(2,128)(2,1)S(1)}, u32[]{:S(2)}, u32[]{:S(2)}) async-start(bf16[64,2,128]{2,1,0:T(2,128)(2,1)} %reshape.105), calls=%async_computation.5 | async-start | bytes 65536 | tf_op jit(solution)/shard_map/all_to_all | solution.py:232
  218.2 30.8 %all-to-all-start.8 = ((f32[64,1,256]{2,1,0:T(1,128)}), f32[64,1,256]{2,1,0:T(1,128)S(1)}, u32[]{:S(2)}, u32[]{:S(2)}) async-start(f32[64,1,256]{2,1,0:T(1,128)} %broadcast_in_dim.14), calls=%async_computation.8 | async-start | bytes 131072 | tf_op jit(solution)/shard_map/all_to_all | solution.py:232
  249.0 10.0 %all-to-all-start.6 = ((bf16[16,16,128]{2,1,0:T(8,128)(2,1)}), bf16[16,16,128]{2,1,0:T(8,128)(2,1)S(1)}, u32[]{:S(2)}, u32[]{:S(2)}) async-start(bf16[16,16,128]{2,1,0:T(8,128)(2,1)} %back.1), calls=%async_computation.6 | async-start | bytes 131072 | tf_op jit(solution)/shard_map/all_to_all | solution.py:232
  260.0 16.6 %all-to-all-start.9 = ((f32[16,50,256]{2,1,0:T(8,128)}), f32[16,50,256]{2,1,0:T(8,128)S(1)}, u32[]{:S(2)}, u32[]{:S(2)}) async-start(f32[16,50,256]{2,1,0:T(8,128)} %broadcast_in_dim.30), calls=%async_computation.9 | async-start | bytes 1835008 | tf_op jit(solution)/shard_map/all_to_all | solution.py:232

commit v2 on v1

v2 whole, which is shorter than its diff:
```python
import math

import jax
import jax.numpy as jnp
from jax import lax
from jax.experimental import pallas as pl
from jax.experimental.pallas import tpu as pltpu
from jax.sharding import PartitionSpec as P

BF = jnp.bfloat16
F32 = jnp.float32
LANES = 128
PART = 8
GROUPS = 4


def matmul(a, b, ca=1, cb=0):
    return lax.dot_general(a, b, (((ca,), (cb,)), ((), ())), preferred_element_type=F32)


def hot(condition):
    return jnp.where(condition, 1.0, 0.0).astype(BF)


def row_choice(slots_row, first, count):
    width = slots_row.shape[1]
    rows = lax.broadcasted_iota(jnp.int32, (count, width), 0)
    return hot(rows == slots_row - first)


def peer_choice(n_peers, n_slots):
    peers = lax.broadcasted_iota(jnp.int32, (n_peers, 1), 0)
    slots = lax.broadcasted_iota(jnp.int32, (1, n_slots), 1)
    return hot(slots // (n_slots // n_peers) == peers)


def pick(table, slots_row):
    total = None
    for first in range(0, table.shape[1], LANES):
        choice = row_choice(slots_row, first, LANES)
        part = matmul(table[:, first : first + LANES], choice)
        total = part if total is None else total + part
    return total


def scatter(values, slots_row, count):
    parts = []
    for first in range(0, count, LANES):
        choice = row_choice(slots_row, first, LANES)
        parts.append(matmul(values, choice, 1, 1))
    return jnp.concatenate(parts, 1)


def cap_lane(shape, cap):
    return lax.rem(lax.broadcasted_iota(jnp.int32, shape, 1), cap)


def peer_rows(n_rows, per_peer, n_slots, cap):
    rows = lax.broadcasted_iota(jnp.int32, (n_rows, 1), 0)
    part = lax.rem(rows, per_peer)
    used = jnp.where(part < cap // PART, rows // per_peer * (cap // PART) + part, -1)
    slots = lax.broadcasted_iota(jnp.int32, (1, n_slots), 1) // PART
    return hot(slots == used)


def to_peers(columns, per_peer, cap):
    k, n_slots = columns.shape
    n_rows = n_slots // cap * per_peer
    lane = cap_lane(columns.shape, PART)
    spread_out = jnp.concatenate(
        [jnp.where(lane == c, columns, 0.0).astype(BF) for c in range(PART)], 0
    )
    return matmul(peer_rows(n_rows, per_peer, n_slots, cap), spread_out, 1, 1)


def from_peers(arrived, per_peer, cap):
    n_rows, width = arrived.shape
    k = width // PART
    n_slots = n_rows // per_peer * cap
    wide = matmul(arrived, peer_rows(n_rows, per_peer, n_slots, cap), 0, 0)
    lane = cap_lane((k, n_slots), PART)
    total = jnp.zeros((k, n_slots), F32)
    for c in range(PART):
        total = jnp.where(lane == c, wide[c * k : c * k + k], total)
    return total


def slots_of(send_rows, send_counts, v_count):
    n_peers, cap = send_rows.shape
    n_slots = n_peers * cap
    chosen = peer_choice(n_peers, n_slots)
    base = 32
    high = send_rows // base
    low = send_rows - high * base
    lane = cap_lane((cap, n_slots), cap)
    c = lax.broadcasted_iota(jnp.int32, (cap, n_slots), 0)
    both = matmul(high.astype(F32).astype(BF), chosen, 0, 0) * base + matmul(
        low.astype(F32).astype(BF), chosen, 0, 0
    )
    rows = jnp.sum(jnp.where(lane == c, both, 0.0), 0, keepdims=True)
    counts = jnp.broadcast_to(send_counts.astype(F32), (8, n_peers)).astype(BF)
    counts = matmul(counts, chosen)[:1]
    unused = cap_lane((1, n_slots), cap).astype(F32) >= counts
    return jnp.where(unused, float(v_count), rows).astype(jnp.int32)


def first_kernel(
    features_ref, send_rows_ref, send_counts_ref, replica_ref, table_ref, slots_ref, payload_ref
):
    k, v_count = table_ref.shape
    rows = lax.broadcasted_iota(jnp.int32, (k, features_ref.shape[1]), 0)
    columns = lax.broadcasted_iota(jnp.int32, (k, features_ref.shape[1]), 1)
    mine = hot(columns == rows + replica_ref[0] * k)
    table = matmul(mine, features_ref[...], 1, 1).astype(BF)
    table_ref[...] = table
    slots = slots_of(send_rows_ref[...], send_counts_ref[...], v_count)
    slots_ref[...] = slots
    cap = send_rows_ref.shape[1]
    payload_ref[...] = to_peers(pick(table, slots), cap // PART, cap).astype(BF)


def edges_kernel(
    cap, per_peer, transpose, arrived_ref, owned_ref, edges_ref, blocks_ref, payload_ref, own_ref,
    table, total,
):
    k, v_count = owned_ref.shape
    own_blocks = v_count // LANES
    all_blocks = table.shape[0]
    arrived = arrived_ref[...]
    mirrors = from_peers(arrived, per_peer, cap).astype(BF)
    owned = owned_ref[...]
    for b in range(own_blocks):
        table[b] = owned[:, b * LANES : b * LANES + LANES]
    for b in range(own_blocks, all_blocks):
        first = (b - own_blocks) * LANES
        table[b] = mirrors[:, first : first + LANES]
    total[...] = jnp.zeros_like(total)
    n_groups, group_rows, width = edges_ref.shape
    per_group = (group_rows - 8) // 2
    positions = lax.broadcasted_iota(jnp.int32, (LANES, width), 0)
    a, b = (1, 0) if transpose else (0, 1)

    together = math.gcd(n_groups, GROUPS)
    tiles = [(j, t) for j in range(together) for t in range(per_group)]

    def group(i, carry):
        g = i * together
        gathered = []
        for j, t in tiles:
            block = blocks_ref[g + j, 2 * t + a]
            slots = edges_ref[g + j, 2 * t + a : 2 * t + a + 1, :]
            gathered.append(matmul(table[block], hot(positions == slots)).astype(BF))
        placed = []
        for (j, t), values in zip(tiles, gathered):
            slots = edges_ref[g + j, 2 * t + b : 2 * t + b + 1, :]
            placed.append(matmul(values, hot(positions == slots), 1, 1))
        for (j, t), values in zip(tiles, placed):
            block = blocks_ref[g + j, 2 * t + b]
            total[block] = total[block] + values
        return carry

    lax.fori_loop(0, n_groups // together, group, 0)
    for b in range(own_blocks):
        own_ref[:, b * LANES : b * LANES + LANES] = total[b]
    back = jnp.concatenate([total[b] for b in range(own_blocks, all_blocks)], 1)
    outgoing = to_peers(back, per_peer, cap)
    if per_peer > cap // PART:
        parts = per_peer - cap // PART
        rows = lax.broadcasted_iota(jnp.int32, (8, arrived.shape[0]), 1)
        part = lax.broadcasted_iota(jnp.int32, (8, arrived.shape[0]), 0)
        chosen = hot(lax.rem(rows, per_peer) == part + cap // PART)
        sums = matmul(chosen, arrived)
        place = lax.rem(lax.broadcasted_iota(jnp.int32, outgoing.shape, 0), per_peer)
        for h in range(parts):
            outgoing = jnp.where(place == cap // PART + h, sums[h : h + 1], outgoing)
    payload_ref[...] = outgoing.astype(BF)


def aggregate_kernel(cap, arrived_ref, own_ref, slots_ref, degree_ref, aggregate_ref, copies_ref):
    k, v_count = own_ref.shape
    returned = from_peers(arrived_ref[...], cap // PART, cap).astype(BF)
    summed = own_ref[...] + scatter(returned, slots_ref[...], v_count)
    aggregate = (summed / degree_ref[...]).astype(BF)
    aggregate_ref[...] = aggregate
    for r in range(copies_ref.shape[0]):
        copies_ref[r] = aggregate


def dense_kernel(
    scale, cap, aggregate_ref, self_ref, gh_ref, w_in_ref, degree_ref, slots_ref, table_ref, mine_ref,
    cotangent_ref, replica_ref, hidden_out_ref, grad_pre_out_ref, spread_ref, payload_ref, hidden_ref,
    grad_pre_ref,
):
    k, v_count = spread_ref.shape
    channels = aggregate_ref.shape[0]
    w_neigh = w_in_ref[channels:, :]
    pre = self_ref[...] + matmul(w_neigh, aggregate_ref[...], 0, 0)
    sigmoid = 1.0 / (1.0 + jnp.exp(-pre))
    hidden_ref[...] = (pre * sigmoid).astype(BF)
    grad_pre = (gh_ref[...] * (sigmoid * (1.0 + pre * (1.0 - sigmoid)))).astype(BF)
    grad_pre_ref[...] = grad_pre
    per_block = LANES // (v_count * k // channels)
    block = pl.multiple_of((replica_ref[0] // per_block) * LANES, LANES)
    hidden_out_ref[...] = hidden_ref[:, pl.ds(block, LANES)]
    grad_pre_out_ref[...] = grad_pre_ref[:, pl.ds(block, LANES)]
    first = pl.multiple_of(channels + replica_ref[0] * k, k)
    spread = matmul(w_in_ref[pl.ds(first, k), :], grad_pre)
    spread = (spread / degree_ref[...]).astype(BF)
    spread_ref[...] = spread

    ones = jnp.ones((k, v_count), BF)
    left = jnp.concatenate([table_ref[...], mine_ref[...], ones], 0)
    grads_in = (matmul(left, grad_pre, 1, 1) * scale).astype(BF)
    first = pl.multiple_of(replica_ref[0] * k, k)
    left = jnp.concatenate([hidden_ref[pl.ds(first, k), :], ones], 0)
    grads_out = (matmul(left, cotangent_ref[...]) * scale).astype(BF)
    grads = jnp.concatenate([grads_in[: 2 * k], grads_out[:k], grads_in[2 * k :], grads_out[k:]], 0)

    parts = cap // PART
    halves = channels // LANES
    per_peer = parts + halves
    payload = to_peers(pick(spread, slots_ref[...]), per_peer, cap)
    n_rows = payload.shape[0]
    rows = lax.broadcasted_iota(jnp.int32, (n_rows, grads.shape[0]), 0)
    source = lax.broadcasted_iota(jnp.int32, (n_rows, grads.shape[0]), 1)
    peer = jnp.where(source == 4 * k, 3 * k + 1, jnp.where(source > 3 * k, -1, source))
    for h in range(halves):
        chosen = hot((rows // per_peer == peer) & (lax.rem(rows, per_peer) == parts + h))
        payload = payload + matmul(chosen, grads[:, h * LANES : h * LANES + LANES])
    payload_ref[...] = payload.astype(BF)


def rows_kernel(
    hidden_ref, grad_pre_ref, w_in_ref, w_out_ref, b_out_ref, replica_ref, output_ref, grad_self_ref,
    rows_ref,
):
    channels = hidden_ref.shape[0]
    share = output_ref.shape[0]
    replica = replica_ref[0]
    per_block = LANES // share
    half = pl.multiple_of(lax.rem(replica, per_block) * share, share)
    rows_ref[...] = matmul(hidden_ref[...], w_out_ref[...], 0, 0)
    output_ref[...] = (rows_ref[pl.ds(half, share), :] + b_out_ref[...]).astype(BF)
    rows_ref[...] = matmul(w_in_ref[:channels, :], grad_pre_ref[...]).T
    grad_self_ref[...] = rows_ref[pl.ds(half, share), :]


def back_kernel(cap, per_peer, arrived_ref, own_ref, slots_ref, copies_ref):
    k, v_count = own_ref.shape
    n_dp = copies_ref.shape[0]
    share = v_count // n_dp
    arrived = arrived_ref[...]
    returned = from_peers(arrived, per_peer, cap).astype(BF)
    summed = (own_ref[...] + scatter(returned, slots_ref[...], v_count)).astype(BF)
    n_rows = copies_ref.shape[1] - k
    parts = cap // PART
    halves = per_peer - parts
    to = lax.broadcasted_iota(jnp.int32, (n_rows, arrived.shape[0]), 0)
    source = lax.broadcasted_iota(jnp.int32, (n_rows, arrived.shape[0]), 1)
    peer, half = source // per_peer, lax.rem(source, per_peer) - parts
    place = jnp.where(peer < 3 * k, half * (3 * k) + peer, halves * 3 * k + (peer - 3 * k) * halves + half)
    chosen = hot((place == to) & (half >= 0))
    grads = matmul(chosen, arrived).astype(BF)
    for r in range(n_dp):
        first = r * share // LANES * LANES
        copies_ref[r, :k] = summed[:, first : first + LANES]
        copies_ref[r, k:] = grads


def last_kernel(
    arrived_ref, grad_self_ref, replica_ref, grad_features_ref, grad_w_in_ref, grad_b_in_ref,
    grad_w_out_ref, grad_b_out_ref, rows_ref,
):
    share, channels = grad_features_ref.shape
    n_dp = arrived_ref.shape[0]
    k = channels // n_dp
    half = pl.multiple_of(lax.rem(replica_ref[0], LANES // share) * share, share)
    columns = jnp.concatenate([arrived_ref[r, :k] for r in range(n_dp)], 0)
    rows_ref[...] = columns.astype(F32).T
    grad_features_ref[...] = (rows_ref[pl.ds(half, share), :] + grad_self_ref[...]).astype(BF)
    halves = channels // LANES
    for h in range(halves):
        lanes = slice(h * LANES, h * LANES + LANES)
        first = k + h * 3 * k
        for r in range(n_dp):
            rows = slice(r * k, r * k + k)
            grad_w_in_ref[rows, lanes] = arrived_ref[r, first : first + k].astype(F32)
            second = slice(channels + r * k, channels + r * k + k)
            grad_w_in_ref[second, lanes] = arrived_ref[r, first + k : first + 2 * k].astype(F32)
            grad_w_out_ref[rows, lanes] = arrived_ref[r, first + 2 * k : first + 3 * k].astype(F32)
        biases = arrived_ref[0, k + halves * 3 * k :].astype(F32)
        grad_b_in_ref[:, lanes] = biases[h : h + 1]
        grad_b_out_ref[:, lanes] = biases[halves + h : halves + h + 1]


def call(kernel, outs, args, smem=(), scratch=(), flops=0, name=None):
    in_specs = [
        pl.BlockSpec(memory_space=pltpu.SMEM if i in smem else pltpu.VMEM) for i in range(len(args))
    ]
    shapes = [jax.ShapeDtypeStruct(s, d) for s, d in outs]
    size = sum(math.prod(s) * jnp.dtype(d).itemsize for s, d in outs)
    size += sum(x.size * x.dtype.itemsize for x in args)
    return pl.pallas_call(
        kernel,
        out_shape=shapes,
        in_specs=in_specs,
        out_specs=[pl.BlockSpec(memory_space=pltpu.VMEM) for _ in outs],
        scratch_shapes=list(scratch),
        compiler_params=pltpu.CompilerParams(vmem_limit_bytes=16 * 1024 * 1024),
        cost_estimate=pl.CostEstimate(flops=flops, bytes_accessed=size, transcendentals=0),
        name=name,
    )(*args)


def swap(values, axis):
    return lax.all_to_all(values, axis, split_axis=0, concat_axis=0, tiled=True)


def on_device(
    features,
    degree,
    send_rows,
    send_counts,
    edge_slots,
    tile_blocks,
    w_in,
    b_in,
    w_out,
    b_out,
    cotangent,
):
    n_dp = lax.axis_size("dp")
    n_dom = lax.axis_size("dom")
    replica = lax.axis_index("dp").astype(jnp.int32).reshape(1)
    v_count, channels = features.shape
    cap = send_rows.shape[2]
    k = channels // n_dp
    share = v_count // n_dp
    n_slots = n_dom * cap
    n_tiles, _, tile_rows = edge_slots.shape[2:]
    blocks_count = (v_count + n_slots) // LANES
    scale = 1.0 / math.sqrt(v_count * n_dom)

    degree_row = degree.astype(F32).reshape(1, v_count)
    parts = cap // PART
    more = parts + channels // LANES

    edges = edge_slots[0, 0].reshape(2 * n_tiles, tile_rows)
    block_row = tile_blocks[0, 0].reshape(1, 2 * n_tiles)
    edges = jnp.concatenate([edges, jnp.pad(block_row, ((0, 7), (0, tile_rows - 2 * n_tiles)))], 0)
    edges = swap(jnp.broadcast_to(edges[None], (n_dp, *edges.shape)), "dp")
    blocks = edges[:, 2 * n_tiles, : 2 * n_tiles]

    table, slots_row, payload = call(
        first_kernel,
        [((k, v_count), BF), ((1, n_slots), jnp.int32), ((n_dom * parts, LANES), BF)],
        [features, send_rows[0], send_counts, replica],
        smem=(3,),
        name="first",
    )
    arrived = swap(payload, "dom")

    w_self = w_in[:channels]
    self_t = jnp.einsum("ah,va->hv", w_self, features, preferred_element_type=F32) + b_in[:, None]
    gh_t = jnp.einsum("ho,vo->hv", w_out, cotangent, preferred_element_type=F32)

    def edge_pass(arrived, owned, per_peer, transpose):
        return call(
            lambda *refs: edges_kernel(cap, per_peer, transpose, *refs),
            [((n_dom * per_peer, LANES), BF), ((k, v_count), F32)],
            [arrived, owned, edges, blocks],
            smem=(3,),
            scratch=[
                pltpu.VMEM((blocks_count, k, LANES), BF),
                pltpu.VMEM((blocks_count, k, LANES), F32),
            ],
            name="edges_back" if transpose else "edges",
        )

    payload, own = edge_pass(arrived, table, parts, False)
    arrived = swap(payload, "dom")
    aggregate, copies = call(
        lambda *refs: aggregate_kernel(cap, *refs),
        [((k, v_count), BF), ((n_dp, k, v_count), BF)],
        [arrived, own, slots_row, degree_row],
        name="aggregate",
    )
    aggregate_all = swap(copies, "dp").reshape(channels, v_count)

    hidden, grad_pre, spread, payload = call(
        lambda *refs: dense_kernel(scale, cap, *refs),
        [((channels, LANES), BF), ((channels, LANES), BF), ((k, v_count), BF), ((n_dom * more, LANES), BF)],
        [aggregate_all, self_t, gh_t, w_in, degree_row, slots_row, table, aggregate, cotangent, replica],
        smem=(9,),
        scratch=[pltpu.VMEM((channels, v_count), BF), pltpu.VMEM((channels, v_count), BF)],
        name="dense",
    )
    arrived = swap(payload, "dom")
    output, grad_self = call(
        rows_kernel,
        [((share, channels), BF), ((share, channels), F32)],
        [hidden, grad_pre, w_in, w_out, b_out.reshape(1, -1), replica],
        smem=(5,),
        scratch=[pltpu.VMEM((LANES, channels), F32)],
        name="rows",
    )
    payload, own = edge_pass(arrived, spread, more, True)
    arrived = swap(payload, "dom")
    grad_rows = 2 * 3 * k + k
    (copies,) = call(
        lambda *refs: back_kernel(cap, more, *refs),
        [((n_dp, k + grad_rows, LANES), BF)],
        [arrived, own, slots_row],
        name="back",
    )
    arrived = swap(copies, "dp")
    grad_features, grad_w_in, grad_b_in, grad_w_out, grad_b_out = call(
        last_kernel,
        [
            ((share, channels), BF),
            ((2 * channels, channels), F32),
            ((1, channels), F32),
            ((channels, channels), F32),
            ((1, channels), F32),
        ],
        [arrived, grad_self, replica],
        smem=(2,),
        scratch=[pltpu.VMEM((LANES, channels), F32)],
        name="last",
    )
    return (output, grad_features, grad_w_in, grad_b_in[0], grad_w_out, grad_b_out[0])


def solution(mesh):
    in_specs = (
        P("dom", None),
        P("dom"),
        P("dom", None, None),
        P("dom", None),
        P("dom", "dp", None, None, None),
        P("dom", "dp", None, None),
        P(),
        P(),
        P(),
        P(),
        P("dom", None),
    )
    out_specs = (P(("dom", "dp"), None), P(("dom", "dp"), None), P(), P(), P(), P())
    return jax.shard_map(
        on_device, mesh=mesh, in_specs=in_specs, out_specs=out_specs, check_vma=False
    )
```

time: 282 us -> 208 us (0.74)
  waiting for transfers between devices: 153 us -> 66 us
  blocking collectives: 0 us -> 62 us
  starting transfers between devices: 80.1 us -> 52.4 us
  local copies, waits for them, and re-layouts: 18.7 us -> 4.58 us
  other arithmetic: 4.4 us -> 0.01 us
    all_to_all x10 -> x5, waiting for transfers between devices: 153 us -> 66 us  [swap(): return lax.all_to_all(values, axis, split_axis=0, concat_axis=0, tiled=True)]
    all_to_all x0 -> x2, blocking collectives: none -> 62 us  [swap(): return lax.all_to_all(values, axis, split_axis=0, concat_axis=0, tiled=True)]
    all_to_all x10 -> x5, starting transfers between devices: 80.1 us -> 52.4 us  [swap(): return lax.all_to_all(values, axis, split_axis=0, concat_axis=0, tiled=True)]
    unnamed x55 -> x24, local copies, waits for them, and re-layouts: 13.6 us -> 3.79 us
    all_to_all x4 -> x0, other arithmetic: 3.39 us -> none  [swap(): return lax.all_to_all(values, axis, split_axis=0, concat_axis=0, tiled=True)]
  transfers between devices with their start and end apart: 10 -> 5, of which waited for: 10 -> 5; matrix products, arithmetic and copies ran while one was open for 2% -> 0% of each run, Pallas kernels for 4% -> 1%
where the time goes in v2:
time: 208 us; the launch traced here: 207 us
  waiting for transfers between devices  66 us (32%)
  blocking collectives  62 us (30%)
  starting transfers between devices  52.4 us (25%)
  Pallas kernels  20.3 us (10%)
  local copies, waits for them, and re-layouts  4.58 us (2%)
    all_to_all x5, waiting for transfers between devices, swap(): return lax.all_to_all(values, axis, split_axis=0, concat_axis=0, tiled=True)  66 us
    all_to_all x2, blocking collectives, swap(): return lax.all_to_all(values, axis, split_axis=0, concat_axis=0, tiled=True)  62 us
    all_to_all x5, starting transfers between devices, swap(): return lax.all_to_all(values, axis, split_axis=0, concat_axis=0, tiled=True)  52.4 us
    pallas_call x8, Pallas kernels, call(): pl.pallas_call(kernel, out_shape=shapes, in_specs=in_specs, out_specs=[pl...  20.3 us
  transfers between devices with their start and end apart: 5, of which 5 were waited for; matrix products, arithmetic and copies ran while one was open for 0% of the time, Pallas kernels for 1%

profile of v2, /device:TPU:1, one launch (start us, length us, event | category | flops | bytes accessed | tf_op | source)
XLA Modules:
  0.0 206.8 jit_solution(9642532477739071688)
XLA Ops:
  0.6 0.0 copy-start.8
  0.6 0.0 copy-start
  0.7 0.8 copy.26
  1.5 0.1 reshape_squeeze.7
  1.5 0.0 copy-done.8
  1.6 0.7 broadcast_in_dim.2
  2.3 0.0 copy-start.7
  2.3 7.7 %all-to-all-start.1 = ((s32[16,24,128]{2,1,0:T(8,128)}), s32[16,24,128]{2,1,0:T(8,128)S(1)}, u32[]{:S(2)}, u32[]{:S(2)}) async-start(s32[16,24,128]{2,1,0:T(8,128)} %broadcast_in_dim.2), calls=%async_computation.1 | async-start | bytes 393216 | tf_op jit(solution)/shard_map/all_to_all | solution.py:316
  10.0 0.0 copy-done.7
  10.0 0.1 copy.25
  10.1 0.0 copy-start.6
  10.1 0.0 copy-done
  10.1 0.6 copy-done.6
  10.7 1.6 first.1
  12.3 4.8 %all-to-all-done.1.refs_2_ = s32[16,24,128]{2,1,0:T(8,128)S(1)} async-done(((s32[16,24,128]{2,1,0:T(8,128)}), s32[16,24,128]{2,1,0:T(8,128)S(1)}, u32[]{:S(2)}, u32[]{:S(2)}) %all-to-all-start.1) | async-done | bytes 196640 | tf_op jit(solution)/shard_map/all_to_all | solution.py:316
  17.2 31.0 %all-to-all-start = ((bf16[64,2,128]{2,1,0:T(2,128)(2,1)}), bf16[64,2,128]{2,1,0:T(2,128)(2,1)S(1)}, u32[]{:S(2)}, u32[]{:S(2)}) async-start(bf16[64,2,128]{2,1,0:T(2,128)(2,1)} %bitcast.2), calls=%async_computation | async-start | bytes 65536 | tf_op jit(solution)/shard_map/all_to_all | solution.py:316
  48.2 22.3 %all-to-all-done = bf16[64,2,128]{2,1,0:T(2,128)(2,1)S(1)} async-done(((bf16[64,2,128]{2,1,0:T(2,128)(2,1)}), bf16[64,2,128]{2,1,0:T(2,128)(2,1)S(1)}, u32[]{:S(2)}, u32[]{:S(2)}) %all-to-all-start) | async-done | bytes 32800 | tf_op jit(solution)/shard_map/all_to_all | solution.py:316
  70.5 5.5 %edges.1 = (bf16[128,128]{1,0:T(8,128)(2,1)}, f32[16,1024]{1,0:T(8,128)S(1)}) custom-call(bf16[128,128]{1,0:T(8,128)(2,1)S(1)} %bitcast.27, bf16[16,1024]{1,0:T(8,128)(2,1)S(1)} %get-tuple-element.27.refs_1_.refs_6_, s32[16,24,128]{2,1,0:T(8,128)S(1)} %all-to-all-done.1.refs_2_, s32[16,16]{1,0:T(8,128)S(1)} %bitcast.29), custom_call_target="tpu_custom_call" | custom-call | bytes 361472 | tf_op jit(solution)/shard_map/edges/pallas_call | solution.py:303
  76.1 0.0 copy-start.9
  76.1 5.8 %all-to-all-start.2 = ((bf16[64,2,128]{2,1,0:T(2,128)(2,1)}), bf16[64,2,128]{2,1,0:T(2,128)(2,1)S(1)}, u32[]{:S(2)}, u32[]{:S(2)}) async-start(bf16[64,2,128]{2,1,0:T(2,128)(2,1)} %bitcast.6), calls=%async_computation.2 | async-start | bytes 65536 | tf_op jit(solution)/shard_map/all_to_all | solution.py:316
  81.8 0.0 copy-done.9
  81.9 22.0 %all-to-all-done.2 = bf16[64,2,128]{2,1,0:T(2,128)(2,1)S(1)} async-done(((bf16[64,2,128]{2,1,0:T(2,128)(2,1)}), bf16[64,2,128]{2,1,0:T(2,128)(2,1)S(1)}, u32[]{:S(2)}, u32[]{:S(2)}) %all-to-all-start.2) | async-done | bytes 32800 | tf_op jit(solution)/shard_map/all_to_all | solution.py:316
  103.8 1.7 aggregate.1
  105.5 0.0 copy-start.1
  105.5 0.0 copy-start.4
  105.5 4.4 %all-to-all-start.3 = ((bf16[16,16,1024]{2,1,0:T(8,128)(2,1)}), bf16[16,16,1024]{2,1,0:T(8,128)(2,1)}, u32[]{:S(2)}, u32[]{:S(2)}) async-start(bf16[16,16,1024]{2,1,0:T(8,128)(2,1)} %get-tuple-element.31), calls=%async_computation.3 | async-start | bytes 1048576 | tf_op jit(solution)/shard_map/all_to_all | solution.py:316
  109.9 0.0 copy-done.1
  109.9 0.0 copy-done.4
  109.9 0.0 copy-start.2
  109.9 0.0 copy-start.10
  109.9 0.3 fusion.1.refs_2_
  110.3 0.6 copy-done.2
  110.9 0.0 copy-done.10
  110.9 0.4 convolution_add_fusion.refs_1_
  111.2 8.3 %all-to-all-done.3 = bf16[16,16,1024]{2,1,0:T(8,128)(2,1)} async-done(((bf16[16,16,1024]{2,1,0:T(8,128)(2,1)}), bf16[16,16,1024]{2,1,0:T(8,128)(2,1)}, u32[]{:S(2)}, u32[]{:S(2)}) %all-to-all-start.3) | async-done | bytes 524320 | tf_op jit(solution)/shard_map/all_to_all | solution.py:316
  119.6 0.0 copy-start.3
  119.6 0.9 copy-done.3
  120.5 2.9 %dense.1 = (bf16[256,128]{1,0:T(8,128)(2,1)S(1)}, bf16[256,128]{1,0:T(8,128)(2,1)S(1)}, bf16[16,1024]{1,0:T(8,128)(2,1)S(1)}, bf16[256,128]{1,0:T(8,128)(2,1)S(1)}) custom-call(bf16[256,1024]{1,0:T(8,128)(2,1)} %bitcast.9.refs_0_, f32[256,1024]{1,0:T(8,128)S(1)} %convolution_add_fusion.refs_1_, f32[256,1024]{1,0:T(8,128)S(1)} %fusion.1.refs_2_, ...), custom_call_target="tpu_custom_call" | custom-call | bytes 3710980 | tf_op jit(solution)/shard_map/dense/pallas_call | solution.py:303
  123.4 31.7 %all_to_all.59 = bf16[64,4,128]{2,1,0:T(4,128)(2,1)S(1)} all-to-all(bf16[64,4,128]{2,1,0:T(4,128)(2,1)S(1)} %bitcast.31), channel_id=1, replica_groups=mesh['dom'=64,'dp'=16] {'dom'}, dimensions={0} | all-to-all | bytes 131072 | tf_op jit(solution)/shard_map/all_to_all | solution.py:316
  155.1 5.0 %edges_back.1 = (bf16[256,128]{1,0:T(8,128)(2,1)S(1)}, f32[16,1024]{1,0:T(8,128)S(1)}) custom-call(bf16[256,128]{1,0:T(8,128)(2,1)S(1)} %bitcast.24, bf16[16,1024]{1,0:T(8,128)(2,1)S(1)} %get-tuple-element.37.refs_1_, s32[16,24,128]{2,1,0:T(8,128)S(1)} %all-to-all-done.1.refs_2_, s32[16,16]{1,0:T(8,128)S(1)} %bitcast.30), custom_call_target="tpu_custom_call" | custom-call | bytes 427008 | tf_op jit(solution)/shard_map/edges_back/pallas_call | solution.py:303
  160.1 30.4 %all_to_all.60 = bf16[64,4,128]{2,1,0:T(4,128)(2,1)S(1)} all-to-all(bf16[64,4,128]{2,1,0:T(4,128)(2,1)S(1)} %bitcast.32), channel_id=1, replica_groups=mesh['dom'=64,'dp'=16] {'dom'}, dimensions={0} | all-to-all | bytes 131072 | tf_op jit(solution)/shard_map/all_to_all | solution.py:316
  190.5 1.7 back.1
  192.2 3.6 %all-to-all-start.6 = ((bf16[16,128,128]{2,1,0:T(8,128)(2,1)}), bf16[16,128,128]{2,1,0:T(8,128)(2,1)S(1)}, u32[]{:S(2)}, u32[]{:S(2)}) async-start(bf16[16,128,128]{2,1,0:T(8,128)(2,1)} %back.1), calls=%async_computation.6 | async-start | bytes 1048576 | tf_op jit(solution)/shard_map/all_to_all | solution.py:316
  195.8 0.0 copy-start.5
  195.8 0.7 copy-done.5
  196.5 0.9 rows.1
  197.3 8.6 %all-to-all-done.6.arrived_ref = bf16[16,128,128]{2,1,0:T(8,128)(2,1)S(1)} async-done(((bf16[16,128,128]{2,1,0:T(8,128)(2,1)}), bf16[16,128,128]{2,1,0:T(8,128)(2,1)S(1)}, u32[]{:S(2)}, u32[]{:S(2)}) %all-to-all-start.6) | async-done | bytes 524320 | tf_op jit(solution)/shard_map/all_to_all | solution.py:316
  205.9 0.9 last.1
  (3 shorter events, 0.0 us)
Async XLA Ops:
  0.6 0.9 copy-start.8
  0.6 9.4 %copy-start = (bf16[1024,256]{1,0:T(8,128)(2,1)S(1)}, bf16[1024,256]{1,0:T(8,128)(2,1)}, u32[]{:S(2)}) copy-start(bf16[1024,256]{1,0:T(8,128)(2,1)} %features_ref.1) | copy-start | bytes 1572868
  2.3 7.7 %copy-start.7 = (s32[1,64,16]{1,2,0:T(8,128)S(1)}, s32[1,64,16]{1,2,0:T(8,128)}, u32[]{:S(2)}) copy-start(s32[1,64,16]{1,2,0:T(8,128)} %param.13) | copy-start | bytes 12292
  2.3 14.9 %all-to-all-start.1 = ((s32[16,24,128]{2,1,0:T(8,128)}), s32[16,24,128]{2,1,0:T(8,128)S(1)}, u32[]{:S(2)}, u32[]{:S(2)}) async-start(s32[16,24,128]{2,1,0:T(8,128)} %broadcast_in_dim.2), calls=%async_computation.1 | async-start | bytes 393216 | tf_op jit(solution)/shard_map/all_to_all | solution.py:316
  10.1 0.7 copy-start.6
  17.2 53.4 %all-to-all-start = ((bf16[64,2,128]{2,1,0:T(2,128)(2,1)}), bf16[64,2,128]{2,1,0:T(2,128)(2,1)S(1)}, u32[]{:S(2)}, u32[]{:S(2)}) async-start(bf16[64,2,128]{2,1,0:T(2,128)(2,1)} %bitcast.2), calls=%async_computation | async-start | bytes 65536 | tf_op jit(solution)/shard_map/all_to_all | solution.py:316
  76.1 5.8 %copy-start.9 = (s32[1024]{0:T(1024)S(1)}, s32[1024]{0:T(1024)}, u32[]{:S(2)}) copy-start(s32[1024]{0:T(1024)} %param.12) | copy-start | bytes 12292
  76.1 27.8 %all-to-all-start.2 = ((bf16[64,2,128]{2,1,0:T(2,128)(2,1)}), bf16[64,2,128]{2,1,0:T(2,128)(2,1)S(1)}, u32[]{:S(2)}, u32[]{:S(2)}) async-start(bf16[64,2,128]{2,1,0:T(2,128)(2,1)} %bitcast.6), calls=%async_computation.2 | async-start | bytes 65536 | tf_op jit(solution)/shard_map/all_to_all | solution.py:316
  105.5 4.4 %copy-start.1 = (bf16[1024,256]{1,0:T(8,128)(2,1)S(1)}, bf16[1024,256]{1,0:T(8,128)(2,1)}, u32[]{:S(2)}) copy-start(bf16[1024,256]{1,0:T(8,128)(2,1)} %refs_8_.1) | copy-start | bytes 1572868
  105.5 4.4 %copy-start.4 = (bf16[256,256]{1,0:T(8,128)(2,1)S(1)}, bf16[256,256]{1,0:T(8,128)(2,1)}, u32[]{:S(2)}) copy-start(bf16[256,256]{1,0:T(8,128)(2,1)} %w_out_ref.1) | copy-start | bytes 393220
  105.5 14.0 %all-to-all-start.3 = ((bf16[16,16,1024]{2,1,0:T(8,128)(2,1)}), bf16[16,16,1024]{2,1,0:T(8,128)(2,1)}, u32[]{:S(2)}, u32[]{:S(2)}) async-start(bf16[16,16,1024]{2,1,0:T(8,128)(2,1)} %get-tuple-element.31), calls=%async_computation.3 | async-start | bytes 1048576 | tf_op jit(solution)/shard_map/all_to_all | solution.py:316
  109.9 1.0 copy-start.2
  109.9 0.9 copy-start.10
  119.6 1.0 copy-start.3
  192.2 13.7 %all-to-all-start.6 = ((bf16[16,128,128]{2,1,0:T(8,128)(2,1)}), bf16[16,128,128]{2,1,0:T(8,128)(2,1)S(1)}, u32[]{:S(2)}, u32[]{:S(2)}) async-start(bf16[16,128,128]{2,1,0:T(8,128)(2,1)} %back.1), calls=%async_computation.6 | async-start | bytes 1048576 | tf_op jit(solution)/shard_map/all_to_all | solution.py:316
  195.8 0.7 copy-start.5

commit v3 on v2

--- a/solution.py
+++ b/solution.py
@@ -11,7 +11,7 @@
 F32 = jnp.float32
 LANES = 128
 PART = 8
-GROUPS = 4
+GROUPS = 8
 
 
 def matmul(a, b, ca=1, cb=0):
@@ -136,27 +136,39 @@
         table[b] = mirrors[:, first : first + LANES]
     total[...] = jnp.zeros_like(total)
     n_groups, group_rows, width = edges_ref.shape
-    per_group = (group_rows - 8) // 2
-    positions = lax.broadcasted_iota(jnp.int32, (LANES, width), 0)
+    per_group = group_rows // 3
+    positions = lax.broadcasted_iota(jnp.int32, (LANES, 2 * width), 0)
     a, b = (1, 0) if transpose else (0, 1)
-
     together = math.gcd(n_groups, GROUPS)
     tiles = [(j, t) for j in range(together) for t in range(per_group)]
+    pairs = list(zip(tiles[::2], tiles[1::2]))
+
+    def halves(product):
+        return product[:k, :LANES], product[k:, LANES:]
 
     def group(i, carry):
         g = i * together
+
+        def slots(tile, side):
+            row = 2 * tile[1] + side
+            return edges_ref[g + tile[0], row : row + 1, :]
+
+        def block(tile, side):
+            return blocks_ref[g + tile[0], 2 * tile[1] + side]
+
         gathered = []
-        for j, t in tiles:
-            block = blocks_ref[g + j, 2 * t + a]
-            slots = edges_ref[g + j, 2 * t + a : 2 * t + a + 1, :]
-            gathered.append(matmul(table[block], hot(positions == slots)).astype(BF))
+        for one, two in pairs:
+            left = jnp.concatenate([table[block(one, a)], table[block(two, a)]], 0)
+            right = hot(positions == jnp.concatenate([slots(one, a), slots(two, a)], 1))
+            gathered.append(jnp.concatenate(halves(matmul(left, right)), 0).astype(BF))
         placed = []
-        for (j, t), values in zip(tiles, gathered):
-            slots = edges_ref[g + j, 2 * t + b : 2 * t + b + 1, :]
-            placed.append(matmul(values, hot(positions == slots), 1, 1))
-        for (j, t), values in zip(tiles, placed):
-            block = blocks_ref[g + j, 2 * t + b]
-            total[block] = total[block] + values
+        for (one, two), values in zip(pairs, gathered):
+            rows = positions[:, :width]
+            right = jnp.concatenate([hot(rows == slots(one, b)), hot(rows == slots(two, b))], 0)
+            placed.extend(halves(matmul(values, right, 1, 1)))
+        for tile, values in zip(tiles, placed):
+            at = block(tile, b)
+            total[at] = total[at] + values
         return carry
 
     lax.fori_loop(0, n_groups // together, group, 0)
@@ -187,14 +199,13 @@
 
 
 def dense_kernel(
-    scale, cap, aggregate_ref, self_ref, gh_ref, w_in_ref, degree_ref, slots_ref, table_ref, mine_ref,
+    scale, cap, aggregate_ref, self_ref, gh_ref, w_neigh_ref, degree_ref, slots_ref, table_ref, mine_ref,
     cotangent_ref, replica_ref, hidden_out_ref, grad_pre_out_ref, spread_ref, payload_ref, hidden_ref,
     grad_pre_ref,
 ):
     k, v_count = spread_ref.shape
     channels = aggregate_ref.shape[0]
-    w_neigh = w_in_ref[channels:, :]
-    pre = self_ref[...] + matmul(w_neigh, aggregate_ref[...], 0, 0)
+    pre = self_ref[...] + matmul(w_neigh_ref[...], aggregate_ref[...], 0, 0)
     sigmoid = 1.0 / (1.0 + jnp.exp(-pre))
     hidden_ref[...] = (pre * sigmoid).astype(BF)
     grad_pre = (gh_ref[...] * (sigmoid * (1.0 + pre * (1.0 - sigmoid)))).astype(BF)
@@ -203,15 +214,14 @@
     block = pl.multiple_of((replica_ref[0] // per_block) * LANES, LANES)
     hidden_out_ref[...] = hidden_ref[:, pl.ds(block, LANES)]
     grad_pre_out_ref[...] = grad_pre_ref[:, pl.ds(block, LANES)]
-    first = pl.multiple_of(channels + replica_ref[0] * k, k)
-    spread = matmul(w_in_ref[pl.ds(first, k), :], grad_pre)
+    first = pl.multiple_of(replica_ref[0] * k, k)
+    spread = matmul(w_neigh_ref[pl.ds(first, k), :], grad_pre)
     spread = (spread / degree_ref[...]).astype(BF)
     spread_ref[...] = spread
 
     ones = jnp.ones((k, v_count), BF)
     left = jnp.concatenate([table_ref[...], mine_ref[...], ones], 0)
     grads_in = (matmul(left, grad_pre, 1, 1) * scale).astype(BF)
-    first = pl.multiple_of(replica_ref[0] * k, k)
     left = jnp.concatenate([hidden_ref[pl.ds(first, k), :], ones], 0)
     grads_out = (matmul(left, cotangent_ref[...]) * scale).astype(BF)
     grads = jnp.concatenate([grads_in[: 2 * k], grads_out[:k], grads_in[2 * k :], grads_out[k:]], 0)
@@ -231,7 +241,7 @@
 
 
 def rows_kernel(
-    hidden_ref, grad_pre_ref, w_in_ref, w_out_ref, b_out_ref, replica_ref, output_ref, grad_self_ref,
+    hidden_ref, grad_pre_ref, w_self_ref, w_out_ref, b_out_ref, replica_ref, output_ref, grad_self_ref,
     rows_ref,
 ):
     channels = hidden_ref.shape[0]
@@ -241,7 +251,7 @@
     half = pl.multiple_of(lax.rem(replica, per_block) * share, share)
     rows_ref[...] = matmul(hidden_ref[...], w_out_ref[...], 0, 0)
     output_ref[...] = (rows_ref[pl.ds(half, share), :] + b_out_ref[...]).astype(BF)
-    rows_ref[...] = matmul(w_in_ref[:channels, :], grad_pre_ref[...]).T
+    rows_ref[...] = matmul(w_self_ref[...], grad_pre_ref[...]).T
     grad_self_ref[...] = rows_ref[pl.ds(half, share), :]
 
 
@@ -306,7 +316,7 @@
         in_specs=in_specs,
         out_specs=[pl.BlockSpec(memory_space=pltpu.VMEM) for _ in outs],
         scratch_shapes=list(scratch),
-        compiler_params=pltpu.CompilerParams(vmem_limit_bytes=16 * 1024 * 1024),
+        compiler_params=pltpu.CompilerParams(vmem_limit_bytes=8 * 1024 * 1024),
         cost_estimate=pl.CostEstimate(flops=flops, bytes_accessed=size, transcendentals=0),
         name=name,
     )(*args)
@@ -346,10 +356,9 @@
     more = parts + channels // LANES
 
     edges = edge_slots[0, 0].reshape(2 * n_tiles, tile_rows)
-    block_row = tile_blocks[0, 0].reshape(1, 2 * n_tiles)
-    edges = jnp.concatenate([edges, jnp.pad(block_row, ((0, 7), (0, tile_rows - 2 * n_tiles)))], 0)
+    edges = jnp.concatenate([edges, jnp.pad(tile_blocks[0, 0], ((0, 0), (0, tile_rows - 2)))], 0)
     edges = swap(jnp.broadcast_to(edges[None], (n_dp, *edges.shape)), "dp")
-    blocks = edges[:, 2 * n_tiles, : 2 * n_tiles]
+    blocks = edges[:, 2 * n_tiles :, :2].reshape(n_dp, 2 * n_tiles)
 
     table, slots_row, payload = call(
         first_kernel,
@@ -390,7 +399,7 @@
     hidden, grad_pre, spread, payload = call(
         lambda *refs: dense_kernel(scale, cap, *refs),
         [((channels, LANES), BF), ((channels, LANES), BF), ((k, v_count), BF), ((n_dom * more, LANES), BF)],
-        [aggregate_all, self_t, gh_t, w_in, degree_row, slots_row, table, aggregate, cotangent, replica],
+        [aggregate_all, self_t, gh_t, w_in[channels:], degree_row, slots_row, table, aggregate, cotangent, replica],
         smem=(9,),
         scratch=[pltpu.VMEM((channels, v_count), BF), pltpu.VMEM((channels, v_count), BF)],
         name="dense",
@@ -399,7 +408,7 @@
     output, grad_self = call(
         rows_kernel,
         [((share, channels), BF), ((share, channels), F32)],
-        [hidden, grad_pre, w_in, w_out, b_out.reshape(1, -1), replica],
+        [hidden, grad_pre, w_self, w_out, b_out.reshape(1, -1), replica],
         smem=(5,),
         scratch=[pltpu.VMEM((LANES, channels), F32)],
         name="rows",

time: 208 us -> 204 us (0.981)
  Pallas kernels: 20.3 us -> 17.3 us
    pallas_call x8, Pallas kernels: 20.3 us -> 17.3 us  [call(): pl.pallas_call(kernel, out_shape=shapes, in_specs=in_specs, out_specs=[pl...]
  transfers between devices with their start and end apart: 5 -> 5, of which waited for: 5 -> 5; matrix products, arithmetic and copies ran while one was open for 0% -> 1% of each run, Pallas kernels for 1% -> 1%
where the time goes in v3:
time: 204 us; the launch traced here: 203 us
  waiting for transfers between devices  65.4 us (32%)
  blocking collectives  62 us (30%)
  starting transfers between devices  52.6 us (26%)
  Pallas kernels  17.3 us (8%)
  local copies, waits for them, and re-layouts  4.12 us (2%)
    all_to_all x5, waiting for transfers between devices, swap(): return lax.all_to_all(values, axis, split_axis=0, concat_axis=0, tiled=True)  65.4 us
    all_to_all x2, blocking collectives, swap(): return lax.all_to_all(values, axis, split_axis=0, concat_axis=0, tiled=True)  62 us
    all_to_all x5, starting transfers between devices, swap(): return lax.all_to_all(values, axis, split_axis=0, concat_axis=0, tiled=True)  52.6 us
    pallas_call x8, Pallas kernels, call(): pl.pallas_call(kernel, out_shape=shapes, in_specs=in_specs, out_specs=[pl...  17.3 us
  transfers between devices with their start and end apart: 5, of which 5 were waited for; matrix products, arithmetic and copies ran while one was open for 1% of the time, Pallas kernels for 1%

profile of v3, /device:TPU:1, one launch (start us, length us, event | category | flops | bytes accessed | tf_op | source)
XLA Modules:
  0.0 203.0 jit_solution(14835651565231924924)
XLA Ops:
  0.6 0.0 copy-start.9
  0.6 0.0 copy-start
  0.7 0.8 copy.24
  1.5 0.0 copy-done.9
  1.5 0.7 broadcast_in_dim.2
  2.2 0.0 copy-start.10
  2.2 7.7 %all-to-all-start.1 = ((s32[16,24,128]{2,1,0:T(8,128)}), s32[16,24,128]{2,1,0:T(8,128)S(1)}, u32[]{:S(2)}, u32[]{:S(2)}) async-start(s32[16,24,128]{2,1,0:T(8,128)} %broadcast_in_dim.2), calls=%async_computation.1 | async-start | bytes 393216 | tf_op jit(solution)/shard_map/all_to_all | solution.py:326
  9.9 0.0 copy-done.10
  9.9 0.1 copy.19
  10.0 0.0 copy-start.6
  10.0 0.0 copy-done
  10.0 0.6 copy-done.6
  10.6 1.6 first.1
  12.3 4.8 %all-to-all-done.1.refs_2_ = s32[16,24,128]{2,1,0:T(8,128)S(1)} async-done(((s32[16,24,128]{2,1,0:T(8,128)}), s32[16,24,128]{2,1,0:T(8,128)S(1)}, u32[]{:S(2)}, u32[]{:S(2)}) %all-to-all-start.1) | async-done | bytes 196640 | tf_op jit(solution)/shard_map/all_to_all | solution.py:326
  17.1 31.1 %all-to-all-start = ((bf16[64,2,128]{2,1,0:T(2,128)(2,1)}), bf16[64,2,128]{2,1,0:T(2,128)(2,1)S(1)}, u32[]{:S(2)}, u32[]{:S(2)}) async-start(bf16[64,2,128]{2,1,0:T(2,128)(2,1)} %bitcast.2), calls=%async_computation | async-start | bytes 65536 | tf_op jit(solution)/shard_map/all_to_all | solution.py:326
  48.2 0.0 copy-done.11
  48.3 0.1 copy.21
  48.4 0.1 copy.22.refs_3_
  48.5 22.1 %all-to-all-done = bf16[64,2,128]{2,1,0:T(2,128)(2,1)S(1)} async-done(((bf16[64,2,128]{2,1,0:T(2,128)(2,1)}), bf16[64,2,128]{2,1,0:T(2,128)(2,1)S(1)}, u32[]{:S(2)}, u32[]{:S(2)}) %all-to-all-start) | async-done | bytes 32800 | tf_op jit(solution)/shard_map/all_to_all | solution.py:326
  70.6 4.1 %edges.1 = (bf16[128,128]{1,0:T(8,128)(2,1)}, f32[16,1024]{1,0:T(8,128)S(1)}) custom-call(bf16[128,128]{1,0:T(8,128)(2,1)S(1)} %bitcast.24, bf16[16,1024]{1,0:T(8,128)(2,1)S(1)} %get-tuple-element.27.refs_1_.refs_6_, s32[16,24,128]{2,1,0:T(8,128)S(1)} %all-to-all-done.1.refs_2_, s32[16,16]{1,0:T(8,128)S(1)} %copy.22.refs_3_), custom_call_target="tpu_custom_call" | custom-call | bytes 361472 | tf_op jit(solution)/shard_map/edges/pallas_call | solution.py:313
  74.6 5.6 %all-to-all-start.2 = ((bf16[64,2,128]{2,1,0:T(2,128)(2,1)}), bf16[64,2,128]{2,1,0:T(2,128)(2,1)S(1)}, u32[]{:S(2)}, u32[]{:S(2)}) async-start(bf16[64,2,128]{2,1,0:T(2,128)(2,1)} %bitcast.7), calls=%async_computation.2 | async-start | bytes 65536 | tf_op jit(solution)/shard_map/all_to_all | solution.py:326
  80.3 0.0 copy-done.1
  80.3 0.0 copy-done.3
  80.3 0.3 fusion.2.refs_2_
  80.6 21.6 %all-to-all-done.2 = bf16[64,2,128]{2,1,0:T(2,128)(2,1)S(1)} async-done(((bf16[64,2,128]{2,1,0:T(2,128)(2,1)}), bf16[64,2,128]{2,1,0:T(2,128)(2,1)S(1)}, u32[]{:S(2)}, u32[]{:S(2)}) %all-to-all-start.2) | async-done | bytes 32800 | tf_op jit(solution)/shard_map/all_to_all | solution.py:326
  102.3 1.7 aggregate.1
  103.9 4.4 %all-to-all-start.3 = ((bf16[16,16,1024]{2,1,0:T(8,128)(2,1)}), bf16[16,16,1024]{2,1,0:T(8,128)(2,1)}, u32[]{:S(2)}, u32[]{:S(2)}) async-start(bf16[16,16,1024]{2,1,0:T(8,128)(2,1)} %get-tuple-element.31), calls=%async_computation.3 | async-start | bytes 1048576 | tf_op jit(solution)/shard_map/all_to_all | solution.py:326
  108.3 0.0 copy-done.7
  108.3 0.0 copy-start.8
  108.3 0.0 copy-start.12
  108.4 0.7 fusion.1
  109.0 0.3 copy-done.8
  109.3 0.0 copy-done.12
  109.3 0.4 convolution_add_fusion.refs_1_
  109.7 8.3 %all-to-all-done.3 = bf16[16,16,1024]{2,1,0:T(8,128)(2,1)} async-done(((bf16[16,16,1024]{2,1,0:T(8,128)(2,1)}), bf16[16,16,1024]{2,1,0:T(8,128)(2,1)}, u32[]{:S(2)}, u32[]{:S(2)}) %all-to-all-start.3) | async-done | bytes 524320 | tf_op jit(solution)/shard_map/all_to_all | solution.py:326
  118.0 2.9 %dense.1 = (bf16[256,128]{1,0:T(8,128)(2,1)S(1)}, bf16[256,128]{1,0:T(8,128)(2,1)S(1)}, bf16[16,1024]{1,0:T(8,128)(2,1)S(1)}, bf16[256,128]{1,0:T(8,128)(2,1)S(1)}) custom-call(bf16[256,1024]{1,0:T(8,128)(2,1)} %bitcast.10.refs_0_, f32[256,1024]{1,0:T(8,128)S(1)} %convolution_add_fusion.refs_1_, f32[256,1024]{1,0:T(8,128)S(1)} %fusion.2.refs_2_, ...), custom_call_target="tpu_custom_call" | custom-call | bytes 3579908 | tf_op jit(solution)/shard_map/dense/pallas_call | solution.py:313
  120.9 31.7 %all_to_all.59 = bf16[64,4,128]{2,1,0:T(4,128)(2,1)S(1)} all-to-all(bf16[64,4,128]{2,1,0:T(4,128)(2,1)S(1)} %bitcast.26), channel_id=1, replica_groups=mesh['dom'=64,'dp'=16] {'dom'}, dimensions={0} | all-to-all | bytes 131072 | tf_op jit(solution)/shard_map/all_to_all | solution.py:326
  152.6 3.6 %edges_back.1 = (bf16[256,128]{1,0:T(8,128)(2,1)S(1)}, f32[16,1024]{1,0:T(8,128)S(1)}) custom-call(bf16[256,128]{1,0:T(8,128)(2,1)S(1)} %bitcast.21, bf16[16,1024]{1,0:T(8,128)(2,1)S(1)} %get-tuple-element.37.refs_1_, s32[16,24,128]{2,1,0:T(8,128)S(1)} %all-to-all-done.1.refs_2_, s32[16,16]{1,0:T(8,128)S(1)} %copy.22.refs_3_), custom_call_target="tpu_custom_call" | custom-call | bytes 427008 | tf_op jit(solution)/shard_map/edges_back/pallas_call | solution.py:313
  156.2 30.4 %all_to_all.60 = bf16[64,4,128]{2,1,0:T(4,128)(2,1)S(1)} all-to-all(bf16[64,4,128]{2,1,0:T(4,128)(2,1)S(1)} %bitcast.27), channel_id=1, replica_groups=mesh['dom'=64,'dp'=16] {'dom'}, dimensions={0} | all-to-all | bytes 131072 | tf_op jit(solution)/shard_map/all_to_all | solution.py:326
  186.5 1.7 back.1
  188.2 3.7 %all-to-all-start.6 = ((bf16[16,128,128]{2,1,0:T(8,128)(2,1)}), bf16[16,128,128]{2,1,0:T(8,128)(2,1)S(1)}, u32[]{:S(2)}, u32[]{:S(2)}) async-start(bf16[16,128,128]{2,1,0:T(8,128)(2,1)} %back.1), calls=%async_computation.6 | async-start | bytes 1048576 | tf_op jit(solution)/shard_map/all_to_all | solution.py:326
  192.0 0.0 copy-start.5
  192.0 0.0 copy-done.2
  192.0 0.0 copy-done.4
  192.0 0.7 copy-done.5
  192.6 0.9 rows.1
  193.5 8.6 %all-to-all-done.6.arrived_ref = bf16[16,128,128]{2,1,0:T(8,128)(2,1)S(1)} async-done(((bf16[16,128,128]{2,1,0:T(8,128)(2,1)}), bf16[16,128,128]{2,1,0:T(8,128)(2,1)S(1)}, u32[]{:S(2)}, u32[]{:S(2)}) %all-to-all-start.6) | async-done | bytes 524320 | tf_op jit(solution)/shard_map/all_to_all | solution.py:326
  202.1 0.9 last.1
  (9 shorter events, 0.0 us)
Async XLA Ops:
  0.6 0.8 copy-start.9
  0.6 9.4 %copy-start = (bf16[1024,256]{1,0:T(8,128)(2,1)S(1)}, bf16[1024,256]{1,0:T(8,128)(2,1)}, u32[]{:S(2)}) copy-start(bf16[1024,256]{1,0:T(8,128)(2,1)} %features_ref.1) | copy-start | bytes 1572868
  2.2 7.7 %copy-start.10 = (s32[1,64,16]{1,2,0:T(8,128)S(1)}, s32[1,64,16]{1,2,0:T(8,128)}, u32[]{:S(2)}) copy-start(s32[1,64,16]{1,2,0:T(8,128)} %param.13) | copy-start | bytes 12292
  2.2 14.9 %all-to-all-start.1 = ((s32[16,24,128]{2,1,0:T(8,128)}), s32[16,24,128]{2,1,0:T(8,128)S(1)}, u32[]{:S(2)}, u32[]{:S(2)}) async-start(s32[16,24,128]{2,1,0:T(8,128)} %broadcast_in_dim.2), calls=%async_computation.1 | async-start | bytes 393216 | tf_op jit(solution)/shard_map/all_to_all | solution.py:326
  10.0 0.7 copy-start.6
  10.6 69.6 %copy-start.1 = (bf16[1024,256]{1,0:T(8,128)(2,1)S(1)}, bf16[1024,256]{1,0:T(8,128)(2,1)}, u32[]{:S(2)}) copy-start(bf16[1024,256]{1,0:T(8,128)(2,1)} %refs_8_.1) | copy-start | bytes 1572868
  17.1 31.1 %copy-start.11 = (s32[1024]{0:T(1024)S(1)}, s32[1024]{0:T(1024)}, u32[]{:S(2)}) copy-start(s32[1024]{0:T(1024)} %param.12) | copy-start | bytes 12292
  17.1 53.5 %all-to-all-start = ((bf16[64,2,128]{2,1,0:T(2,128)(2,1)}), bf16[64,2,128]{2,1,0:T(2,128)(2,1)S(1)}, u32[]{:S(2)}, u32[]{:S(2)}) async-start(bf16[64,2,128]{2,1,0:T(2,128)(2,1)} %bitcast.2), calls=%async_computation | async-start | bytes 65536 | tf_op jit(solution)/shard_map/all_to_all | solution.py:326
  70.6 9.7 %copy-start.3 = (bf16[256,256]{1,0:T(8,128)(2,1)S(1)}, bf16[256,256]{1,0:T(8,128)(2,1)}, u32[]{:S(2)}) copy-start(bf16[256,256]{1,0:T(8,128)(2,1)} %w_out_ref.1) | copy-start | bytes 393220
  74.6 27.6 %all-to-all-start.2 = ((bf16[64,2,128]{2,1,0:T(2,128)(2,1)}), bf16[64,2,128]{2,1,0:T(2,128)(2,1)S(1)}, u32[]{:S(2)}, u32[]{:S(2)}) async-start(bf16[64,2,128]{2,1,0:T(2,128)(2,1)} %bitcast.7), calls=%async_computation.2 | async-start | bytes 65536 | tf_op jit(solution)/shard_map/all_to_all | solution.py:326
  103.9 4.4 %copy-start.7 = (bf16[512,256]{1,0:T(8,128)(2,1)S(1)}, bf16[512,256]{1,0:T(8,128)(2,1)}, u32[]{:S(2)}) copy-start(bf16[512,256]{1,0:T(8,128)(2,1)} %param.17) | copy-start | bytes 786436
  103.9 14.0 %all-to-all-start.3 = ((bf16[16,16,1024]{2,1,0:T(8,128)(2,1)}), bf16[16,16,1024]{2,1,0:T(8,128)(2,1)}, u32[]{:S(2)}, u32[]{:S(2)}) async-start(bf16[16,16,1024]{2,1,0:T(8,128)(2,1)} %get-tuple-element.31), calls=%async_computation.3 | async-start | bytes 1048576 | tf_op jit(solution)/shard_map/all_to_all | solution.py:326
  108.3 1.0 copy-start.8
  108.3 1.0 copy-start.12
  188.2 3.7 %copy-start.2 = (bf16[256,256]{1,0:T(8,128)(2,1)S(1)}, bf16[256,256]{1,0:T(8,128)(2,1)}, u32[]{:S(2)}) copy-start(bf16[256,256]{1,0:T(8,128)(2,1)} %get-tuple-element.46.w_self_ref) | copy-start | bytes 393220
  188.2 3.7 %copy-start.4 = (bf16[256,256]{1,0:T(8,128)(2,1)S(1)}, bf16[256,256]{1,0:T(8,128)(2,1)}, u32[]{:S(2)}) copy-start(bf16[256,256]{1,0:T(8,128)(2,1)} %w_out_ref.1) | copy-start | bytes 393220
  188.2 13.8 %all-to-all-start.6 = ((bf16[16,128,128]{2,1,0:T(8,128)(2,1)}), bf16[16,128,128]{2,1,0:T(8,128)(2,1)S(1)}, u32[]{:S(2)}, u32[]{:S(2)}) async-start(bf16[16,128,128]{2,1,0:T(8,128)(2,1)} %back.1), calls=%async_computation.6 | async-start | bytes 1048576 | tf_op jit(solution)/shard_map/all_to_all | solution.py:326
  192.0 0.7 copy-start.5

commit v4 on v3

--- a/solution.py
+++ b/solution.py
@@ -26,12 +26,6 @@
     width = slots_row.shape[1]
     rows = lax.broadcasted_iota(jnp.int32, (count, width), 0)
     return hot(rows == slots_row - first)
-
-
-def peer_choice(n_peers, n_slots):
-    peers = lax.broadcasted_iota(jnp.int32, (n_peers, 1), 0)
-    slots = lax.broadcasted_iota(jnp.int32, (1, n_slots), 1)
-    return hot(slots // (n_slots // n_peers) == peers)
 
 
 def pick(table, slots_row):
@@ -85,23 +79,45 @@
     return total
 
 
+def to_rows(columns):
+    width = columns.shape[1] // PART
+    tall = jnp.concatenate([columns[:, c * width : c * width + width] for c in range(PART)], 0)
+    return tall.T.astype(BF)
+
+
+def from_tall(tall):
+    k = tall.shape[0] // PART
+    return jnp.concatenate([tall[c * k : c * k + k] for c in range(PART)], 1)
+
+
+def part_rows(n_rows, per_peer, parts):
+    n_parts = n_rows // per_peer * parts
+    rows = lax.broadcasted_iota(jnp.int32, (n_rows, 1), 0)
+    part = lax.rem(rows, per_peer)
+    source = jnp.where(part < parts, rows // per_peer * parts + part, -1)
+    return hot(lax.broadcasted_iota(jnp.int32, (1, n_parts), 1) == source)
+
+
 def slots_of(send_rows, send_counts, v_count):
     n_peers, cap = send_rows.shape
     n_slots = n_peers * cap
-    chosen = peer_choice(n_peers, n_slots)
+    parts = cap // PART
+    width = n_peers * parts
+    slots = lax.broadcasted_iota(jnp.int32, (1, n_slots), 1)
+    within = lax.rem(slots, width)
+    place = lax.rem(within, parts) * PART + slots // width
+    chosen = hot(lax.broadcasted_iota(jnp.int32, (n_peers, 1), 0) == within // parts)
     base = 32
     high = send_rows // base
     low = send_rows - high * base
-    lane = cap_lane((cap, n_slots), cap)
-    c = lax.broadcasted_iota(jnp.int32, (cap, n_slots), 0)
     both = matmul(high.astype(F32).astype(BF), chosen, 0, 0) * base + matmul(
         low.astype(F32).astype(BF), chosen, 0, 0
     )
-    rows = jnp.sum(jnp.where(lane == c, both, 0.0), 0, keepdims=True)
+    c = lax.broadcasted_iota(jnp.int32, (cap, n_slots), 0)
+    rows = jnp.sum(jnp.where(c == place, both, 0.0), 0, keepdims=True)
     counts = jnp.broadcast_to(send_counts.astype(F32), (8, n_peers)).astype(BF)
     counts = matmul(counts, chosen)[:1]
-    unused = cap_lane((1, n_slots), cap).astype(F32) >= counts
-    return jnp.where(unused, float(v_count), rows).astype(jnp.int32)
+    return jnp.where(place.astype(F32) >= counts, float(v_count), rows).astype(jnp.int32)
 
 
 def first_kernel(
@@ -115,14 +131,26 @@
     table_ref[...] = table
     slots = slots_of(send_rows_ref[...], send_counts_ref[...], v_count)
     slots_ref[...] = slots
-    cap = send_rows_ref.shape[1]
-    payload_ref[...] = to_peers(pick(table, slots), cap // PART, cap).astype(BF)
+    payload_ref[...] = to_rows(pick(table, slots))
+
+
+def inputs_kernel(
+    features_ref, cotangent_ref, w_in_ref, b_in_ref, w_out_ref, b_out_ref, degree_ref, self_ref, gh_ref,
+    vectors_ref,
+):
+    w_self = w_in_ref[: features_ref.shape[1], :].astype(F32).T.astype(BF)
+    self_ref[...] = matmul(w_self, features_ref[...], 1, 1) + b_in_ref[...].T
+    gh_ref[...] = matmul(w_out_ref[...], cotangent_ref[...], 1, 1)
+    vectors_ref[...] = jnp.zeros_like(vectors_ref)
+    vectors_ref[:1, :] = degree_ref[...].astype(F32)
+    vectors_ref[1:2, : b_out_ref.shape[1]] = b_out_ref[...]
 
 
 def edges_kernel(
-    cap, per_peer, transpose, arrived_ref, owned_ref, edges_ref, blocks_ref, payload_ref, own_ref,
-    table, total,
-):
+    cap, per_peer, transpose, arrived_ref, owned_ref, edges_ref, blocks_ref, ready_ref, payload_ref,
+    own_ref, table, total,
+):
+    del ready_ref
     k, v_count = owned_ref.shape
     own_blocks = v_count // LANES
     all_blocks = table.shape[0]
@@ -188,35 +216,39 @@
     payload_ref[...] = outgoing.astype(BF)
 
 
-def aggregate_kernel(cap, arrived_ref, own_ref, slots_ref, degree_ref, aggregate_ref, copies_ref):
+def aggregate_kernel(arrived_ref, own_ref, slots_ref, vectors_ref, aggregate_ref, copies_ref):
     k, v_count = own_ref.shape
-    returned = from_peers(arrived_ref[...], cap // PART, cap).astype(BF)
+    returned = from_tall(arrived_ref[...].astype(F32).T.astype(BF))
     summed = own_ref[...] + scatter(returned, slots_ref[...], v_count)
-    aggregate = (summed / degree_ref[...]).astype(BF)
+    aggregate = (summed / vectors_ref[:1, :]).astype(BF)
     aggregate_ref[...] = aggregate
     for r in range(copies_ref.shape[0]):
         copies_ref[r] = aggregate
 
 
 def dense_kernel(
-    scale, cap, aggregate_ref, self_ref, gh_ref, w_neigh_ref, degree_ref, slots_ref, table_ref, mine_ref,
-    cotangent_ref, replica_ref, hidden_out_ref, grad_pre_out_ref, spread_ref, payload_ref, hidden_ref,
-    grad_pre_ref,
+    scale, cap, aggregate_ref, self_ref, gh_ref, w_in_ref, vectors_ref, slots_ref, table_ref, mine_ref,
+    cotangent_ref, w_out_ref, replica_ref, output_ref, grad_self_ref, spread_ref, payload_ref,
+    hidden_ref, grad_pre_ref, rows_ref,
 ):
     k, v_count = spread_ref.shape
     channels = aggregate_ref.shape[0]
-    pre = self_ref[...] + matmul(w_neigh_ref[...], aggregate_ref[...], 0, 0)
+    pre = self_ref[...] + matmul(w_in_ref[channels:, :], aggregate_ref[...], 0, 0)
     sigmoid = 1.0 / (1.0 + jnp.exp(-pre))
     hidden_ref[...] = (pre * sigmoid).astype(BF)
     grad_pre = (gh_ref[...] * (sigmoid * (1.0 + pre * (1.0 - sigmoid)))).astype(BF)
     grad_pre_ref[...] = grad_pre
-    per_block = LANES // (v_count * k // channels)
+    share = output_ref.shape[0]
+    per_block = LANES // share
     block = pl.multiple_of((replica_ref[0] // per_block) * LANES, LANES)
-    hidden_out_ref[...] = hidden_ref[:, pl.ds(block, LANES)]
-    grad_pre_out_ref[...] = grad_pre_ref[:, pl.ds(block, LANES)]
+    half = pl.multiple_of(lax.rem(replica_ref[0], per_block) * share, share)
+    rows_ref[0] = matmul(hidden_ref[:, pl.ds(block, LANES)], w_out_ref[...], 0, 0)
+    output_ref[...] = (rows_ref[0, pl.ds(half, share), :] + vectors_ref[1:2, :channels]).astype(BF)
+    rows_ref[1] = matmul(w_in_ref[:channels, :], grad_pre_ref[:, pl.ds(block, LANES)]).T
+    grad_self_ref[...] = rows_ref[1, pl.ds(half, share), :]
     first = pl.multiple_of(replica_ref[0] * k, k)
-    spread = matmul(w_neigh_ref[pl.ds(first, k), :], grad_pre)
-    spread = (spread / degree_ref[...]).astype(BF)
+    spread = matmul(w_in_ref[pl.ds(pl.multiple_of(channels + first, k), k), :], grad_pre)
+    spread = (spread / vectors_ref[:1, :]).astype(BF)
     spread_ref[...] = spread
 
     ones = jnp.ones((k, v_count), BF)
@@ -229,8 +261,9 @@
     parts = cap // PART
     halves = channels // LANES
     per_peer = parts + halves
-    payload = to_peers(pick(spread, slots_ref[...]), per_peer, cap)
-    n_rows = payload.shape[0]
+    picked = to_rows(pick(spread, slots_ref[...]))
+    n_rows = picked.shape[0] // parts * per_peer
+    payload = matmul(part_rows(n_rows, per_peer, parts), picked)
     rows = lax.broadcasted_iota(jnp.int32, (n_rows, grads.shape[0]), 0)
     source = lax.broadcasted_iota(jnp.int32, (n_rows, grads.shape[0]), 1)
     peer = jnp.where(source == 4 * k, 3 * k + 1, jnp.where(source > 3 * k, -1, source))
@@ -240,27 +273,13 @@
     payload_ref[...] = payload.astype(BF)
 
 
-def rows_kernel(
-    hidden_ref, grad_pre_ref, w_self_ref, w_out_ref, b_out_ref, replica_ref, output_ref, grad_self_ref,
-    rows_ref,
-):
-    channels = hidden_ref.shape[0]
-    share = output_ref.shape[0]
-    replica = replica_ref[0]
-    per_block = LANES // share
-    half = pl.multiple_of(lax.rem(replica, per_block) * share, share)
-    rows_ref[...] = matmul(hidden_ref[...], w_out_ref[...], 0, 0)
-    output_ref[...] = (rows_ref[pl.ds(half, share), :] + b_out_ref[...]).astype(BF)
-    rows_ref[...] = matmul(w_self_ref[...], grad_pre_ref[...]).T
-    grad_self_ref[...] = rows_ref[pl.ds(half, share), :]
-
-
 def back_kernel(cap, per_peer, arrived_ref, own_ref, slots_ref, copies_ref):
     k, v_count = own_ref.shape
     n_dp = copies_ref.shape[0]
     share = v_count // n_dp
     arrived = arrived_ref[...]
-    returned = from_peers(arrived, per_peer, cap).astype(BF)
+    tall = matmul(arrived, part_rows(arrived.shape[0], per_peer, cap // PART), 0, 0)
+    returned = from_tall(tall.astype(BF))
     summed = (own_ref[...] + scatter(returned, slots_ref[...], v_count)).astype(BF)
     n_rows = copies_ref.shape[1] - k
     parts = cap // PART
@@ -278,9 +297,10 @@
 
 
 def last_kernel(
-    arrived_ref, grad_self_ref, replica_ref, grad_features_ref, grad_w_in_ref, grad_b_in_ref,
-    grad_w_out_ref, grad_b_out_ref, rows_ref,
-):
+    arrived_ref, grad_self_ref, rows_out_ref, replica_ref, output_ref, grad_features_ref, grad_w_in_ref,
+    grad_b_in_ref, grad_w_out_ref, grad_b_out_ref, rows_ref,
+):
+    output_ref[...] = rows_out_ref[...]
     share, channels = grad_features_ref.shape
     n_dp = arrived_ref.shape[0]
     k = channels // n_dp
@@ -351,7 +371,6 @@
     blocks_count = (v_count + n_slots) // LANES
     scale = 1.0 / math.sqrt(v_count * n_dom)
 
-    degree_row = degree.astype(F32).reshape(1, v_count)
     parts = cap // PART
     more = parts + channels // LANES
 
@@ -368,16 +387,21 @@
         name="first",
     )
     arrived = swap(payload, "dom")
-
-    w_self = w_in[:channels]
-    self_t = jnp.einsum("ah,va->hv", w_self, features, preferred_element_type=F32) + b_in[:, None]
-    gh_t = jnp.einsum("ho,vo->hv", w_out, cotangent, preferred_element_type=F32)
+    self_t, gh_t, vectors = call(
+        inputs_kernel,
+        [((channels, v_count), F32), ((channels, v_count), F32), ((8, v_count), F32)],
+        [
+            features, cotangent, w_in, b_in.reshape(1, -1), w_out, b_out.reshape(1, -1),
+            degree.reshape(1, v_count),
+        ],
+        name="inputs",
+    )
 
     def edge_pass(arrived, owned, per_peer, transpose):
         return call(
             lambda *refs: edges_kernel(cap, per_peer, transpose, *refs),
             [((n_dom * per_peer, LANES), BF), ((k, v_count), F32)],
-            [arrived, owned, edges, blocks],
+            [arrived, owned, edges, blocks, vectors],
             smem=(3,),
             scratch=[
                 pltpu.VMEM((blocks_count, k, LANES), BF),
@@ -389,30 +413,29 @@
     payload, own = edge_pass(arrived, table, parts, False)
     arrived = swap(payload, "dom")
     aggregate, copies = call(
-        lambda *refs: aggregate_kernel(cap, *refs),
+        aggregate_kernel,
         [((k, v_count), BF), ((n_dp, k, v_count), BF)],
-        [arrived, own, slots_row, degree_row],
+        [arrived, own, slots_row, vectors],
         name="aggregate",
     )
     aggregate_all = swap(copies, "dp").reshape(channels, v_count)
 
-    hidden, grad_pre, spread, payload = call(
+    output, grad_self, spread, payload = call(
         lambda *refs: dense_kernel(scale, cap, *refs),
-        [((channels, LANES), BF), ((channels, LANES), BF), ((k, v_count), BF), ((n_dom * more, LANES), BF)],
-        [aggregate_all, self_t, gh_t, w_in[channels:], degree_row, slots_row, table, aggregate, cotangent, replica],
-        smem=(9,),
-        scratch=[pltpu.VMEM((channels, v_count), BF), pltpu.VMEM((channels, v_count), BF)],
+        [((share, channels), BF), ((share, channels), F32), ((k, v_count), BF), ((n_dom * more, LANES), BF)],
+        [
+            aggregate_all, self_t, gh_t, w_in, vectors, slots_row, table, aggregate, cotangent, w_out,
+            replica,
+        ],
+        smem=(10,),
+        scratch=[
+            pltpu.VMEM((channels, v_count), BF),
+            pltpu.VMEM((channels, v_count), BF),
+            pltpu.VMEM((2, LANES, channels), F32),
+        ],
         name="dense",
     )
     arrived = swap(payload, "dom")
-    output, grad_self = call(
-        rows_kernel,
-        [((share, channels), BF), ((share, channels), F32)],
-        [hidden, grad_pre, w_self, w_out, b_out.reshape(1, -1), replica],
-        smem=(5,),
-        scratch=[pltpu.VMEM((LANES, channels), F32)],
-        name="rows",
-    )
     payload, own = edge_pass(arrived, spread, more, True)
     arrived = swap(payload, "dom")
     grad_rows = 2 * 3 * k + k
@@ -423,17 +446,18 @@
         name="back",
     )
     arrived = swap(copies, "dp")
-    grad_features, grad_w_in, grad_b_in, grad_w_out, grad_b_out = call(
+    output, grad_features, grad_w_in, grad_b_in, grad_w_out, grad_b_out = call(
         last_kernel,
         [
+            ((share, channels), BF),
             ((share, channels), BF),
             ((2 * channels, channels), F32),
             ((1, channels), F32),
             ((channels, channels), F32),
             ((1, channels), F32),
         ],
-        [arrived, grad_self, replica],
-        smem=(2,),
+        [arrived, grad_self, output, replica],
+        smem=(3,),
         scratch=[pltpu.VMEM((LANES, channels), F32)],
         name="last",
     )

time: 204 us -> 197 us (0.966)
  blocking collectives: 62 us -> 114 us
  waiting for transfers between devices: 65.4 us -> 25.5 us
  starting transfers between devices: 52.6 us -> 39 us
  Pallas kernels: 17.3 us -> 13.4 us
    all_to_all x2 -> x5, blocking collectives: 62 us -> 114 us  [swap(): return lax.all_to_all(values, axis, split_axis=0, concat_axis=0, tiled=True)]
    all_to_all x5 -> x2, waiting for transfers between devices: 65.4 us -> 25.5 us  [swap(): return lax.all_to_all(values, axis, split_axis=0, concat_axis=0, tiled=True)]
    all_to_all x5 -> x2, starting transfers between devices: 52.6 us -> 39 us  [swap(): return lax.all_to_all(values, axis, split_axis=0, concat_axis=0, tiled=True)]
    pallas_call x8, Pallas kernels: 17.3 us -> 13.4 us  [call(): pl.pallas_call(kernel, out_shape=shapes, in_specs=in_specs, out_specs=[pl...]
  transfers between devices with their start and end apart: 5 -> 2, of which waited for: 5 -> 2; matrix products, arithmetic and copies ran while one was open for 1% -> 0% of each run, Pallas kernels for 1% -> 1%
where the time goes in v4:
time: 197 us; the launch traced here: 196 us
  blocking collectives  114 us (58%)
  starting transfers between devices  39 us (20%)
  waiting for transfers between devices  25.5 us (13%)
  Pallas kernels  13.4 us (7%)
  local copies, waits for them, and re-layouts  3.43 us (2%)
    all_to_all x5, blocking collectives, swap(): return lax.all_to_all(values, axis, split_axis=0, concat_axis=0, tiled=True)  114 us
    all_to_all x2, starting transfers between devices, swap(): return lax.all_to_all(values, axis, split_axis=0, concat_axis=0, tiled=True)  39 us
    all_to_all x2, waiting for transfers between devices, swap(): return lax.all_to_all(values, axis, split_axis=0, concat_axis=0, tiled=True)  25.5 us
    pallas_call x8, Pallas kernels, call(): pl.pallas_call(kernel, out_shape=shapes, in_specs=in_specs, out_specs=[pl...  13.4 us
  transfers between devices with their start and end apart: 2, of which 2 were waited for; matrix products, arithmetic and copies ran while one was open for 0% of the time, Pallas kernels for 1%

profile of v4, /device:TPU:1, one launch (start us, length us, event | category | flops | bytes accessed | tf_op | source)
XLA Modules:
  0.0 196.3 jit_solution(16781250632284584703)
XLA Ops:
  0.6 0.0 copy-start.9
  0.6 0.0 copy-start
  0.7 0.8 copy.24
  1.5 0.0 copy-done.9
  1.5 0.0 copy-start.10
  1.5 0.0 copy-start.8
  1.5 0.7 broadcast_in_dim.2
  2.2 0.0 copy-start.1
  2.2 7.7 %all-to-all-start.1 = ((s32[16,24,128]{2,1,0:T(8,128)}), s32[16,24,128]{2,1,0:T(8,128)S(1)}, u32[]{:S(2)}, u32[]{:S(2)}) async-start(s32[16,24,128]{2,1,0:T(8,128)} %broadcast_in_dim.2), calls=%async_computation.1 | async-start | bytes 393216 | tf_op jit(solution)/shard_map/all_to_all | solution.py:346
  9.9 0.0 copy-done.10
  9.9 0.1 copy.19
  10.0 0.0 copy-done
  10.0 0.0 copy-done.8
  10.0 0.0 copy-start.4
  10.0 1.4 first.1
  11.4 5.7 %all-to-all-done.1.refs_2_ = s32[16,24,128]{2,1,0:T(8,128)S(1)} async-done(((s32[16,24,128]{2,1,0:T(8,128)}), s32[16,24,128]{2,1,0:T(8,128)S(1)}, u32[]{:S(2)}, u32[]{:S(2)}) %all-to-all-start.1) | async-done | bytes 196640 | tf_op jit(solution)/shard_map/all_to_all | solution.py:346
  17.1 0.0 copy-start.7
  17.1 31.3 %all-to-all-start = ((bf16[64,2,128]{2,1,0:T(2,128)(2,1)}), bf16[64,2,128]{2,1,0:T(2,128)(2,1)}, u32[]{:S(2)}, u32[]{:S(2)}) async-start(bf16[64,2,128]{2,1,0:T(2,128)(2,1)} %bitcast.2), calls=%async_computation | async-start | bytes 65536 | tf_op jit(solution)/shard_map/all_to_all | solution.py:346
  48.4 0.0 copy-start.5
  48.4 0.0 copy-start.6
  48.5 0.0 copy-done.1
  48.5 0.0 copy-done.4
  48.5 0.0 copy-done.7
  48.5 0.6 copy-done.5
  49.1 0.0 copy-done.6
  49.1 0.0 copy-start.2
  49.1 0.9 copy-done.2
  50.1 0.5 inputs.1
  50.6 0.1 copy.21
  50.7 0.1 copy.22.refs_3_
  50.8 19.9 %all-to-all-done = bf16[64,2,128]{2,1,0:T(2,128)(2,1)} async-done(((bf16[64,2,128]{2,1,0:T(2,128)(2,1)}), bf16[64,2,128]{2,1,0:T(2,128)(2,1)}, u32[]{:S(2)}, u32[]{:S(2)}) %all-to-all-start) | async-done | bytes 32800 | tf_op jit(solution)/shard_map/all_to_all | solution.py:346
  70.7 3.5 %edges.1 = (bf16[128,128]{1,0:T(8,128)(2,1)S(1)}, f32[16,1024]{1,0:T(8,128)S(1)}) custom-call(bf16[128,128]{1,0:T(8,128)(2,1)} %bitcast.3.refs_0_, bf16[16,1024]{1,0:T(8,128)(2,1)S(1)} %get-tuple-element.29.refs_1_.refs_6_, s32[16,24,128]{2,1,0:T(8,128)S(1)} %all-to-all-done.1.refs_2_, s32[16,16]{1,0:T(8,128)S(1)} %copy.22.refs_3_, ...), custom_call_target="tpu_custom_call" | custom-call | bytes 394240 | tf_op jit(solution)/shard_map/edges/pallas_call | solution.py:333
  74.2 26.8 %all_to_all.59 = bf16[64,2,128]{2,1,0:T(2,128)(2,1)S(1)} all-to-all(bf16[64,2,128]{2,1,0:T(2,128)(2,1)S(1)} %bitcast.26), channel_id=1, replica_groups=mesh['dom'=64,'dp'=16] {'dom'}, dimensions={0} | all-to-all | bytes 65536 | tf_op jit(solution)/shard_map/all_to_all | solution.py:346
  101.0 0.7 aggregate.1
  101.8 0.0 copy-start.3
  101.8 12.3 %all_to_all.60 = bf16[16,16,1024]{2,1,0:T(8,128)(2,1)S(1)} all-to-all(bf16[16,16,1024]{2,1,0:T(8,128)(2,1)S(1)} %get-tuple-element.34), channel_id=1, replica_groups=mesh['dom'=64,'dp'=16] {'dp'}, dimensions={0} | all-to-all | bytes 1048576 | tf_op jit(solution)/shard_map/all_to_all | solution.py:346
  114.0 0.0 copy-done.3
  114.0 1.9 dense.1
  115.9 31.9 %all_to_all.61 = bf16[64,4,128]{2,1,0:T(4,128)(2,1)S(1)} all-to-all(bf16[64,4,128]{2,1,0:T(4,128)(2,1)S(1)} %bitcast.24), channel_id=1, replica_groups=mesh['dom'=64,'dp'=16] {'dom'}, dimensions={0} | all-to-all | bytes 131072 | tf_op jit(solution)/shard_map/all_to_all | solution.py:346
  147.8 3.6 %edges_back.1 = (bf16[256,128]{1,0:T(8,128)(2,1)S(1)}, f32[16,1024]{1,0:T(8,128)S(1)}) custom-call(bf16[256,128]{1,0:T(8,128)(2,1)S(1)} %bitcast.21, bf16[16,1024]{1,0:T(8,128)(2,1)S(1)} %get-tuple-element.39.refs_1_, s32[16,24,128]{2,1,0:T(8,128)S(1)} %all-to-all-done.1.refs_2_, s32[16,16]{1,0:T(8,128)S(1)} %copy.22.refs_3_, ...), custom_call_target="tpu_custom_call" | custom-call | bytes 459776 | tf_op jit(solution)/shard_map/edges_back/pallas_call | solution.py:333
  151.4 30.4 %all_to_all.62 = bf16[64,4,128]{2,1,0:T(4,128)(2,1)S(1)} all-to-all(bf16[64,4,128]{2,1,0:T(4,128)(2,1)S(1)} %bitcast.25), channel_id=1, replica_groups=mesh['dom'=64,'dp'=16] {'dom'}, dimensions={0} | all-to-all | bytes 131072 | tf_op jit(solution)/shard_map/all_to_all | solution.py:346
  181.8 0.9 back.1
  182.6 12.7 %all_to_all.63.arrived_ref = bf16[16,128,128]{2,1,0:T(8,128)(2,1)S(1)} all-to-all(bf16[16,128,128]{2,1,0:T(8,128)(2,1)S(1)} %back.1), channel_id=1, replica_groups=mesh['dom'=64,'dp'=16] {'dp'}, dimensions={0} | all-to-all | bytes 1048576 | tf_op jit(solution)/shard_map/all_to_all | solution.py:346
  195.3 1.0 last.1
  (2 shorter events, 0.0 us)
Async XLA Ops:
  0.6 0.8 copy-start.9
  0.6 9.4 %copy-start = (bf16[1024,256]{1,0:T(8,128)(2,1)S(1)}, bf16[1024,256]{1,0:T(8,128)(2,1)}, u32[]{:S(2)}) copy-start(bf16[1024,256]{1,0:T(8,128)(2,1)} %features_ref.3) | copy-start | bytes 1572868
  1.5 8.4 %copy-start.10 = (s32[1,64,16]{1,2,0:T(8,128)S(1)}, s32[1,64,16]{1,2,0:T(8,128)}, u32[]{:S(2)}) copy-start(s32[1,64,16]{1,2,0:T(8,128)} %param.13) | copy-start | bytes 12292
  1.5 8.5 %copy-start.8 = (s32[1,64]{1,0:T(1,128)S(1)}, s32[1,64]{1,0:T(1,128)}, u32[]{:S(2)}) copy-start(s32[1,64]{1,0:T(1,128)} %send_counts_ref.1) | copy-start | bytes 772
  2.2 46.3 %copy-start.1 = (bf16[1024,256]{1,0:T(8,128)(2,1)S(1)}, bf16[1024,256]{1,0:T(8,128)(2,1)}, u32[]{:S(2)}) copy-start(bf16[1024,256]{1,0:T(8,128)(2,1)} %refs_8_.1) | copy-start | bytes 1572868
  2.2 14.9 %all-to-all-start.1 = ((s32[16,24,128]{2,1,0:T(8,128)}), s32[16,24,128]{2,1,0:T(8,128)S(1)}, u32[]{:S(2)}, u32[]{:S(2)}) async-start(s32[16,24,128]{2,1,0:T(8,128)} %broadcast_in_dim.2), calls=%async_computation.1 | async-start | bytes 393216 | tf_op jit(solution)/shard_map/all_to_all | solution.py:346
  10.0 38.5 %copy-start.4 = (bf16[256,256]{1,0:T(8,128)(2,1)S(1)}, bf16[256,256]{1,0:T(8,128)(2,1)}, u32[]{:S(2)}) copy-start(bf16[256,256]{1,0:T(8,128)(2,1)} %refs_9_.1) | copy-start | bytes 393220
  17.1 31.4 %copy-start.7 = (f32[256]{0:T(256)S(1)}, f32[256]{0:T(256)}, u32[]{:S(2)}) copy-start(f32[256]{0:T(256)} %param.20) | copy-start | bytes 3076
  17.1 53.6 %all-to-all-start = ((bf16[64,2,128]{2,1,0:T(2,128)(2,1)}), bf16[64,2,128]{2,1,0:T(2,128)(2,1)}, u32[]{:S(2)}, u32[]{:S(2)}) async-start(bf16[64,2,128]{2,1,0:T(2,128)(2,1)} %bitcast.2), calls=%async_computation | async-start | bytes 65536 | tf_op jit(solution)/shard_map/all_to_all | solution.py:346
  48.4 0.7 copy-start.5
  48.4 0.7 copy-start.6
  49.1 0.9 copy-start.2
  101.8 12.3 %copy-start.3 = (bf16[512,256]{1,0:T(8,128)(2,1)S(1)}, bf16[512,256]{1,0:T(8,128)(2,1)}, u32[]{:S(2)}) copy-start(bf16[512,256]{1,0:T(8,128)(2,1)} %refs_3_.1) | copy-start | bytes 786436

commit v5 on v4

--- a/solution.py
+++ b/solution.py
@@ -11,7 +11,17 @@
 F32 = jnp.float32
 LANES = 128
 PART = 8
-GROUPS = 8
+GROUPS = 16
+SHIFT = 16
+
+
+def far(size):
+    return size // 2 + size // 8
+
+
+def turn(rows):
+    half = rows.shape[0] // 2
+    return jnp.concatenate([rows[half:], rows[:half]], 0)
 
 
 def matmul(a, b, ca=1, cb=0):
@@ -120,6 +130,18 @@
     return jnp.where(place.astype(F32) >= counts, float(v_count), rows).astype(jnp.int32)
 
 
+def pack_kernel(edges_ref, blocks_ref, copies_ref):
+    n_tiles, _, width = edges_ref.shape
+    sources, targets = edges_ref[:, 0, :], edges_ref[:, 1, :]
+    packed = (targets << SHIFT) + (sources & ((1 << SHIFT) - 1))
+    lane = lax.broadcasted_iota(jnp.int32, (n_tiles, width), 1)
+    blocks = blocks_ref[...]
+    blocks = jnp.where(lane == 0, blocks[:, :1], jnp.where(lane == 1, blocks[:, 1:2], 0))
+    for r in range(copies_ref.shape[0]):
+        copies_ref[r, :n_tiles, :] = packed
+        copies_ref[r, n_tiles:, :] = blocks
+
+
 def first_kernel(
     features_ref, send_rows_ref, send_counts_ref, replica_ref, table_ref, slots_ref, payload_ref
 ):
@@ -131,7 +153,7 @@
     table_ref[...] = table
     slots = slots_of(send_rows_ref[...], send_counts_ref[...], v_count)
     slots_ref[...] = slots
-    payload_ref[...] = to_rows(pick(table, slots))
+    payload_ref[...] = turn(to_rows(pick(table, slots)))
 
 
 def inputs_kernel(
@@ -154,9 +176,9 @@
     k, v_count = owned_ref.shape
     own_blocks = v_count // LANES
     all_blocks = table.shape[0]
-    arrived = arrived_ref[...]
-    mirrors = from_peers(arrived, per_peer, cap).astype(BF)
-    owned = owned_ref[...]
+    arrived = turn(arrived_ref[...])
+    mirrors = from_peers(arrived, per_peer, cap)
+    owned = owned_ref[...].astype(F32)
     for b in range(own_blocks):
         table[b] = owned[:, b * LANES : b * LANES + LANES]
     for b in range(own_blocks, all_blocks):
@@ -164,36 +186,33 @@
         table[b] = mirrors[:, first : first + LANES]
     total[...] = jnp.zeros_like(total)
     n_groups, group_rows, width = edges_ref.shape
-    per_group = group_rows // 3
-    positions = lax.broadcasted_iota(jnp.int32, (LANES, 2 * width), 0)
+    per_group = group_rows // 2
+    positions = lax.broadcasted_iota(jnp.int32, (LANES, width), 0)
     a, b = (1, 0) if transpose else (0, 1)
     together = math.gcd(n_groups, GROUPS)
     tiles = [(j, t) for j in range(together) for t in range(per_group)]
-    pairs = list(zip(tiles[::2], tiles[1::2]))
-
-    def halves(product):
-        return product[:k, :LANES], product[k:, LANES:]
 
     def group(i, carry):
         g = i * together
 
         def slots(tile, side):
-            row = 2 * tile[1] + side
-            return edges_ref[g + tile[0], row : row + 1, :]
+            packed = edges_ref[g + tile[0], tile[1] : tile[1] + 1, :]
+            return packed >> SHIFT if side else packed & ((1 << SHIFT) - 1)
 
         def block(tile, side):
             return blocks_ref[g + tile[0], 2 * tile[1] + side]
 
         gathered = []
-        for one, two in pairs:
-            left = jnp.concatenate([table[block(one, a)], table[block(two, a)]], 0)
-            right = hot(positions == jnp.concatenate([slots(one, a), slots(two, a)], 1))
-            gathered.append(jnp.concatenate(halves(matmul(left, right)), 0).astype(BF))
+        for tile in tiles:
+            lanes = jnp.broadcast_to(slots(tile, a) & (LANES - 1), (k, width))
+            values = jnp.take_along_axis(table[block(tile, a)], lanes, axis=1, mode="promise_in_bounds")
+            gathered.append(values.astype(BF))
         placed = []
-        for (one, two), values in zip(pairs, gathered):
-            rows = positions[:, :width]
-            right = jnp.concatenate([hot(rows == slots(one, b)), hot(rows == slots(two, b))], 0)
-            placed.extend(halves(matmul(values, right, 1, 1)))
+        for n in range(0, len(tiles), 2):
+            left = jnp.concatenate(gathered[n : n + 2], 0)
+            right = jnp.concatenate([hot(positions == slots(tile, b)) for tile in tiles[n : n + 2]], 0)
+            product = matmul(left, right, 1, 1)
+            placed.extend([product[:k, :LANES], product[k:, LANES:]])
         for tile, values in zip(tiles, placed):
             at = block(tile, b)
             total[at] = total[at] + values
@@ -213,12 +232,12 @@
         place = lax.rem(lax.broadcasted_iota(jnp.int32, outgoing.shape, 0), per_peer)
         for h in range(parts):
             outgoing = jnp.where(place == cap // PART + h, sums[h : h + 1], outgoing)
-    payload_ref[...] = outgoing.astype(BF)
+    payload_ref[...] = turn(outgoing.astype(BF))
 
 
 def aggregate_kernel(arrived_ref, own_ref, slots_ref, vectors_ref, aggregate_ref, copies_ref):
     k, v_count = own_ref.shape
-    returned = from_tall(arrived_ref[...].astype(F32).T.astype(BF))
+    returned = from_tall(turn(arrived_ref[...]).astype(F32).T.astype(BF))
     summed = own_ref[...] + scatter(returned, slots_ref[...], v_count)
     aggregate = (summed / vectors_ref[:1, :]).astype(BF)
     aggregate_ref[...] = aggregate
@@ -232,8 +251,10 @@
     hidden_ref, grad_pre_ref, rows_ref,
 ):
     k, v_count = spread_ref.shape
-    channels = aggregate_ref.shape[0]
-    pre = self_ref[...] + matmul(w_in_ref[channels:, :], aggregate_ref[...], 0, 0)
+    n_dp = aggregate_ref.shape[0]
+    channels = n_dp * k
+    aggregate = jnp.concatenate([aggregate_ref[r ^ far(n_dp)] for r in range(n_dp)], 0)
+    pre = self_ref[...] + matmul(w_in_ref[channels:, :], aggregate, 0, 0)
     sigmoid = 1.0 / (1.0 + jnp.exp(-pre))
     hidden_ref[...] = (pre * sigmoid).astype(BF)
     grad_pre = (gh_ref[...] * (sigmoid * (1.0 + pre * (1.0 - sigmoid)))).astype(BF)
@@ -270,14 +291,14 @@
     for h in range(halves):
         chosen = hot((rows // per_peer == peer) & (lax.rem(rows, per_peer) == parts + h))
         payload = payload + matmul(chosen, grads[:, h * LANES : h * LANES + LANES])
-    payload_ref[...] = payload.astype(BF)
+    payload_ref[...] = turn(payload.astype(BF))
 
 
 def back_kernel(cap, per_peer, arrived_ref, own_ref, slots_ref, copies_ref):
     k, v_count = own_ref.shape
     n_dp = copies_ref.shape[0]
     share = v_count // n_dp
-    arrived = arrived_ref[...]
+    arrived = turn(arrived_ref[...])
     tall = matmul(arrived, part_rows(arrived.shape[0], per_peer, cap // PART), 0, 0)
     returned = from_tall(tall.astype(BF))
     summed = (own_ref[...] + scatter(returned, slots_ref[...], v_count)).astype(BF)
@@ -292,8 +313,8 @@
     grads = matmul(chosen, arrived).astype(BF)
     for r in range(n_dp):
         first = r * share // LANES * LANES
-        copies_ref[r, :k] = summed[:, first : first + LANES]
-        copies_ref[r, k:] = grads
+        copies_ref[r ^ far(n_dp), :k] = summed[:, first : first + LANES]
+        copies_ref[r ^ far(n_dp), k:] = grads
 
 
 def last_kernel(
@@ -305,7 +326,7 @@
     n_dp = arrived_ref.shape[0]
     k = channels // n_dp
     half = pl.multiple_of(lax.rem(replica_ref[0], LANES // share) * share, share)
-    columns = jnp.concatenate([arrived_ref[r, :k] for r in range(n_dp)], 0)
+    columns = jnp.concatenate([arrived_ref[r ^ far(n_dp), :k] for r in range(n_dp)], 0)
     rows_ref[...] = columns.astype(F32).T
     grad_features_ref[...] = (rows_ref[pl.ds(half, share), :] + grad_self_ref[...]).astype(BF)
     halves = channels // LANES
@@ -314,10 +335,10 @@
         first = k + h * 3 * k
         for r in range(n_dp):
             rows = slice(r * k, r * k + k)
-            grad_w_in_ref[rows, lanes] = arrived_ref[r, first : first + k].astype(F32)
+            grad_w_in_ref[rows, lanes] = arrived_ref[r ^ far(n_dp), first : first + k].astype(F32)
             second = slice(channels + r * k, channels + r * k + k)
-            grad_w_in_ref[second, lanes] = arrived_ref[r, first + k : first + 2 * k].astype(F32)
-            grad_w_out_ref[rows, lanes] = arrived_ref[r, first + 2 * k : first + 3 * k].astype(F32)
+            grad_w_in_ref[second, lanes] = arrived_ref[r ^ far(n_dp), first + k : first + 2 * k].astype(F32)
+            grad_w_out_ref[rows, lanes] = arrived_ref[r ^ far(n_dp), first + 2 * k : first + 3 * k].astype(F32)
         biases = arrived_ref[0, k + halves * 3 * k :].astype(F32)
         grad_b_in_ref[:, lanes] = biases[h : h + 1]
         grad_b_out_ref[:, lanes] = biases[halves + h : halves + h + 1]
@@ -343,7 +364,12 @@
 
 
 def swap(values, axis):
-    return lax.all_to_all(values, axis, split_axis=0, concat_axis=0, tiled=True)
+    size = lax.axis_size(axis)
+    if axis == "dom":
+        group = [(i + size // 2) % size for i in range(size)]
+    else:
+        group = [i ^ far(size) for i in range(size)]
+    return lax.all_to_all(values, axis, split_axis=0, concat_axis=0, axis_index_groups=[group], tiled=True)
 
 
 def on_device(
@@ -374,10 +400,14 @@
     parts = cap // PART
     more = parts + channels // LANES
 
-    edges = edge_slots[0, 0].reshape(2 * n_tiles, tile_rows)
-    edges = jnp.concatenate([edges, jnp.pad(tile_blocks[0, 0], ((0, 0), (0, tile_rows - 2)))], 0)
-    edges = swap(jnp.broadcast_to(edges[None], (n_dp, *edges.shape)), "dp")
-    blocks = edges[:, 2 * n_tiles :, :2].reshape(n_dp, 2 * n_tiles)
+    (edges,) = call(
+        pack_kernel,
+        [((n_dp, 2 * n_tiles, tile_rows), jnp.int32)],
+        [edge_slots[0, 0], tile_blocks[0, 0]],
+        name="pack",
+    )
+    edges = swap(edges, "dp")
+    blocks = edges[:, n_tiles:, :2].reshape(n_dp, 2 * n_tiles)
 
     table, slots_row, payload = call(
         first_kernel,
@@ -404,7 +434,7 @@
             [arrived, owned, edges, blocks, vectors],
             smem=(3,),
             scratch=[
-                pltpu.VMEM((blocks_count, k, LANES), BF),
+                pltpu.VMEM((blocks_count, k, LANES), F32),
                 pltpu.VMEM((blocks_count, k, LANES), F32),
             ],
             name="edges_back" if transpose else "edges",
@@ -418,7 +448,7 @@
         [arrived, own, slots_row, vectors],
         name="aggregate",
     )
-    aggregate_all = swap(copies, "dp").reshape(channels, v_count)
+    aggregate_all = swap(copies, "dp")
 
     output, grad_self, spread, payload = call(
         lambda *refs: dense_kernel(scale, cap, *refs),

time: 197 us -> 181 us (0.919)
  waiting for transfers between devices: 25.5 us -> 1.31 us
  starting transfers between devices: 39 us -> 46.8 us
    all_to_all x2, waiting for transfers between devices: 25.5 us -> 1.31 us  [swap(): lax.all_to_all(values, axis, split_axis=0, concat_axis=0, axis_index_grou...]
    all_to_all x2, starting transfers between devices: 39 us -> 46.8 us  [swap(): lax.all_to_all(values, axis, split_axis=0, concat_axis=0, axis_index_grou...]
    pallas_call x8 -> x9, Pallas kernels: 13.4 us -> 12.5 us  [call(): pl.pallas_call(kernel, out_shape=shapes, in_specs=in_specs, out_specs=[pl...]
  transfers between devices with their start and end apart: 2 -> 2, of which waited for: 2 -> 1; matrix products, arithmetic and copies ran while one was open for 0% -> 0% of each run, Pallas kernels for 1% -> 1%
where the time goes in v5:
time: 181 us
  blocking collectives  115 us (64%)
  starting transfers between devices  46.8 us (26%)
  Pallas kernels  12.5 us (7%)
  local copies, waits for them, and re-layouts  4.46 us (2%)
    all_to_all x5, blocking collectives, swap(): lax.all_to_all(values, axis, split_axis=0, concat_axis=0, axis_index_grou...  115 us
    all_to_all x2, starting transfers between devices, swap(): lax.all_to_all(values, axis, split_axis=0, concat_axis=0, axis_index_grou...  46.8 us
    pallas_call x9, Pallas kernels, call(): pl.pallas_call(kernel, out_shape=shapes, in_specs=in_specs, out_specs=[pl...  12.5 us
  transfers between devices with their start and end apart: 2, of which 1 were waited for; matrix products, arithmetic and copies ran while one was open for 0% of the time, Pallas kernels for 1%

profile of v5, /device:TPU:1, one launch (start us, length us, event | category | flops | bytes accessed | tf_op | source)
XLA Modules:
  0.0 180.9 jit_solution(4661452287955673972)
XLA Ops:
  0.6 0.0 copy-start.6
  0.6 0.8 copy.20.blocks_ref
  1.4 0.0 copy-done.6
  1.4 0.0 copy-start.11
  1.4 0.0 copy-start.5
  1.4 0.7 pack.1
  2.1 0.0 copy-start.4
  2.1 9.7 %all-to-all-start.1 = ((s32[16,16,128]{2,1,0:T(8,128)}), s32[16,16,128]{2,1,0:T(8,128)S(1)}, u32[]{:S(2)}, u32[]{:S(2)}) async-start(s32[16,16,128]{2,1,0:T(8,128)} %pack.1), calls=%async_computation.1 | async-start | bytes 262144 | tf_op jit(solution)/shard_map/all_to_all | solution.py:372
  11.8 0.0 copy-done.11
  11.8 0.1 copy.19
  11.9 0.0 copy-start.10
  11.9 0.7 copy-done.10
  12.6 0.0 copy-start
  12.6 1.0 copy-done
  13.6 0.0 copy-start.1
  13.6 1.4 first.1
  15.0 0.0 all-to-all-done.1.refs_2_
  15.0 0.0 copy-start.9
  15.0 37.1 %all-to-all-start = ((bf16[64,2,128]{2,1,0:T(2,128)(2,1)}), bf16[64,2,128]{2,1,0:T(2,128)(2,1)S(1)}, u32[]{:S(2)}, u32[]{:S(2)}) async-start(bf16[64,2,128]{2,1,0:T(2,128)(2,1)} %bitcast.2), calls=%async_computation | async-start | bytes 65536 | tf_op jit(solution)/shard_map/all_to_all | solution.py:372
  52.1 0.0 copy-start.7
  52.2 0.0 copy-start.8
  52.2 0.0 copy-done.5
  52.2 0.0 copy-done.4
  52.2 0.0 copy-done.1
  52.2 0.0 copy-done.9
  52.2 0.6 copy-done.7
  52.8 0.0 copy-done.8
  52.8 0.0 copy-start.2
  52.8 1.0 copy-done.2
  53.9 0.5 inputs.1
  54.4 0.1 copy.21
  54.5 0.1 copy.22.refs_3_
  54.6 1.3 all-to-all-done
  55.9 2.5 %edges.1 = (bf16[128,128]{1,0:T(8,128)(2,1)S(1)}, f32[16,1024]{1,0:T(8,128)S(1)}) custom-call(bf16[128,128]{1,0:T(8,128)(2,1)S(1)} %bitcast.22, bf16[16,1024]{1,0:T(8,128)(2,1)S(1)} %get-tuple-element.29.refs_1_.refs_6_, s32[16,16,128]{2,1,0:T(8,128)S(1)} %all-to-all-done.1.refs_2_, s32[16,16]{1,0:T(8,128)S(1)} %copy.22.refs_3_, ...), custom_call_target="tpu_custom_call" | custom-call | bytes 328704 | tf_op jit(solution)/shard_map/edges/pallas_call | solution.py:354
  58.5 27.4 %all_to_all.59 = bf16[64,2,128]{2,1,0:T(2,128)(2,1)S(1)} all-to-all(bf16[64,2,128]{2,1,0:T(2,128)(2,1)S(1)} %bitcast.25), channel_id=1, replica_groups={{512,528,544,560,576,592,608,624,640,656,672,688,704,720,736,752,768,78..., dimensions={0} | all-to-all | bytes 65536 | tf_op jit(solution)/shard_map/all_to_all | solution.py:372
  85.8 0.7 aggregate.1
  86.6 0.0 copy-start.3
  86.6 14.5 %all_to_all.60.refs_0_ = bf16[16,16,1024]{2,1,0:T(8,128)(2,1)S(1)} all-to-all(bf16[16,16,1024]{2,1,0:T(8,128)(2,1)S(1)} %get-tuple-element.34), channel_id=1, replica_groups={{10,11,8,9,14,15,12,13,2,3,0,1,6,7,4,5},{26,27,24,25,30,31,28,29,18,19,..., dimensions={0} | all-to-all | bytes 1048576 | tf_op jit(solution)/shard_map/all_to_all | solution.py:372
  101.1 0.0 copy-done.3
  101.1 1.9 %dense.1 = (bf16[64,256]{1,0:T(8,128)(2,1)S(1)}, f32[64,256]{1,0:T(8,128)S(1)}, bf16[16,1024]{1,0:T(8,128)(2,1)S(1)}, bf16[256,128]{1,0:T(8,128)(2,1)S(1)}) custom-call(bf16[16,16,1024]{2,1,0:T(8,128)(2,1)S(1)} %all_to_all.60.refs_0_, f32[256,1024]{1,0:T(8,128)S(1)} %get-tuple-element.35.refs_1_, f32[256,1024]{1,0:T(8,128)S(1)} %get-tuple-element.36.refs_2_, ...), custom_call_target="tpu_custom_call" | custom-call | bytes 3837956 | tf_op jit(solution)/shard_map/dense/pallas_call | solution.py:354
  103.0 28.9 %all_to_all.61 = bf16[64,4,128]{2,1,0:T(4,128)(2,1)S(1)} all-to-all(bf16[64,4,128]{2,1,0:T(4,128)(2,1)S(1)} %bitcast.23), channel_id=1, replica_groups={{512,528,544,560,576,592,608,624,640,656,672,688,704,720,736,752,768,78..., dimensions={0} | all-to-all | bytes 131072 | tf_op jit(solution)/shard_map/all_to_all | solution.py:372
  131.9 2.9 %edges_back.1 = (bf16[256,128]{1,0:T(8,128)(2,1)S(1)}, f32[16,1024]{1,0:T(8,128)S(1)}) custom-call(bf16[256,128]{1,0:T(8,128)(2,1)S(1)} %bitcast.19, bf16[16,1024]{1,0:T(8,128)(2,1)S(1)} %get-tuple-element.39.refs_1_, s32[16,16,128]{2,1,0:T(8,128)S(1)} %all-to-all-done.1.refs_2_, s32[16,16]{1,0:T(8,128)S(1)} %copy.22.refs_3_, ...), custom_call_target="tpu_custom_call" | custom-call | bytes 394240 | tf_op jit(solution)/shard_map/edges_back/pallas_call | solution.py:354
  134.8 30.2 %all_to_all.62 = bf16[64,4,128]{2,1,0:T(4,128)(2,1)S(1)} all-to-all(bf16[64,4,128]{2,1,0:T(4,128)(2,1)S(1)} %bitcast.24), channel_id=1, replica_groups={{512,528,544,560,576,592,608,624,640,656,672,688,704,720,736,752,768,78..., dimensions={0} | all-to-all | bytes 131072 | tf_op jit(solution)/shard_map/all_to_all | solution.py:372
  165.0 0.9 back.1
  165.9 14.0 %all_to_all.63.arrived_ref = bf16[16,128,128]{2,1,0:T(8,128)(2,1)S(1)} all-to-all(bf16[16,128,128]{2,1,0:T(8,128)(2,1)S(1)} %back.1), channel_id=1, replica_groups={{10,11,8,9,14,15,12,13,2,3,0,1,6,7,4,5},{26,27,24,25,30,31,28,29,18,19,..., dimensions={0} | all-to-all | bytes 1048576 | tf_op jit(solution)/shard_map/all_to_all | solution.py:372
  179.9 1.0 last.1
  (1 shorter events, 0.0 us)
Async XLA Ops:
  0.6 0.8 copy-start.6
  1.4 10.4 %copy-start.11 = (s32[1,64,16]{1,2,0:T(8,128)S(1)}, s32[1,64,16]{1,2,0:T(8,128)}, u32[]{:S(2)}) copy-start(s32[1,64,16]{1,2,0:T(8,128)} %param.13) | copy-start | bytes 12292
  1.4 50.8 %copy-start.5 = (bf16[256,256]{1,0:T(8,128)(2,1)S(1)}, bf16[256,256]{1,0:T(8,128)(2,1)}, u32[]{:S(2)}) copy-start(bf16[256,256]{1,0:T(8,128)(2,1)} %refs_9_.1) | copy-start | bytes 393220
  2.1 50.0 %copy-start.4 = (bf16[512,256]{1,0:T(8,128)(2,1)S(1)}, bf16[512,256]{1,0:T(8,128)(2,1)}, u32[]{:S(2)}) copy-start(bf16[512,256]{1,0:T(8,128)(2,1)} %refs_3_.1) | copy-start | bytes 786436
  2.1 12.9 %all-to-all-start.1 = ((s32[16,16,128]{2,1,0:T(8,128)}), s32[16,16,128]{2,1,0:T(8,128)S(1)}, u32[]{:S(2)}, u32[]{:S(2)}) async-start(s32[16,16,128]{2,1,0:T(8,128)} %pack.1), calls=%async_computation.1 | async-start | bytes 262144 | tf_op jit(solution)/shard_map/all_to_all | solution.py:372
  11.9 0.7 copy-start.10
  12.6 1.0 copy-start
  13.6 38.6 %copy-start.1 = (bf16[1024,256]{1,0:T(8,128)(2,1)S(1)}, bf16[1024,256]{1,0:T(8,128)(2,1)}, u32[]{:S(2)}) copy-start(bf16[1024,256]{1,0:T(8,128)(2,1)} %features_ref.3) | copy-start | bytes 1572868
  15.0 37.2 %copy-start.9 = (f32[256]{0:T(256)S(1)}, f32[256]{0:T(256)}, u32[]{:S(2)}) copy-start(f32[256]{0:T(256)} %param.20) | copy-start | bytes 3076
  15.0 40.9 %all-to-all-start = ((bf16[64,2,128]{2,1,0:T(2,128)(2,1)}), bf16[64,2,128]{2,1,0:T(2,128)(2,1)S(1)}, u32[]{:S(2)}, u32[]{:S(2)}) async-start(bf16[64,2,128]{2,1,0:T(2,128)(2,1)} %bitcast.2), calls=%async_computation | async-start | bytes 65536 | tf_op jit(solution)/shard_map/all_to_all | solution.py:372
  52.1 0.7 copy-start.7
  52.2 0.7 copy-start.8
  52.8 1.0 copy-start.2
  86.6 14.5 %copy-start.3 = (bf16[1024,256]{1,0:T(8,128)(2,1)S(1)}, bf16[1024,256]{1,0:T(8,128)(2,1)}, u32[]{:S(2)}) copy-start(bf16[1024,256]{1,0:T(8,128)(2,1)} %refs_8_.1) | copy-start | bytes 1572868

commit v6 on v5

--- a/solution.py
+++ b/solution.py
@@ -13,15 +13,15 @@
 PART = 8
 GROUPS = 16
 SHIFT = 16
+STRIDE = 33
 
 
 def far(size):
     return size // 2 + size // 8
 
 
-def turn(rows):
-    half = rows.shape[0] // 2
-    return jnp.concatenate([rows[half:], rows[:half]], 0)
+def peer_at(position, size):
+    return (size // 2 + STRIDE * position) % size
 
 
 def matmul(a, b, ca=1, cb=0):
@@ -62,7 +62,8 @@
 def peer_rows(n_rows, per_peer, n_slots, cap):
     rows = lax.broadcasted_iota(jnp.int32, (n_rows, 1), 0)
     part = lax.rem(rows, per_peer)
-    used = jnp.where(part < cap // PART, rows // per_peer * (cap // PART) + part, -1)
+    peer = peer_at(rows // per_peer, n_rows // per_peer)
+    used = jnp.where(part < cap // PART, peer * (cap // PART) + part, -1)
     slots = lax.broadcasted_iota(jnp.int32, (1, n_slots), 1) // PART
     return hot(slots == used)
 
@@ -116,7 +117,7 @@
     slots = lax.broadcasted_iota(jnp.int32, (1, n_slots), 1)
     within = lax.rem(slots, width)
     place = lax.rem(within, parts) * PART + slots // width
-    chosen = hot(lax.broadcasted_iota(jnp.int32, (n_peers, 1), 0) == within // parts)
+    chosen = hot(lax.broadcasted_iota(jnp.int32, (n_peers, 1), 0) == peer_at(within // parts, n_peers))
     base = 32
     high = send_rows // base
     low = send_rows - high * base
@@ -153,7 +154,7 @@
     table_ref[...] = table
     slots = slots_of(send_rows_ref[...], send_counts_ref[...], v_count)
     slots_ref[...] = slots
-    payload_ref[...] = turn(to_rows(pick(table, slots)))
+    payload_ref[...] = to_rows(pick(table, slots))
 
 
 def inputs_kernel(
@@ -176,7 +177,7 @@
     k, v_count = owned_ref.shape
     own_blocks = v_count // LANES
     all_blocks = table.shape[0]
-    arrived = turn(arrived_ref[...])
+    arrived = arrived_ref[...]
     mirrors = from_peers(arrived, per_peer, cap)
     owned = owned_ref[...].astype(F32)
     for b in range(own_blocks):
@@ -232,12 +233,12 @@
         place = lax.rem(lax.broadcasted_iota(jnp.int32, outgoing.shape, 0), per_peer)
         for h in range(parts):
             outgoing = jnp.where(place == cap // PART + h, sums[h : h + 1], outgoing)
-    payload_ref[...] = turn(outgoing.astype(BF))
+    payload_ref[...] = outgoing.astype(BF)
 
 
 def aggregate_kernel(arrived_ref, own_ref, slots_ref, vectors_ref, aggregate_ref, copies_ref):
     k, v_count = own_ref.shape
-    returned = from_tall(turn(arrived_ref[...]).astype(F32).T.astype(BF))
+    returned = from_tall(arrived_ref[...].astype(F32).T.astype(BF))
     summed = own_ref[...] + scatter(returned, slots_ref[...], v_count)
     aggregate = (summed / vectors_ref[:1, :]).astype(BF)
     aggregate_ref[...] = aggregate
@@ -289,16 +290,16 @@
     source = lax.broadcasted_iota(jnp.int32, (n_rows, grads.shape[0]), 1)
     peer = jnp.where(source == 4 * k, 3 * k + 1, jnp.where(source > 3 * k, -1, source))
     for h in range(halves):
-        chosen = hot((rows // per_peer == peer) & (lax.rem(rows, per_peer) == parts + h))
+        chosen = hot((peer_at(rows // per_peer, n_rows // per_peer) == peer) & (lax.rem(rows, per_peer) == parts + h))
         payload = payload + matmul(chosen, grads[:, h * LANES : h * LANES + LANES])
-    payload_ref[...] = turn(payload.astype(BF))
+    payload_ref[...] = payload.astype(BF)
 
 
 def back_kernel(cap, per_peer, arrived_ref, own_ref, slots_ref, copies_ref):
     k, v_count = own_ref.shape
     n_dp = copies_ref.shape[0]
     share = v_count // n_dp
-    arrived = turn(arrived_ref[...])
+    arrived = arrived_ref[...]
     tall = matmul(arrived, part_rows(arrived.shape[0], per_peer, cap // PART), 0, 0)
     returned = from_tall(tall.astype(BF))
     summed = (own_ref[...] + scatter(returned, slots_ref[...], v_count)).astype(BF)
@@ -307,7 +308,8 @@
     halves = per_peer - parts
     to = lax.broadcasted_iota(jnp.int32, (n_rows, arrived.shape[0]), 0)
     source = lax.broadcasted_iota(jnp.int32, (n_rows, arrived.shape[0]), 1)
-    peer, half = source // per_peer, lax.rem(source, per_peer) - parts
+    peer = peer_at(source // per_peer, arrived.shape[0] // per_peer)
+    half = lax.rem(source, per_peer) - parts
     place = jnp.where(peer < 3 * k, half * (3 * k) + peer, halves * 3 * k + (peer - 3 * k) * halves + half)
     chosen = hot((place == to) & (half >= 0))
     grads = matmul(chosen, arrived).astype(BF)
@@ -366,7 +368,7 @@
 def swap(values, axis):
     size = lax.axis_size(axis)
     if axis == "dom":
-        group = [(i + size // 2) % size for i in range(size)]
+        group = [peer_at(i, size) for i in range(size)]
     else:
         group = [i ^ far(size) for i in range(size)]
     return lax.all_to_all(values, axis, split_axis=0, concat_axis=0, axis_index_groups=[group], tiled=True)

time: 181 us -> 180 us (level)
  blocking collectives: 115 us -> 113 us
    all_to_all x5, blocking collectives: 115 us -> 113 us  [swap(): lax.all_to_all(values, axis, split_axis=0, concat_axis=0, axis_index_grou...]
where the time goes in v6:
time: 180 us; the launch traced here: 179 us
  blocking collectives  113 us (63%)
  starting transfers between devices  46.7 us (26%)
  Pallas kernels  12.6 us (7%)
  local copies, waits for them, and re-layouts  4.46 us (2%)
    all_to_all x5, blocking collectives, swap(): lax.all_to_all(values, axis, split_axis=0, concat_axis=0, axis_index_grou...  113 us
    all_to_all x2, starting transfers between devices, swap(): lax.all_to_all(values, axis, split_axis=0, concat_axis=0, axis_index_grou...  46.7 us
    pallas_call x9, Pallas kernels, call(): pl.pallas_call(kernel, out_shape=shapes, in_specs=in_specs, out_specs=[pl...  12.6 us
  transfers between devices with their start and end apart: 2, of which 1 were waited for; matrix products, arithmetic and copies ran while one was open for 0% of the time, Pallas kernels for 1%

profile of v6, /device:TPU:1, one launch (start us, length us, event | category | flops | bytes accessed | tf_op | source)
XLA Modules:
  0.0 178.9 jit_solution(10337281116923894509)
XLA Ops:
  0.6 0.0 copy-start.6
  0.6 0.8 copy.20.blocks_ref
  1.4 0.0 copy-done.6
  1.4 0.0 copy-start.11
  1.4 0.0 copy-start.5
  1.4 0.7 pack.1
  2.1 0.0 copy-start.4
  2.1 9.7 %all-to-all-start.1 = ((s32[16,16,128]{2,1,0:T(8,128)}), s32[16,16,128]{2,1,0:T(8,128)S(1)}, u32[]{:S(2)}, u32[]{:S(2)}) async-start(s32[16,16,128]{2,1,0:T(8,128)} %pack.1), calls=%async_computation.1 | async-start | bytes 262144 | tf_op jit(solution)/shard_map/all_to_all | solution.py:374
  11.8 0.0 copy-done.11
  11.8 0.1 copy.19
  11.9 0.0 copy-start.10
  11.9 0.7 copy-done.10
  12.6 0.0 copy-start
  12.6 1.0 copy-done
  13.6 0.0 copy-start.1
  13.6 1.4 first.1
  15.0 0.0 all-to-all-done.1.refs_2_
  15.0 0.0 copy-start.9
  15.0 37.0 %all-to-all-start = ((bf16[64,2,128]{2,1,0:T(2,128)(2,1)}), bf16[64,2,128]{2,1,0:T(2,128)(2,1)S(1)}, u32[]{:S(2)}, u32[]{:S(2)}) async-start(bf16[64,2,128]{2,1,0:T(2,128)(2,1)} %bitcast.2), calls=%async_computation | async-start | bytes 65536 | tf_op jit(solution)/shard_map/all_to_all | solution.py:374
  52.0 0.0 copy-start.7
  52.0 0.0 copy-start.8
  52.0 0.0 copy-done.5
  52.0 0.0 copy-done.4
  52.1 0.0 copy-done.1
  52.1 0.0 copy-done.9
  52.1 0.6 copy-done.7
  52.7 0.0 copy-done.8
  52.7 0.0 copy-start.2
  52.7 1.0 copy-done.2
  53.8 0.5 inputs.1
  54.3 0.1 copy.21
  54.4 0.1 copy.22.refs_3_
  54.5 1.4 all-to-all-done
  55.8 2.5 %edges.1 = (bf16[128,128]{1,0:T(8,128)(2,1)S(1)}, f32[16,1024]{1,0:T(8,128)S(1)}) custom-call(bf16[128,128]{1,0:T(8,128)(2,1)S(1)} %bitcast.22, bf16[16,1024]{1,0:T(8,128)(2,1)S(1)} %get-tuple-element.29.refs_1_.refs_6_, s32[16,16,128]{2,1,0:T(8,128)S(1)} %all-to-all-done.1.refs_2_, s32[16,16]{1,0:T(8,128)S(1)} %copy.22.refs_3_, ...), custom_call_target="tpu_custom_call" | custom-call | bytes 328704 | tf_op jit(solution)/shard_map/edges/pallas_call | solution.py:356
  58.4 26.4 %all_to_all.59 = bf16[64,2,128]{2,1,0:T(2,128)(2,1)S(1)} all-to-all(bf16[64,2,128]{2,1,0:T(2,128)(2,1)S(1)} %bitcast.25), channel_id=1, replica_groups={{512,16,544,48,576,80,608,112,640,144,672,176,704,208,736,240,768,272,8..., dimensions={0} | all-to-all | bytes 65536 | tf_op jit(solution)/shard_map/all_to_all | solution.py:374
  84.7 0.7 aggregate.1
  85.5 0.0 copy-start.3
  85.5 14.5 %all_to_all.60.refs_0_ = bf16[16,16,1024]{2,1,0:T(8,128)(2,1)S(1)} all-to-all(bf16[16,16,1024]{2,1,0:T(8,128)(2,1)S(1)} %get-tuple-element.34), channel_id=1, replica_groups={{10,11,8,9,14,15,12,13,2,3,0,1,6,7,4,5},{26,27,24,25,30,31,28,29,18,19,..., dimensions={0} | all-to-all | bytes 1048576 | tf_op jit(solution)/shard_map/all_to_all | solution.py:374
  100.0 0.0 copy-done.3
  100.0 1.9 %dense.1 = (bf16[64,256]{1,0:T(8,128)(2,1)S(1)}, f32[64,256]{1,0:T(8,128)S(1)}, bf16[16,1024]{1,0:T(8,128)(2,1)S(1)}, bf16[256,128]{1,0:T(8,128)(2,1)S(1)}) custom-call(bf16[16,16,1024]{2,1,0:T(8,128)(2,1)S(1)} %all_to_all.60.refs_0_, f32[256,1024]{1,0:T(8,128)S(1)} %get-tuple-element.35.refs_1_, f32[256,1024]{1,0:T(8,128)S(1)} %get-tuple-element.36.refs_2_, ...), custom_call_target="tpu_custom_call" | custom-call | bytes 3837956 | tf_op jit(solution)/shard_map/dense/pallas_call | solution.py:356
  101.9 29.0 %all_to_all.61 = bf16[64,4,128]{2,1,0:T(4,128)(2,1)S(1)} all-to-all(bf16[64,4,128]{2,1,0:T(4,128)(2,1)S(1)} %bitcast.23), channel_id=1, replica_groups={{512,16,544,48,576,80,608,112,640,144,672,176,704,208,736,240,768,272,8..., dimensions={0} | all-to-all | bytes 131072 | tf_op jit(solution)/shard_map/all_to_all | solution.py:374
  130.9 3.0 %edges_back.1 = (bf16[256,128]{1,0:T(8,128)(2,1)S(1)}, f32[16,1024]{1,0:T(8,128)S(1)}) custom-call(bf16[256,128]{1,0:T(8,128)(2,1)S(1)} %bitcast.19, bf16[16,1024]{1,0:T(8,128)(2,1)S(1)} %get-tuple-element.39.refs_1_, s32[16,16,128]{2,1,0:T(8,128)S(1)} %all-to-all-done.1.refs_2_, s32[16,16]{1,0:T(8,128)S(1)} %copy.22.refs_3_, ...), custom_call_target="tpu_custom_call" | custom-call | bytes 394240 | tf_op jit(solution)/shard_map/edges_back/pallas_call | solution.py:356
  133.9 29.2 %all_to_all.62 = bf16[64,4,128]{2,1,0:T(4,128)(2,1)S(1)} all-to-all(bf16[64,4,128]{2,1,0:T(4,128)(2,1)S(1)} %bitcast.24), channel_id=1, replica_groups={{512,16,544,48,576,80,608,112,640,144,672,176,704,208,736,240,768,272,8..., dimensions={0} | all-to-all | bytes 131072 | tf_op jit(solution)/shard_map/all_to_all | solution.py:374
  163.1 0.9 back.1
  164.0 14.0 %all_to_all.63.arrived_ref = bf16[16,128,128]{2,1,0:T(8,128)(2,1)S(1)} all-to-all(bf16[16,128,128]{2,1,0:T(8,128)(2,1)S(1)} %back.1), channel_id=1, replica_groups={{10,11,8,9,14,15,12,13,2,3,0,1,6,7,4,5},{26,27,24,25,30,31,28,29,18,19,..., dimensions={0} | all-to-all | bytes 1048576 | tf_op jit(solution)/shard_map/all_to_all | solution.py:374
  178.0 1.0 last.1
  (1 shorter events, 0.0 us)
Async XLA Ops:
  0.6 0.8 copy-start.6
  1.4 10.4 %copy-start.11 = (s32[1,64,16]{1,2,0:T(8,128)S(1)}, s32[1,64,16]{1,2,0:T(8,128)}, u32[]{:S(2)}) copy-start(s32[1,64,16]{1,2,0:T(8,128)} %param.13) | copy-start | bytes 12292
  1.4 50.6 %copy-start.5 = (bf16[256,256]{1,0:T(8,128)(2,1)S(1)}, bf16[256,256]{1,0:T(8,128)(2,1)}, u32[]{:S(2)}) copy-start(bf16[256,256]{1,0:T(8,128)(2,1)} %refs_9_.1) | copy-start | bytes 393220
  2.1 49.9 %copy-start.4 = (bf16[512,256]{1,0:T(8,128)(2,1)S(1)}, bf16[512,256]{1,0:T(8,128)(2,1)}, u32[]{:S(2)}) copy-start(bf16[512,256]{1,0:T(8,128)(2,1)} %refs_3_.1) | copy-start | bytes 786436
  2.1 12.9 %all-to-all-start.1 = ((s32[16,16,128]{2,1,0:T(8,128)}), s32[16,16,128]{2,1,0:T(8,128)S(1)}, u32[]{:S(2)}, u32[]{:S(2)}) async-start(s32[16,16,128]{2,1,0:T(8,128)} %pack.1), calls=%async_computation.1 | async-start | bytes 262144 | tf_op jit(solution)/shard_map/all_to_all | solution.py:374
  11.9 0.7 copy-start.10
  12.6 1.0 copy-start
  13.6 38.4 %copy-start.1 = (bf16[1024,256]{1,0:T(8,128)(2,1)S(1)}, bf16[1024,256]{1,0:T(8,128)(2,1)}, u32[]{:S(2)}) copy-start(bf16[1024,256]{1,0:T(8,128)(2,1)} %features_ref.3) | copy-start | bytes 1572868
  15.0 37.0 %copy-start.9 = (f32[256]{0:T(256)S(1)}, f32[256]{0:T(256)}, u32[]{:S(2)}) copy-start(f32[256]{0:T(256)} %param.20) | copy-start | bytes 3076
  15.0 40.8 %all-to-all-start = ((bf16[64,2,128]{2,1,0:T(2,128)(2,1)}), bf16[64,2,128]{2,1,0:T(2,128)(2,1)S(1)}, u32[]{:S(2)}, u32[]{:S(2)}) async-start(bf16[64,2,128]{2,1,0:T(2,128)(2,1)} %bitcast.2), calls=%async_computation | async-start | bytes 65536 | tf_op jit(solution)/shard_map/all_to_all | solution.py:374
  52.0 0.7 copy-start.7
  52.0 0.7 copy-start.8
  52.7 1.0 copy-start.2
  85.5 14.5 %copy-start.3 = (bf16[1024,256]{1,0:T(8,128)(2,1)S(1)}, bf16[1024,256]{1,0:T(8,128)(2,1)}, u32[]{:S(2)}) copy-start(bf16[1024,256]{1,0:T(8,128)(2,1)} %refs_8_.1) | copy-start | bytes 1572868

commit v7 on v6

--- a/solution.py
+++ b/solution.py
@@ -18,6 +18,14 @@
 
 def far(size):
     return size // 2 + size // 8
+
+
+def replica_at(position, size):
+    return (far(size) + (size // 2 + 1) * position) % size
+
+
+def place_of(replica, size):
+    return ((size // 2 + 1) * (replica - far(size))) % size
 
 
 def peer_at(position, size):
@@ -254,7 +262,7 @@
     k, v_count = spread_ref.shape
     n_dp = aggregate_ref.shape[0]
     channels = n_dp * k
-    aggregate = jnp.concatenate([aggregate_ref[r ^ far(n_dp)] for r in range(n_dp)], 0)
+    aggregate = jnp.concatenate([aggregate_ref[place_of(r, n_dp)] for r in range(n_dp)], 0)
     pre = self_ref[...] + matmul(w_in_ref[channels:, :], aggregate, 0, 0)
     sigmoid = 1.0 / (1.0 + jnp.exp(-pre))
     hidden_ref[...] = (pre * sigmoid).astype(BF)
@@ -315,8 +323,8 @@
     grads = matmul(chosen, arrived).astype(BF)
     for r in range(n_dp):
         first = r * share // LANES * LANES
-        copies_ref[r ^ far(n_dp), :k] = summed[:, first : first + LANES]
-        copies_ref[r ^ far(n_dp), k:] = grads
+        copies_ref[place_of(r, n_dp), :k] = summed[:, first : first + LANES]
+        copies_ref[place_of(r, n_dp), k:] = grads
 
 
 def last_kernel(
@@ -328,7 +336,7 @@
     n_dp = arrived_ref.shape[0]
     k = channels // n_dp
     half = pl.multiple_of(lax.rem(replica_ref[0], LANES // share) * share, share)
-    columns = jnp.concatenate([arrived_ref[r ^ far(n_dp), :k] for r in range(n_dp)], 0)
+    columns = jnp.concatenate([arrived_ref[place_of(r, n_dp), :k] for r in range(n_dp)], 0)
     rows_ref[...] = columns.astype(F32).T
     grad_features_ref[...] = (rows_ref[pl.ds(half, share), :] + grad_self_ref[...]).astype(BF)
     halves = channels // LANES
@@ -337,10 +345,10 @@
         first = k + h * 3 * k
         for r in range(n_dp):
             rows = slice(r * k, r * k + k)
-            grad_w_in_ref[rows, lanes] = arrived_ref[r ^ far(n_dp), first : first + k].astype(F32)
+            grad_w_in_ref[rows, lanes] = arrived_ref[place_of(r, n_dp), first : first + k].astype(F32)
             second = slice(channels + r * k, channels + r * k + k)
-            grad_w_in_ref[second, lanes] = arrived_ref[r ^ far(n_dp), first + k : first + 2 * k].astype(F32)
-            grad_w_out_ref[rows, lanes] = arrived_ref[r ^ far(n_dp), first + 2 * k : first + 3 * k].astype(F32)
+            grad_w_in_ref[second, lanes] = arrived_ref[place_of(r, n_dp), first + k : first + 2 * k].astype(F32)
+            grad_w_out_ref[rows, lanes] = arrived_ref[place_of(r, n_dp), first + 2 * k : first + 3 * k].astype(F32)
         biases = arrived_ref[0, k + halves * 3 * k :].astype(F32)
         grad_b_in_ref[:, lanes] = biases[h : h + 1]
         grad_b_out_ref[:, lanes] = biases[halves + h : halves + h + 1]
@@ -370,7 +378,7 @@
     if axis == "dom":
         group = [peer_at(i, size) for i in range(size)]
     else:
-        group = [i ^ far(size) for i in range(size)]
+        group = [replica_at(i, size) for i in range(size)]
     return lax.all_to_all(values, axis, split_axis=0, concat_axis=0, axis_index_groups=[group], tiled=True)
 
 

time: 180 us -> 179 us (level)
  no operation moved by 1% of the time
where the time goes in v7:
time: 179 us
  blocking collectives  113 us (63%)
  starting transfers between devices  46.6 us (26%)
  Pallas kernels  12.6 us (7%)
  local copies, waits for them, and re-layouts  4.46 us (2%)
    all_to_all x5, blocking collectives, swap(): lax.all_to_all(values, axis, split_axis=0, concat_axis=0, axis_index_grou...  113 us
    all_to_all x2, starting transfers between devices, swap(): lax.all_to_all(values, axis, split_axis=0, concat_axis=0, axis_index_grou...  46.6 us
    pallas_call x9, Pallas kernels, call(): pl.pallas_call(kernel, out_shape=shapes, in_specs=in_specs, out_specs=[pl...  12.6 us
  transfers between devices with their start and end apart: 2, of which 1 were waited for; matrix products, arithmetic and copies ran while one was open for 0% of the time, Pallas kernels for 1%

profile of v7, /device:TPU:1, one launch (start us, length us, event | category | flops | bytes accessed | tf_op | source)
XLA Modules:
  0.0 178.6 jit_solution(9951722269896923375)
XLA Ops:
  0.6 0.0 copy-start.6
  0.6 0.8 copy.20.blocks_ref
  1.4 0.0 copy-done.6
  1.4 0.0 copy-start.11
  1.4 0.0 copy-start.5
  1.4 0.7 pack.1
  2.1 0.0 copy-start.4
  2.1 9.7 %all-to-all-start.1 = ((s32[16,16,128]{2,1,0:T(8,128)}), s32[16,16,128]{2,1,0:T(8,128)S(1)}, u32[]{:S(2)}, u32[]{:S(2)}) async-start(s32[16,16,128]{2,1,0:T(8,128)} %pack.1), calls=%async_computation.1 | async-start | bytes 262144 | tf_op jit(solution)/shard_map/all_to_all | solution.py:382
  11.8 0.0 copy-done.11
  11.8 0.1 copy.19
  11.9 0.0 copy-start.10
  11.9 0.7 copy-done.10
  12.6 0.0 copy-start
  12.6 1.0 copy-done
  13.6 0.0 copy-start.1
  13.6 1.4 first.1
  15.0 0.0 all-to-all-done.1.refs_2_
  15.0 0.0 copy-start.9
  15.0 37.0 %all-to-all-start = ((bf16[64,2,128]{2,1,0:T(2,128)(2,1)}), bf16[64,2,128]{2,1,0:T(2,128)(2,1)S(1)}, u32[]{:S(2)}, u32[]{:S(2)}) async-start(bf16[64,2,128]{2,1,0:T(2,128)(2,1)} %bitcast.2), calls=%async_computation | async-start | bytes 65536 | tf_op jit(solution)/shard_map/all_to_all | solution.py:382
  52.0 0.0 copy-start.7
  52.0 0.0 copy-start.8
  52.0 0.0 copy-done.5
  52.0 0.0 copy-done.4
  52.0 0.0 copy-done.1
  52.0 0.0 copy-done.9
  52.0 0.6 copy-done.7
  52.7 0.0 copy-done.8
  52.7 0.0 copy-start.2
  52.7 1.0 copy-done.2
  53.7 0.5 inputs.1
  54.3 0.1 copy.21
  54.4 0.1 copy.22.refs_3_
  54.5 1.4 all-to-all-done
  55.8 2.5 %edges.1 = (bf16[128,128]{1,0:T(8,128)(2,1)S(1)}, f32[16,1024]{1,0:T(8,128)S(1)}) custom-call(bf16[128,128]{1,0:T(8,128)(2,1)S(1)} %bitcast.22, bf16[16,1024]{1,0:T(8,128)(2,1)S(1)} %get-tuple-element.29.refs_1_.refs_6_, s32[16,16,128]{2,1,0:T(8,128)S(1)} %all-to-all-done.1.refs_2_, s32[16,16]{1,0:T(8,128)S(1)} %copy.22.refs_3_, ...), custom_call_target="tpu_custom_call" | custom-call | bytes 328704 | tf_op jit(solution)/shard_map/edges/pallas_call | solution.py:364
  58.4 26.4 %all_to_all.59 = bf16[64,2,128]{2,1,0:T(2,128)(2,1)S(1)} all-to-all(bf16[64,2,128]{2,1,0:T(2,128)(2,1)S(1)} %bitcast.25), channel_id=1, replica_groups={{512,16,544,48,576,80,608,112,640,144,672,176,704,208,736,240,768,272,8..., dimensions={0} | all-to-all | bytes 65536 | tf_op jit(solution)/shard_map/all_to_all | solution.py:382
  84.7 0.7 aggregate.1
  85.5 0.0 copy-start.3
  85.5 13.8 %all_to_all.60.refs_0_ = bf16[16,16,1024]{2,1,0:T(8,128)(2,1)S(1)} all-to-all(bf16[16,16,1024]{2,1,0:T(8,128)(2,1)S(1)} %get-tuple-element.34), channel_id=1, replica_groups={{10,3,12,5,14,7,0,9,2,11,4,13,6,15,8,1},{26,19,28,21,30,23,16,25,18,27,..., dimensions={0} | all-to-all | bytes 1048576 | tf_op jit(solution)/shard_map/all_to_all | solution.py:382
  99.3 0.0 copy-done.3
  99.3 1.9 %dense.1 = (bf16[64,256]{1,0:T(8,128)(2,1)S(1)}, f32[64,256]{1,0:T(8,128)S(1)}, bf16[16,1024]{1,0:T(8,128)(2,1)S(1)}, bf16[256,128]{1,0:T(8,128)(2,1)S(1)}) custom-call(bf16[16,16,1024]{2,1,0:T(8,128)(2,1)S(1)} %all_to_all.60.refs_0_, f32[256,1024]{1,0:T(8,128)S(1)} %get-tuple-element.35.refs_1_, f32[256,1024]{1,0:T(8,128)S(1)} %get-tuple-element.36.refs_2_, ...), custom_call_target="tpu_custom_call" | custom-call | bytes 3837956 | tf_op jit(solution)/shard_map/dense/pallas_call | solution.py:364
  101.1 30.4 %all_to_all.61 = bf16[64,4,128]{2,1,0:T(4,128)(2,1)S(1)} all-to-all(bf16[64,4,128]{2,1,0:T(4,128)(2,1)S(1)} %bitcast.23), channel_id=1, replica_groups={{512,16,544,48,576,80,608,112,640,144,672,176,704,208,736,240,768,272,8..., dimensions={0} | all-to-all | bytes 131072 | tf_op jit(solution)/shard_map/all_to_all | solution.py:382
  131.5 3.0 %edges_back.1 = (bf16[256,128]{1,0:T(8,128)(2,1)S(1)}, f32[16,1024]{1,0:T(8,128)S(1)}) custom-call(bf16[256,128]{1,0:T(8,128)(2,1)S(1)} %bitcast.19, bf16[16,1024]{1,0:T(8,128)(2,1)S(1)} %get-tuple-element.39.refs_1_, s32[16,16,128]{2,1,0:T(8,128)S(1)} %all-to-all-done.1.refs_2_, s32[16,16]{1,0:T(8,128)S(1)} %copy.22.refs_3_, ...), custom_call_target="tpu_custom_call" | custom-call | bytes 394240 | tf_op jit(solution)/shard_map/edges_back/pallas_call | solution.py:364
  134.5 29.2 %all_to_all.62 = bf16[64,4,128]{2,1,0:T(4,128)(2,1)S(1)} all-to-all(bf16[64,4,128]{2,1,0:T(4,128)(2,1)S(1)} %bitcast.24), channel_id=1, replica_groups={{512,16,544,48,576,80,608,112,640,144,672,176,704,208,736,240,768,272,8..., dimensions={0} | all-to-all | bytes 131072 | tf_op jit(solution)/shard_map/all_to_all | solution.py:382
  163.6 0.9 back.1
  164.5 13.1 %all_to_all.63.arrived_ref = bf16[16,128,128]{2,1,0:T(8,128)(2,1)S(1)} all-to-all(bf16[16,128,128]{2,1,0:T(8,128)(2,1)S(1)} %back.1), channel_id=1, replica_groups={{10,3,12,5,14,7,0,9,2,11,4,13,6,15,8,1},{26,19,28,21,30,23,16,25,18,27,..., dimensions={0} | all-to-all | bytes 1048576 | tf_op jit(solution)/shard_map/all_to_all | solution.py:382
  177.6 1.0 last.1
  (1 shorter events, 0.0 us)
Async XLA Ops:
  0.6 0.8 copy-start.6
  1.4 10.4 %copy-start.11 = (s32[1,64,16]{1,2,0:T(8,128)S(1)}, s32[1,64,16]{1,2,0:T(8,128)}, u32[]{:S(2)}) copy-start(s32[1,64,16]{1,2,0:T(8,128)} %param.13) | copy-start | bytes 12292
  1.4 50.6 %copy-start.5 = (bf16[256,256]{1,0:T(8,128)(2,1)S(1)}, bf16[256,256]{1,0:T(8,128)(2,1)}, u32[]{:S(2)}) copy-start(bf16[256,256]{1,0:T(8,128)(2,1)} %refs_9_.1) | copy-start | bytes 393220
  2.1 49.9 %copy-start.4 = (bf16[512,256]{1,0:T(8,128)(2,1)S(1)}, bf16[512,256]{1,0:T(8,128)(2,1)}, u32[]{:S(2)}) copy-start(bf16[512,256]{1,0:T(8,128)(2,1)} %refs_3_.1) | copy-start | bytes 786436
  2.1 12.9 %all-to-all-start.1 = ((s32[16,16,128]{2,1,0:T(8,128)}), s32[16,16,128]{2,1,0:T(8,128)S(1)}, u32[]{:S(2)}, u32[]{:S(2)}) async-start(s32[16,16,128]{2,1,0:T(8,128)} %pack.1), calls=%async_computation.1 | async-start | bytes 262144 | tf_op jit(solution)/shard_map/all_to_all | solution.py:382
  11.9 0.7 copy-start.10
  12.6 1.0 copy-start
  13.6 38.4 %copy-start.1 = (bf16[1024,256]{1,0:T(8,128)(2,1)S(1)}, bf16[1024,256]{1,0:T(8,128)(2,1)}, u32[]{:S(2)}) copy-start(bf16[1024,256]{1,0:T(8,128)(2,1)} %features_ref.3) | copy-start | bytes 1572868
  15.0 37.0 %copy-start.9 = (f32[256]{0:T(256)S(1)}, f32[256]{0:T(256)}, u32[]{:S(2)}) copy-start(f32[256]{0:T(256)} %param.20) | copy-start | bytes 3076
  15.0 40.8 %all-to-all-start = ((bf16[64,2,128]{2,1,0:T(2,128)(2,1)}), bf16[64,2,128]{2,1,0:T(2,128)(2,1)S(1)}, u32[]{:S(2)}, u32[]{:S(2)}) async-start(bf16[64,2,128]{2,1,0:T(2,128)(2,1)} %bitcast.2), calls=%async_computation | async-start | bytes 65536 | tf_op jit(solution)/shard_map/all_to_all | solution.py:382
  52.0 0.7 copy-start.7
  52.0 0.7 copy-start.8
  52.7 1.0 copy-start.2
  85.5 13.8 %copy-start.3 = (bf16[1024,256]{1,0:T(8,128)(2,1)S(1)}, bf16[1024,256]{1,0:T(8,128)(2,1)}, u32[]{:S(2)}) copy-start(bf16[1024,256]{1,0:T(8,128)(2,1)} %refs_8_.1) | copy-start | bytes 1572868
